TPU v7x, 512 devices: a whole 4x4x16 slice. The times are simulated.
512 devices in a mesh: gx: 8 (over z_lo), gy: 8 (over y, core), gz: 8 (over z_hi, x).
Axes of the slice: x: 4, y: 4, z: 16 (z_hi: 2, z_lo: 8; z = z_hi * 8 + z_lo), core: 2. Of those that a mesh axis runs over, the one named last changes fastest.
Arguments:
- orbitals: float32 [16, 32, 32, 1024], P(None, 'gx', 'gy', 'gz'), may hold values from -5000 to 5000
- potential: float32 [32, 32, 1024], P('gx', 'gy', 'gz'), may hold values from 0 to 2
Outputs:
- q_block: float32 [16, 32, 32, 1024], P(None, 'gx', 'gy', 'gz')
- ritz: float32 [16, 16], replicated
All inputs are finite; a program needn't handle non-finite values.
Results may differ from a plain program's by a relative error of at most 0.0003.
Values sent between devices are 32-bit elements; how exact they have to be, the bound alone decides.
No kernel may reach another device: no remote copies, remote signals or barrier semaphores. Data moves between devices by JAX's collectives and lax.ppermute only.
A program may use at most 64 MiB of HBM per device.

v0:
```python
import functools

import jax
import jax.numpy as jnp
from jax import lax
from jax.experimental import pallas as pl
from jax.experimental.pallas import tpu as pltpu
from jax.sharding import PartitionSpec as P

WEIGHTS = (-205.0 / 72.0, 8.0 / 5.0, -1.0 / 5.0, 8.0 / 315.0, -1.0 / 560.0)
HALF = (12.0 - 1.5) / 2.0
MIDDLE = (12.0 + 1.5) / 2.0
ORB = 16
SIDE = 4
CELLS = SIDE * SIDE
LANES = 128
EXT = 16
BLOCK = CELLS * ORB
EDGE = SIDE * ORB
PAYLOAD = 2 * ORB + 8


def lane_index(rows):
    return lax.broadcasted_iota(jnp.int32, (rows, LANES), 1)


def rolled(value, amount):
    amount %= LANES
    return pltpu.roll(value, amount, 1) if amount else value


def rows_of(ref, cell):
    return ref[cell * ORB : (cell + 1) * ORB, :]


def face_masks(flags, rows):
    lane = lane_index(rows)
    even = flags[2] == 0
    upper = jnp.where(even, LANES - EXT, 0)
    lower = jnp.where(even, 0, LANES - EXT)
    first = (lane >= upper) & (lane < upper + EXT)
    second = (lane >= lower) & (lane < lower + EXT)
    return first, second


def payload_kernel(flags, orbitals, potential, first, second):
    mask1, mask2 = face_masks(flags, ORB)
    row1, row2 = face_masks(flags, 1)
    for high in range(2):
        sums = [jnp.zeros((ORB, LANES), jnp.float32)] * 2 + [jnp.zeros((1, LANES), jnp.float32)] * 2
        for low in range(8):
            cell = 8 * high + low
            value = orbitals[pl.ds(cell, ORB, stride=CELLS), :]
            local = potential[cell : cell + 1, :]
            parts = (
                jnp.where(mask1, value, 0.0),
                jnp.where(mask2, value, 0.0),
                jnp.where(row1, local, 0.0),
                jnp.where(row2, local, 0.0),
            )
            sums = [s + rolled(p, EXT * low) for s, p in zip(sums, parts)]
        for out, value, local in ((first, sums[0], sums[2]), (second, sums[1], sums[3])):
            out[high * ORB : (high + 1) * ORB, :] = value
            out[2 * ORB + high : 2 * ORB + high + 1, :] = local
    for out in (first, second):
        out[2 * ORB + 2 :, :] = jnp.zeros((PAYLOAD - 2 * ORB - 2, LANES), jnp.float32)


def extend_kernel(flags, orbitals, second, first, field, edge_potential):
    mask1, mask2 = face_masks(flags, ORB)
    row1, row2 = face_masks(flags, 1)
    for cell in range(CELLS):
        field[cell * ORB : (cell + 1) * ORB, :] = orbitals[pl.ds(cell, ORB, stride=CELLS), :]
    for x in range(SIDE):
        total, total_potential = 0.0, 0.0
        for y in range(SIDE):
            high, low = divmod(x * SIDE + y, 8)

            def unpack(start, size, keep1, keep2):
                one = rolled(first[start : start + size, :], -EXT * low)
                two = rolled(second[start : start + size, :], -EXT * low)
                return rolled(jnp.where(keep2, one, 0.0) + jnp.where(keep1, two, 0.0), 2 * EXT * y)

            total = total + unpack(high * ORB, ORB, mask1, mask2)
            total_potential = total_potential + unpack(2 * ORB + high, 1, row1, row2)
        field[BLOCK + x * ORB : BLOCK + (x + 1) * ORB, :] = total
        edge_potential[x : x + 1, :] = total_potential


def edge_of(ref, x):
    return ref[x * ORB : (x + 1) * ORB, :]


def step_kernel(scale, with_previous, split, flags, potential, edge_potential, field, y1, x2, y2, x1, *rest):
    previous = rest[0] if with_previous else None
    out = rest[-2] if split else rest[-1]
    lane = lane_index(ORB)
    place = lane % (2 * EXT)
    lane_y = ((lane + EXT) // (2 * EXT)) % SIDE
    inside = ((place < EXT) & (flags[4] != 0)) | ((place >= EXT) & (flags[3] != 0))
    window = (lane < EXT) | (lane >= LANES - EXT)
    even_x, even_y = flags[0] == 0, flags[1] == 0
    weight = [-0.5 * scale * w for w in WEIGHTS]
    shift = MIDDLE + 1.5 * WEIGHTS[0]

    def line(get, one, two, even):
        pairs = [(get(one, i), get(two, i)) for i in range(SIDE)]
        below = [jnp.where(even, b, a) for a, b in pairs]
        above = [jnp.where(even, a, b) for a, b in pairs]
        return below + [get(field, i) for i in range(SIDE)] + above

    for y in range(SIDE):
        along = line(lambda ref, x: rows_of(ref, x * SIDE + y), x1, x2, even_x)
        for x in range(SIDE):
            cell = x * SIDE + y
            here = along[SIDE + x]
            there = rolled(edge_of(field, CELLS + x), -2 * EXT * y)
            total = (potential[cell : cell + 1, :] - shift) * scale * here
            for k in range(1, 5):
                pairs = along[SIDE + x + k] + along[SIDE + x - k]
                pairs = pairs + rolled(jnp.where(lane < k, there, here), -k)
                pairs = pairs + rolled(jnp.where(lane >= LANES - k, there, here), k)
                total = total + weight[k] * pairs
            if with_previous:
                total = total - rows_of(previous, cell)
            out[cell * ORB : (cell + 1) * ORB, :] = total
    for x in range(SIDE):
        along = line(lambda ref, y: rows_of(ref, x * SIDE + y), y1, y2, even_y)
        for y in range(SIDE):
            cell = x * SIDE + y
            total = rows_of(out, cell)
            for k in range(1, 5):
                total = total + weight[k] * (along[SIDE + y + k] + along[SIDE + y - k])
            out[cell * ORB : (cell + 1) * ORB, :] = total
    along = line(lambda ref, x: edge_of(ref, CELLS + x), x1, x2, even_x)
    for x in range(SIDE):
        here = along[SIDE + x]
        one, two = edge_of(y1, CELLS + x), edge_of(y2, CELLS + x)
        below, above = jnp.where(even_y, two, one), jnp.where(even_y, one, two)
        there = 0.0
        for y in range(SIDE):
            there = there + rolled(jnp.where(window, rows_of(field, x * SIDE + y), 0.0), 2 * EXT * y)
        total = (edge_potential[x : x + 1, :] - shift) * scale * here
        for k in range(1, 5):
            pairs = along[SIDE + x + k] + along[SIDE + x - k]
            pairs = pairs + rolled(jnp.where(lane_y < k, above, here), -2 * EXT * k)
            pairs = pairs + rolled(jnp.where(lane_y >= SIDE - k, below, here), 2 * EXT * k)
            pairs = pairs + rolled(jnp.where(place < k, there, here), -k)
            pairs = pairs + rolled(jnp.where(place >= 2 * EXT - k, there, here), k)
            total = total + weight[k] * pairs
        if with_previous:
            total = total - edge_of(previous, CELLS + x)
        total = jnp.where(inside, total, 0.0)
        if split:
            rest[-1][x * ORB : (x + 1) * ORB, :] = total
        else:
            out[BLOCK + x * ORB : BLOCK + (x + 1) * ORB, :] = total


def dot(a, b, contract):
    return lax.dot_general(
        a, b, ((contract[:1], contract[1:]), ((), ())), precision=lax.Precision.HIGHEST, preferred_element_type=jnp.float32
    )


def sums_kernel(potential, field, edge, after_y, after_x, sums):
    lane = lane_index(ORB)
    here_all, image_all = [], []
    for x in range(SIDE):
        for y in range(SIDE):
            cell = x * SIDE + y
            here, there = rows_of(field, cell), rolled(edge_of(edge, x), -2 * EXT * y)
            image = (0.5 * potential[cell : cell + 1, :] - 0.75 * WEIGHTS[0]) * here
            for k in range(1, 5):
                up = rows_of(field, cell + k * SIDE) if x + k < SIDE else rows_of(after_x, cell + (k - SIDE) * SIDE)
                up = up + (rows_of(field, cell + k) if y + k < SIDE else rows_of(after_y, cell + k - SIDE))
                up = up + rolled(jnp.where(lane < k, there, here), -k)
                image = image + (-0.5 * WEIGHTS[k]) * up
            here_all.append(here)
            image_all.append(image)
    here = jnp.concatenate(here_all, axis=1)
    image = jnp.concatenate(image_all, axis=1)
    sums[...] = jnp.zeros_like(sums)
    sums[:, : 2 * ORB] = dot(here, jnp.concatenate([here, image], axis=0), (1, 1))


def finish_kernel(cell_total, sums, field, q_block, ritz):
    sums = sums[...] * (1.0 / cell_total)
    row = lax.broadcasted_iota(jnp.int32, (ORB, LANES), 0)
    lane = lane_index(ORB)
    work = jnp.where(lane < ORB, sums, jnp.where(lane == row + ORB, 1.0, 0.0))
    for k in range(ORB - 1):
        pivot = work[k : k + 1, :]
        factor = work[:, k : k + 1] / pivot[:, k : k + 1]
        work = work - jnp.where(row > k, factor, 0.0) * pivot
    diagonal = jnp.sum(jnp.where(lane == row, work, 0.0), axis=1, keepdims=True)
    inverse = (work * (1.0 / jnp.sqrt(diagonal)))[:, ORB : 2 * ORB]
    half = sums[:, ORB : 2 * ORB]
    part = dot(dot(inverse, half, (1, 0)), inverse, (1, 1))
    ritz[...] = part + part.T
    for cell in range(CELLS):
        q_block[pl.ds(cell, ORB, stride=CELLS), :] = dot(inverse, rows_of(field, cell), (1, 0))


def swap(value, axis, first):
    pairs = []
    for i in range(first, lax.axis_size(axis) - 1, 2):
        pairs += [(i, i + 1), (i + 1, i)]
    return lax.ppermute(value, axis, pairs)


def from_above(value, axis):
    return lax.ppermute(value, axis, [(i + 1, i) for i in range(lax.axis_size(axis) - 1)])


def sum_everywhere(value):
    if all(lax.axis_size(axis) == 8 for axis in ("gx", "gy", "gz")):
        fours = [[0, 1, 2, 3], [4, 5, 6, 7]]
        value = lax.psum(value, "gy")
        value = lax.psum(value, "gz", axis_index_groups=fours)
        value = lax.psum(value, "gx", axis_index_groups=fours)
        rings = [[8 * gx + gz, 8 * gx + 32 + gz, 8 * gx + gz + 4, 8 * gx + 32 + gz + 4] for gx in range(4) for gz in range(4)]
        return lax.psum(value, ("gx", "gz"), axis_index_groups=rings)
    return lax.psum(value, ("gx", "gy", "gz"))


def call(kernel, outs, smem=True):
    def run(*operands):
        specs = [pl.BlockSpec(memory_space=pltpu.VMEM)] * len(operands)
        if smem:
            specs[0] = pl.BlockSpec(memory_space=pltpu.SMEM)
        return pl.pallas_call(
            kernel,
            out_shape=[jax.ShapeDtypeStruct(shape, jnp.float32) for shape in outs],
            in_specs=specs,
            out_specs=[pl.BlockSpec(memory_space=pltpu.VMEM)] * len(outs),
            compiler_params=pltpu.CompilerParams(vmem_limit_bytes=8 * 1024 * 1024),
        )(*operands)

    return run


def body(orbitals, potential):
    at = [lax.axis_index(axis) for axis in ("gx", "gy", "gz")]
    cell_total = orbitals[0].size * lax.axis_size("gx") * lax.axis_size("gy") * lax.axis_size("gz")
    flags = jnp.stack(
        [at[0] % 2, at[1] % 2, at[2] % 2, (at[2] > 0).astype(jnp.int32), (at[2] < lax.axis_size("gz") - 1).astype(jnp.int32)]
    ).astype(jnp.int32)
    shape = orbitals.shape
    orbitals = orbitals.reshape(BLOCK, LANES)
    potential = potential.reshape(CELLS, LANES)
    block, edge, sent = (BLOCK, LANES), (EDGE, LANES), (BLOCK + EDGE, LANES)

    first, second = call(payload_kernel, ((PAYLOAD, LANES),) * 2)(flags, orbitals, potential)
    second, first = swap(second, "gz", 1), swap(first, "gz", 0)
    field, edge_potential = call(extend_kernel, (sent, (8, LANES)))(flags, orbitals, second, first)

    def advance(field, scale, previous, split):
        y2, y1, x2, x1 = [swap(field, axis, first) for axis in ("gy", "gx") for first in (1, 0)]
        kernel = functools.partial(step_kernel, scale, bool(previous), split)
        outs = (block, edge) if split else (sent,)
        return call(kernel, outs)(flags, potential, edge_potential, field, y1, x2, y2, x1, *previous)

    (field1,) = advance(field, 1.0 / HALF, (), False)
    (field2,) = advance(field1, 2.0 / HALF, (field,), False)
    field, edge = advance(field2, 2.0 / HALF, (field1,), True)
    after_y, after_x = from_above(field, "gy"), from_above(field, "gx")
    sums = call(sums_kernel, ((ORB, LANES),), smem=False)(potential, field, edge, after_y, after_x)[0]
    sums = sum_everywhere(sums)
    q_block, ritz = call(functools.partial(finish_kernel, cell_total), (block, (ORB, ORB)), smem=False)(sums, field)
    return q_block.reshape(shape), ritz


def solution(mesh):
    placed = (P(None, "gx", "gy", "gz"), P("gx", "gy", "gz"))
    return jax.shard_map(
        body,
        mesh=mesh,
        in_specs=placed,
        out_specs=(P(None, "gx", "gy", "gz"), P()),
        check_vma=False,
    )
```

profile of v0, /device:TPU:2, one launch (start us, length us, event | category | flops | bytes accessed | tf_op | source)
XLA Modules:
  0.0 132.8 jit_solution(14751503946506920285)
XLA Ops:
  1.4 0.9 copy-done
  2.3 0.7 shard_map.41
  3.0 3.4 %collective-permute-start = (f32[40,128]{1,0:T(8,128)S(1)}, f32[40,128]{1,0:T(8,128)S(1)}, u32[]{:S(2)}, u32[]{:S(2)}) collective-permute-start(f32[40,128]{1,0:T(8,128)S(1)} %get-tuple-element.10), channel_id=1, source_target_pairs={{1,2},{2,1},{3,4},{4,3},{5,6},{6,5},{9,10},{10,9},{11,12},{12,11},... | collective-permute-start | bytes 61448 | tf_op jit(solution)/shard_map/ppermute | solution.py:209
  6.4 5.1 %collective-permute-start.1 = (f32[40,128]{1,0:T(8,128)S(1)}, f32[40,128]{1,0:T(8,128)S(1)}, u32[]{:S(2)}, u32[]{:S(2)}) collective-permute-start(f32[40,128]{1,0:T(8,128)S(1)} %get-tuple-element.11), channel_id=1, source_target_pairs={{0,1},{1,0},{2,3},{3,2},{4,5},{5,4},{6,7},{7,6},{8,9},{9,8},{10,11... | collective-permute-start | bytes 61448 | tf_op jit(solution)/shard_map/ppermute | solution.py:209
  11.5 1.7 %collective-permute-done.1.first = f32[40,128]{1,0:T(8,128)S(1)} collective-permute-done((f32[40,128]{1,0:T(8,128)S(1)}, f32[40,128]{1,0:T(8,128)S(1)}, u32[]{:S(2)}, u32[]{:S(2)}) %collective-permute-start.1) | collective-permute-done | bytes 20512 | tf_op jit(solution)/shard_map/ppermute | solution.py:209
  13.2 0.8 shard_map.42
  14.0 2.7 %collective-permute-start.5 = (f32[320,128]{1,0:T(8,128)S(1)}, f32[320,128]{1,0:T(8,128)S(1)}, u32[]{:S(2)}, u32[]{:S(2)}) collective-permute-start(f32[320,128]{1,0:T(8,128)S(1)} %get-tuple-element.13.field.rest_0_), channel_id=1, source_target_pairs={{0,64},{64,0},{128,192},{192,128},{256,320},{320,256},{384,448},{4... | collective-permute-start | bytes 491528 | tf_op jit(solution)/shard_map/ppermute | solution.py:209
  16.7 0.7 collective-permute-start.4
  17.4 0.7 collective-permute-start.3
  18.1 4.8 %collective-permute-start.2 = (f32[320,128]{1,0:T(8,128)S(1)}, f32[320,128]{1,0:T(8,128)S(1)}, u32[]{:S(2)}, u32[]{:S(2)}) collective-permute-start(f32[320,128]{1,0:T(8,128)S(1)} %get-tuple-element.13.field.rest_0_), channel_id=1, source_target_pairs={{0,8},{8,0},{16,24},{24,16},{32,40},{40,32},{48,56},{56,48},{1,9},... | collective-permute-start | bytes 491528 | tf_op jit(solution)/shard_map/ppermute | solution.py:209
  22.9 1.0 collective-permute-done.2.y1
  23.9 2.0 %shard_map.43.field.rest_0_ = f32[320,128]{1,0:T(8,128)S(1)} custom-call(s32[5]{0:T(128)S(1)} %stack.31.flags, f32[16,128]{1,0:T(8,128)S(1)} %bitcast.11, f32[8,128]{1,0:T(8,128)S(1)} %get-tuple-element.12.edge_potential, f32[320,128]{1,0:T(8,128)S(1)} %get-tuple-element.13.field.rest_0_, f32[320,128]{1,0:T(8,128)S(1)} %collective-permute-done.2.y1, ...), custom_call_target="tpu_custom_call" | custom-call | tf_op jit(solution)/shard_map/pallas_call | solution.py:232
  25.9 6.7 %collective-permute-start.9 = (f32[320,128]{1,0:T(8,128)S(1)}, f32[320,128]{1,0:T(8,128)S(1)}, u32[]{:S(2)}, u32[]{:S(2)}) collective-permute-start(f32[320,128]{1,0:T(8,128)S(1)} %shard_map.43.field.rest_0_), channel_id=1, source_target_pairs={{0,64},{64,0},{128,192},{192,128},{256,320},{320,256},{384,448},{4... | collective-permute-start | bytes 491528 | tf_op jit(solution)/shard_map/ppermute | solution.py:209
  32.6 0.7 collective-permute-start.8
  33.3 0.7 collective-permute-start.7
  34.0 4.8 %collective-permute-start.6 = (f32[320,128]{1,0:T(8,128)S(1)}, f32[320,128]{1,0:T(8,128)S(1)}, u32[]{:S(2)}, u32[]{:S(2)}) collective-permute-start(f32[320,128]{1,0:T(8,128)S(1)} %shard_map.43.field.rest_0_), channel_id=1, source_target_pairs={{0,8},{8,0},{16,24},{24,16},{32,40},{40,32},{48,56},{56,48},{1,9},... | collective-permute-start | bytes 491528 | tf_op jit(solution)/shard_map/ppermute | solution.py:209
  38.9 1.0 collective-permute-done.6.y1
  39.8 2.0 %shard_map.44.field = f32[320,128]{1,0:T(8,128)S(1)} custom-call(s32[5]{0:T(128)S(1)} %stack.31.flags, f32[16,128]{1,0:T(8,128)S(1)} %bitcast.12, f32[8,128]{1,0:T(8,128)S(1)} %get-tuple-element.12.edge_potential, f32[320,128]{1,0:T(8,128)S(1)} %shard_map.43.field.rest_0_, f32[320,128]{1,0:T(8,128)S(1)} %collective-permute-done.6.y1, ...), custom_call_target="tpu_custom_call" | custom-call | tf_op jit(solution)/shard_map/pallas_call | solution.py:232
  41.9 7.9 %collective-permute-start.13 = (f32[320,128]{1,0:T(8,128)S(1)}, f32[320,128]{1,0:T(8,128)S(1)}, u32[]{:S(2)}, u32[]{:S(2)}) collective-permute-start(f32[320,128]{1,0:T(8,128)S(1)} %shard_map.44.field), channel_id=1, source_target_pairs={{0,64},{64,0},{128,192},{192,128},{256,320},{320,256},{384,448},{4... | collective-permute-start | bytes 491528 | tf_op jit(solution)/shard_map/ppermute | solution.py:209
  49.8 0.7 collective-permute-start.12
  50.5 0.7 collective-permute-start.11
  51.2 4.9 %collective-permute-start.10 = (f32[320,128]{1,0:T(8,128)S(1)}, f32[320,128]{1,0:T(8,128)S(1)}, u32[]{:S(2)}, u32[]{:S(2)}) collective-permute-start(f32[320,128]{1,0:T(8,128)S(1)} %shard_map.44.field), channel_id=1, source_target_pairs={{0,8},{8,0},{16,24},{24,16},{32,40},{40,32},{48,56},{56,48},{1,9},... | collective-permute-start | bytes 491528 | tf_op jit(solution)/shard_map/ppermute | solution.py:209
  56.1 1.0 collective-permute-done.10.y1
  57.1 2.0 %shard_map.45 = (f32[256,128]{1,0:T(8,128)S(1)}, f32[64,128]{1,0:T(8,128)S(1)}) custom-call(s32[5]{0:T(128)S(1)} %stack.31.flags, f32[16,128]{1,0:T(8,128)S(1)} %bitcast.13, f32[8,128]{1,0:T(8,128)S(1)} %get-tuple-element.12.edge_potential, f32[320,128]{1,0:T(8,128)S(1)} %shard_map.44.field, f32[320,128]{1,0:T(8,128)S(1)} %collective-permute-done.10.y1, ...), custom_call_target="tpu_custom_call" | custom-call | tf_op jit(solution)/shard_map/pallas_call | solution.py:232
  59.1 1.3 collective-permute-start.15
  60.4 1.3 collective-permute-start.14
  61.7 8.1 %collective-permute-done.15.after_x = f32[256,128]{1,0:T(8,128)S(1)} collective-permute-done((f32[256,128]{1,0:T(8,128)S(1)}, f32[256,128]{1,0:T(8,128)S(1)}, u32[]{:S(2)}, u32[]{:S(2)}) %collective-permute-start.15) | collective-permute-done | bytes 131104 | tf_op jit(solution)/shard_map/ppermute | solution.py:213
  70.4 13.6 %psum.28 = f32[16,128]{1,0:T(8,128)S(1)} all-reduce(f32[16,128]{1,0:T(8,128)S(1)} %shard_map.46), channel_id=1, replica_groups=mesh['gx'=8,'gy'=8,'gz'=8] {'gy'}, use_global_device_ids=true, to_apply=%region_0.1 | all-reduce | flops 2048 | bytes 16384 | tf_op jit(solution)/shard_map/psum | solution.py:219
  84.0 15.9 %psum.29 = f32[16,128]{1,0:T(8,128)S(1)} all-reduce(f32[16,128]{1,0:T(8,128)S(1)} %psum.28), channel_id=1, replica_groups={{0,1,2,3},{4,5,6,7},{8,9,10,11},{12,13,14,15},{16,17,18,19},{20,21,22,2..., use_global_device_ids=true, to_apply=%region_1.2 | all-reduce | flops 2048 | bytes 16384 | tf_op jit(solution)/shard_map/psum | solution.py:220
  99.9 13.6 %psum.30 = f32[16,128]{1,0:T(8,128)S(1)} all-reduce(f32[16,128]{1,0:T(8,128)S(1)} %psum.29), channel_id=1, replica_groups={{0,64,128,192},{256,320,384,448},{1,65,129,193},{257,321,385,449},{2,66..., use_global_device_ids=true, to_apply=%region_2.3 | all-reduce | flops 2048 | bytes 16384 | tf_op jit(solution)/shard_map/psum | solution.py:221
  113.6 16.7 %psum.31.sums = f32[16,128]{1,0:T(8,128)S(1)} all-reduce(f32[16,128]{1,0:T(8,128)S(1)} %psum.30), channel_id=1, replica_groups={{0,256,4,260},{1,257,5,261},{2,258,6,262},{3,259,7,263},{64,320,68,324}..., use_global_device_ids=true, to_apply=%region_3.4 | all-reduce | flops 2048 | bytes 16384 | tf_op jit(solution)/shard_map/psum | solution.py:223
  130.3 2.5 %shard_map.47 = (f32[256,128]{1,0:T(8,128)}, f32[16,16]{1,0:T(8,128)}) custom-call(f32[16,128]{1,0:T(8,128)S(1)} %psum.31.sums, f32[256,128]{1,0:T(8,128)S(1)} %get-tuple-element.14.field), custom_call_target="tpu_custom_call" | custom-call | tf_op jit(solution)/shard_map/pallas_call | solution.py:232
  (16 shorter events, 1.4 us)
Async XLA Ops:
  0.7 0.7 copy-start.1
  1.4 0.9 copy-start
  3.0 8.5 %collective-permute-start = (f32[40,128]{1,0:T(8,128)S(1)}, f32[40,128]{1,0:T(8,128)S(1)}, u32[]{:S(2)}, u32[]{:S(2)}) collective-permute-start(f32[40,128]{1,0:T(8,128)S(1)} %get-tuple-element.10), channel_id=1, source_target_pairs={{1,2},{2,1},{3,4},{4,3},{5,6},{6,5},{9,10},{10,9},{11,12},{12,11},... | collective-permute-start | bytes 61448 | tf_op jit(solution)/shard_map/ppermute | solution.py:209
  6.4 6.8 %collective-permute-start.1 = (f32[40,128]{1,0:T(8,128)S(1)}, f32[40,128]{1,0:T(8,128)S(1)}, u32[]{:S(2)}, u32[]{:S(2)}) collective-permute-start(f32[40,128]{1,0:T(8,128)S(1)} %get-tuple-element.11), channel_id=1, source_target_pairs={{0,1},{1,0},{2,3},{3,2},{4,5},{5,4},{6,7},{7,6},{8,9},{9,8},{10,11... | collective-permute-start | bytes 61448 | tf_op jit(solution)/shard_map/ppermute | solution.py:209
  14.0 8.9 %collective-permute-start.5 = (f32[320,128]{1,0:T(8,128)S(1)}, f32[320,128]{1,0:T(8,128)S(1)}, u32[]{:S(2)}, u32[]{:S(2)}) collective-permute-start(f32[320,128]{1,0:T(8,128)S(1)} %get-tuple-element.13.field.rest_0_), channel_id=1, source_target_pairs={{0,64},{64,0},{128,192},{192,128},{256,320},{320,256},{384,448},{4... | collective-permute-start | bytes 491528 | tf_op jit(solution)/shard_map/ppermute | solution.py:209
  16.7 6.2 %collective-permute-start.4 = (f32[320,128]{1,0:T(8,128)S(1)}, f32[320,128]{1,0:T(8,128)S(1)}, u32[]{:S(2)}, u32[]{:S(2)}) collective-permute-start(f32[320,128]{1,0:T(8,128)S(1)} %get-tuple-element.13.field.rest_0_), channel_id=1, source_target_pairs={{8,16},{16,8},{24,32},{32,24},{40,48},{48,40},{9,17},{17,9},{25,33... | collective-permute-start | bytes 491528 | tf_op jit(solution)/shard_map/ppermute | solution.py:209
  17.4 5.5 %collective-permute-start.3 = (f32[320,128]{1,0:T(8,128)S(1)}, f32[320,128]{1,0:T(8,128)S(1)}, u32[]{:S(2)}, u32[]{:S(2)}) collective-permute-start(f32[320,128]{1,0:T(8,128)S(1)} %get-tuple-element.13.field.rest_0_), channel_id=1, source_target_pairs={{64,128},{128,64},{192,256},{256,192},{320,384},{384,320},{65,129}... | collective-permute-start | bytes 491528 | tf_op jit(solution)/shard_map/ppermute | solution.py:209
  18.1 5.9 %collective-permute-start.2 = (f32[320,128]{1,0:T(8,128)S(1)}, f32[320,128]{1,0:T(8,128)S(1)}, u32[]{:S(2)}, u32[]{:S(2)}) collective-permute-start(f32[320,128]{1,0:T(8,128)S(1)} %get-tuple-element.13.field.rest_0_), channel_id=1, source_target_pairs={{0,8},{8,0},{16,24},{24,16},{32,40},{40,32},{48,56},{56,48},{1,9},... | collective-permute-start | bytes 491528 | tf_op jit(solution)/shard_map/ppermute | solution.py:209
  25.9 12.9 %collective-permute-start.9 = (f32[320,128]{1,0:T(8,128)S(1)}, f32[320,128]{1,0:T(8,128)S(1)}, u32[]{:S(2)}, u32[]{:S(2)}) collective-permute-start(f32[320,128]{1,0:T(8,128)S(1)} %shard_map.43.field.rest_0_), channel_id=1, source_target_pairs={{0,64},{64,0},{128,192},{192,128},{256,320},{320,256},{384,448},{4... | collective-permute-start | bytes 491528 | tf_op jit(solution)/shard_map/ppermute | solution.py:209
  32.6 6.2 %collective-permute-start.8 = (f32[320,128]{1,0:T(8,128)S(1)}, f32[320,128]{1,0:T(8,128)S(1)}, u32[]{:S(2)}, u32[]{:S(2)}) collective-permute-start(f32[320,128]{1,0:T(8,128)S(1)} %shard_map.43.field.rest_0_), channel_id=1, source_target_pairs={{8,16},{16,8},{24,32},{32,24},{40,48},{48,40},{9,17},{17,9},{25,33... | collective-permute-start | bytes 491528 | tf_op jit(solution)/shard_map/ppermute | solution.py:209
  33.3 5.5 %collective-permute-start.7 = (f32[320,128]{1,0:T(8,128)S(1)}, f32[320,128]{1,0:T(8,128)S(1)}, u32[]{:S(2)}, u32[]{:S(2)}) collective-permute-start(f32[320,128]{1,0:T(8,128)S(1)} %shard_map.43.field.rest_0_), channel_id=1, source_target_pairs={{64,128},{128,64},{192,256},{256,192},{320,384},{384,320},{65,129}... | collective-permute-start | bytes 491528 | tf_op jit(solution)/shard_map/ppermute | solution.py:209
  34.0 5.8 %collective-permute-start.6 = (f32[320,128]{1,0:T(8,128)S(1)}, f32[320,128]{1,0:T(8,128)S(1)}, u32[]{:S(2)}, u32[]{:S(2)}) collective-permute-start(f32[320,128]{1,0:T(8,128)S(1)} %shard_map.43.field.rest_0_), channel_id=1, source_target_pairs={{0,8},{8,0},{16,24},{24,16},{32,40},{40,32},{48,56},{56,48},{1,9},... | collective-permute-start | bytes 491528 | tf_op jit(solution)/shard_map/ppermute | solution.py:209
  41.9 14.2 %collective-permute-start.13 = (f32[320,128]{1,0:T(8,128)S(1)}, f32[320,128]{1,0:T(8,128)S(1)}, u32[]{:S(2)}, u32[]{:S(2)}) collective-permute-start(f32[320,128]{1,0:T(8,128)S(1)} %shard_map.44.field), channel_id=1, source_target_pairs={{0,64},{64,0},{128,192},{192,128},{256,320},{320,256},{384,448},{4... | collective-permute-start | bytes 491528 | tf_op jit(solution)/shard_map/ppermute | solution.py:209
  49.8 6.3 %collective-permute-start.12 = (f32[320,128]{1,0:T(8,128)S(1)}, f32[320,128]{1,0:T(8,128)S(1)}, u32[]{:S(2)}, u32[]{:S(2)}) collective-permute-start(f32[320,128]{1,0:T(8,128)S(1)} %shard_map.44.field), channel_id=1, source_target_pairs={{8,16},{16,8},{24,32},{32,24},{40,48},{48,40},{9,17},{17,9},{25,33... | collective-permute-start | bytes 491528 | tf_op jit(solution)/shard_map/ppermute | solution.py:209
  50.5 5.6 %collective-permute-start.11 = (f32[320,128]{1,0:T(8,128)S(1)}, f32[320,128]{1,0:T(8,128)S(1)}, u32[]{:S(2)}, u32[]{:S(2)}) collective-permute-start(f32[320,128]{1,0:T(8,128)S(1)} %shard_map.44.field), channel_id=1, source_target_pairs={{64,128},{128,64},{192,256},{256,192},{320,384},{384,320},{65,129}... | collective-permute-start | bytes 491528 | tf_op jit(solution)/shard_map/ppermute | solution.py:209
  51.2 5.9 %collective-permute-start.10 = (f32[320,128]{1,0:T(8,128)S(1)}, f32[320,128]{1,0:T(8,128)S(1)}, u32[]{:S(2)}, u32[]{:S(2)}) collective-permute-start(f32[320,128]{1,0:T(8,128)S(1)} %shard_map.44.field), channel_id=1, source_target_pairs={{0,8},{8,0},{16,24},{24,16},{32,40},{40,32},{48,56},{56,48},{1,9},... | collective-permute-start | bytes 491528 | tf_op jit(solution)/shard_map/ppermute | solution.py:209
  59.1 10.7 %collective-permute-start.15 = (f32[256,128]{1,0:T(8,128)S(1)}, f32[256,128]{1,0:T(8,128)S(1)}, u32[]{:S(2)}, u32[]{:S(2)}) collective-permute-start(f32[256,128]{1,0:T(8,128)S(1)} %get-tuple-element.14.field), channel_id=1, source_target_pairs={{64,0},{128,64},{192,128},{256,192},{320,256},{384,320},{448,384},... | collective-permute-start | bytes 393224 | tf_op jit(solution)/shard_map/ppermute | solution.py:213
  60.4 9.4 %collective-permute-start.14 = (f32[256,128]{1,0:T(8,128)S(1)}, f32[256,128]{1,0:T(8,128)S(1)}, u32[]{:S(2)}, u32[]{:S(2)}) collective-permute-start(f32[256,128]{1,0:T(8,128)S(1)} %get-tuple-element.14.field), channel_id=1, source_target_pairs={{8,0},{16,8},{24,16},{32,24},{40,32},{48,40},{56,48},{9,1},{17,9},... | collective-permute-start | bytes 393224 | tf_op jit(solution)/shard_map/ppermute | solution.py:213
where the time goes:
time: 133 us
  blocking collectives  59.9 us (45%)
  starting transfers between devices  46.9 us (35%)
  waiting for transfers between devices  12.8 us (10%)
  Pallas kernels  10.7 us (8%)
  local copies, waits for them, and re-layouts  1.59 us (1%)
    ppermute x14, starting transfers between devices, swap(): return lax.ppermute(value, axis, pairs)  44.4 us
    psum x1, blocking collectives, sum_everywhere(): return lax.psum(value, ('gx', 'gz'), axis_index_groups=rings)  16.7 us
    psum x1, blocking collectives, sum_everywhere(): value = lax.psum(value, 'gz', axis_index_groups=fours)  15.9 us
    psum x1, blocking collectives, sum_everywhere(): value = lax.psum(value, 'gx', axis_index_groups=fours)  13.6 us
    psum x1, blocking collectives, sum_everywhere(): value = lax.psum(value, 'gy')  13.6 us
    pallas_call x7, Pallas kernels, run(): pl.pallas_call(kernel, out_shape=[jax.ShapeDtypeStruct(shape, jnp.float32...  10.7 us
    ppermute x2, waiting for transfers between devices, from_above(): lax.ppermute(value, axis, [(i + 1, i) for i in range(lax.axis_size(axis)...  8.12 us
    ppermute x14, waiting for transfers between devices, swap(): return lax.ppermute(value, axis, pairs)  4.69 us
  transfers between devices with their start and end apart: 16, of which 5 were waited for; matrix products, arithmetic and copies ran while one was open for 0% of the time, Pallas kernels for 0%

commit v1 on v0

--- a/solution.py
+++ b/solution.py
@@ -163,19 +163,26 @@
     )
 
 
-def sums_kernel(potential, field, edge, after_y, after_x, sums):
+def sums_kernel(flags, potential, field, edge, after_y, beside_x, sums):
     lane = lane_index(ORB)
+    up = flags[1] == 0
+    along_x = {}
+    for y in range(SIDE):
+        rows = [rows_of(ref, x * SIDE + y) for ref in (field, beside_x) for x in range(SIDE)]
+        line = [jnp.where(up, rows[start + i], rows[start + SIDE - 1 - i]) for start in (0, SIDE) for i in range(SIDE)]
+        terms = [sum(-0.5 * WEIGHTS[k] * line[i + k] for k in range(1, 5)) for i in range(SIDE)]
+        for x in range(SIDE):
+            along_x[x, y] = jnp.where(up, terms[x], terms[SIDE - 1 - x])
     here_all, image_all = [], []
     for x in range(SIDE):
         for y in range(SIDE):
             cell = x * SIDE + y
             here, there = rows_of(field, cell), rolled(edge_of(edge, x), -2 * EXT * y)
-            image = (0.5 * potential[cell : cell + 1, :] - 0.75 * WEIGHTS[0]) * here
+            image = (0.5 * potential[cell : cell + 1, :] - 0.75 * WEIGHTS[0]) * here + along_x[x, y]
             for k in range(1, 5):
-                up = rows_of(field, cell + k * SIDE) if x + k < SIDE else rows_of(after_x, cell + (k - SIDE) * SIDE)
-                up = up + (rows_of(field, cell + k) if y + k < SIDE else rows_of(after_y, cell + k - SIDE))
-                up = up + rolled(jnp.where(lane < k, there, here), -k)
-                image = image + (-0.5 * WEIGHTS[k]) * up
+                above = rows_of(field, cell + k) if y + k < SIDE else rows_of(after_y, cell + k - SIDE)
+                above = above + rolled(jnp.where(lane < k, there, here), -k)
+                image = image + (-0.5 * WEIGHTS[k]) * above
             here_all.append(here)
             image_all.append(image)
     here = jnp.concatenate(here_all, axis=1)
@@ -209,6 +216,25 @@
     return lax.ppermute(value, axis, pairs)
 
 
+def swap_x(value, turn):
+    deep, wide = lax.axis_size("gx"), lax.axis_size("gy")
+    pairs = []
+    for j in range(wide):
+        for i in range((turn + j) % 2, deep - 1, 2):
+            pairs += [(i * wide + j, (i + 1) * wide + j), ((i + 1) * wide + j, i * wide + j)]
+    return lax.ppermute(value, ("gx", "gy"), pairs)
+
+
+def one_side_x(value):
+    deep, wide = lax.axis_size("gx"), lax.axis_size("gy")
+    pairs = []
+    for j in range(wide):
+        for i in range(deep - 1):
+            low, high = i * wide + j, (i + 1) * wide + j
+            pairs.append((low, high) if j % 2 else (high, low))
+    return lax.ppermute(value, ("gx", "gy"), pairs)
+
+
 def from_above(value, axis):
     return lax.ppermute(value, axis, [(i + 1, i) for i in range(lax.axis_size(axis) - 1)])
 
@@ -216,7 +242,8 @@
 def sum_everywhere(value):
     if all(lax.axis_size(axis) == 8 for axis in ("gx", "gy", "gz")):
         fours = [[0, 1, 2, 3], [4, 5, 6, 7]]
-        value = lax.psum(value, "gy")
+        value = value + lax.ppermute(value, "gy", [(i, i ^ 1) for i in range(8)])
+        value = lax.psum(value, "gy", axis_index_groups=[[0, 2, 4, 6], [1, 3, 5, 7]])
         value = lax.psum(value, "gz", axis_index_groups=fours)
         value = lax.psum(value, "gx", axis_index_groups=fours)
         rings = [[8 * gx + gz, 8 * gx + 32 + gz, 8 * gx + gz + 4, 8 * gx + 32 + gz + 4] for gx in range(4) for gz in range(4)]
@@ -244,7 +271,7 @@
     at = [lax.axis_index(axis) for axis in ("gx", "gy", "gz")]
     cell_total = orbitals[0].size * lax.axis_size("gx") * lax.axis_size("gy") * lax.axis_size("gz")
     flags = jnp.stack(
-        [at[0] % 2, at[1] % 2, at[2] % 2, (at[2] > 0).astype(jnp.int32), (at[2] < lax.axis_size("gz") - 1).astype(jnp.int32)]
+        [(at[0] + at[1]) % 2, at[1] % 2, at[2] % 2, (at[2] > 0).astype(jnp.int32), (at[2] < lax.axis_size("gz") - 1).astype(jnp.int32)]
     ).astype(jnp.int32)
     shape = orbitals.shape
     orbitals = orbitals.reshape(BLOCK, LANES)
@@ -256,7 +283,7 @@
     field, edge_potential = call(extend_kernel, (sent, (8, LANES)))(flags, orbitals, second, first)
 
     def advance(field, scale, previous, split):
-        y2, y1, x2, x1 = [swap(field, axis, first) for axis in ("gy", "gx") for first in (1, 0)]
+        y2, y1, x2, x1 = swap(field, "gy", 1), swap(field, "gy", 0), swap_x(field, 1), swap_x(field, 0)
         kernel = functools.partial(step_kernel, scale, bool(previous), split)
         outs = (block, edge) if split else (sent,)
         return call(kernel, outs)(flags, potential, edge_potential, field, y1, x2, y2, x1, *previous)
@@ -264,8 +291,8 @@
     (field1,) = advance(field, 1.0 / HALF, (), False)
     (field2,) = advance(field1, 2.0 / HALF, (field,), False)
     field, edge = advance(field2, 2.0 / HALF, (field1,), True)
-    after_y, after_x = from_above(field, "gy"), from_above(field, "gx")
-    sums = call(sums_kernel, ((ORB, LANES),), smem=False)(potential, field, edge, after_y, after_x)[0]
+    after_y, beside_x = from_above(field, "gy"), one_side_x(field)
+    sums = call(sums_kernel, ((ORB, LANES),))(flags, potential, field, edge, after_y, beside_x)[0]
     sums = sum_everywhere(sums)
     q_block, ritz = call(functools.partial(finish_kernel, cell_total), (block, (ORB, ORB)), smem=False)(sums, field)
     return q_block.reshape(shape), ritz

time: 133 us -> 131 us (0.985)
  starting transfers between devices: 46.9 us -> 51.1 us
  blocking collectives: 59.9 us -> 56.1 us
  waiting for transfers between devices: 12.8 us -> 9.76 us
    ppermute x0 -> x8, starting transfers between devices: none -> 17.7 us  [the longest x6 11.7 us: swap_x(): return lax.ppermute(value, ('gx', 'gy'), pairs)]
    ppermute x14 -> x8, starting transfers between devices: 44.4 us -> 32.1 us  [swap(): return lax.ppermute(value, axis, pairs)]
    ppermute x2 -> x1, waiting for transfers between devices: 8.12 us -> 0.01 us  [from_above(): lax.ppermute(value, axis, [(i + 1, i) for i in range(lax.axis_size(axis)...]
    ppermute x0 -> x8, waiting for transfers between devices: none -> 5.08 us  [the longest x1 4.26 us: one_side_x(): return lax.ppermute(value, ('gx', 'gy'), pairs)]
    psum x1, blocking collectives: 13.6 us -> 12.2 us  [sum_everywhere(): lax.psum(value, 'gy', axis_index_groups=[[0, 2, 4, 6], [1, 3, 5, 7]])]
    ppermute x14 -> x8, waiting for transfers between devices: 4.69 us -> 4.67 us  [swap(): return lax.ppermute(value, axis, pairs)]
  transfers between devices with their start and end apart: 16 -> 17, of which waited for: 5 -> 6; matrix products, arithmetic and copies ran while one was open for 0% -> 0% of each run, Pallas kernels for 0% -> 0%
where the time goes in v1:
time: 131 us
  blocking collectives  56.1 us (43%)
  starting transfers between devices  51.1 us (39%)
  Pallas kernels  11.2 us (9%)
  waiting for transfers between devices  9.76 us (7%)
  local copies, waits for them, and re-layouts  1.59 us (1%)
    ppermute x8, starting transfers between devices, swap(): return lax.ppermute(value, axis, pairs)  32.1 us
    psum x1, blocking collectives, sum_everywhere(): return lax.psum(value, ('gx', 'gz'), axis_index_groups=rings)  15.7 us
    psum x1, blocking collectives, sum_everywhere(): value = lax.psum(value, 'gz', axis_index_groups=fours)  15.4 us
    psum x1, blocking collectives, sum_everywhere(): value = lax.psum(value, 'gx', axis_index_groups=fours)  12.8 us
    psum x1, blocking collectives, sum_everywhere(): lax.psum(value, 'gy', axis_index_groups=[[0, 2, 4, 6], [1, 3, 5, 7]])  12.2 us
    ppermute x6, starting transfers between devices, swap_x(): return lax.ppermute(value, ('gx', 'gy'), pairs)  11.7 us
    pallas_call x7, Pallas kernels, run(): pl.pallas_call(kernel, out_shape=[jax.ShapeDtypeStruct(shape, jnp.float32...  11.2 us
    ppermute x1, starting transfers between devices, sum_everywhere(): value = value + lax.ppermute(value, 'gy', [(i, i ^ 1) for i in range(8)])  4.78 us
  transfers between devices with their start and end apart: 17, of which 6 were waited for; matrix products, arithmetic and copies ran while one was open for 0% of the time, Pallas kernels for 0%

profile of v1, /device:TPU:2, one launch (start us, length us, event | category | flops | bytes accessed | tf_op | source)
XLA Modules:
  0.0 130.7 jit_solution(4734557907836071114)
XLA Ops:
  1.4 0.9 copy-done
  2.3 0.7 shard_map.41
  3.0 3.4 %collective-permute-start = (f32[40,128]{1,0:T(8,128)S(1)}, f32[40,128]{1,0:T(8,128)S(1)}, u32[]{:S(2)}, u32[]{:S(2)}) collective-permute-start(f32[40,128]{1,0:T(8,128)S(1)} %get-tuple-element.10), channel_id=1, source_target_pairs={{1,2},{2,1},{3,4},{4,3},{5,6},{6,5},{9,10},{10,9},{11,12},{12,11},... | collective-permute-start | bytes 61448 | tf_op jit(solution)/shard_map/ppermute | solution.py:216
  6.4 5.1 %collective-permute-start.1 = (f32[40,128]{1,0:T(8,128)S(1)}, f32[40,128]{1,0:T(8,128)S(1)}, u32[]{:S(2)}, u32[]{:S(2)}) collective-permute-start(f32[40,128]{1,0:T(8,128)S(1)} %get-tuple-element.11), channel_id=1, source_target_pairs={{0,1},{1,0},{2,3},{3,2},{4,5},{5,4},{6,7},{7,6},{8,9},{9,8},{10,11... | collective-permute-start | bytes 61448 | tf_op jit(solution)/shard_map/ppermute | solution.py:216
  11.5 1.7 %collective-permute-done.1.first = f32[40,128]{1,0:T(8,128)S(1)} collective-permute-done((f32[40,128]{1,0:T(8,128)S(1)}, f32[40,128]{1,0:T(8,128)S(1)}, u32[]{:S(2)}, u32[]{:S(2)}) %collective-permute-start.1) | collective-permute-done | bytes 20512 | tf_op jit(solution)/shard_map/ppermute | solution.py:216
  13.2 0.8 shard_map.42
  14.0 2.7 %collective-permute-start.5 = (f32[320,128]{1,0:T(8,128)S(1)}, f32[320,128]{1,0:T(8,128)S(1)}, u32[]{:S(2)}, u32[]{:S(2)}) collective-permute-start(f32[320,128]{1,0:T(8,128)S(1)} %get-tuple-element.13.field.rest_0_), channel_id=1, source_target_pairs={{0,64},{64,0},{128,192},{192,128},{256,320},{320,256},{384,448},{4... | collective-permute-start | bytes 491528 | tf_op jit(solution)/shard_map/ppermute | solution.py:225
  17.4 0.7 collective-permute-start.3
  18.1 6.1 %collective-permute-start.2 = (f32[320,128]{1,0:T(8,128)S(1)}, f32[320,128]{1,0:T(8,128)S(1)}, u32[]{:S(2)}, u32[]{:S(2)}) collective-permute-start(f32[320,128]{1,0:T(8,128)S(1)} %get-tuple-element.13.field.rest_0_), channel_id=1, source_target_pairs={{0,8},{8,0},{16,24},{24,16},{32,40},{40,32},{48,56},{56,48},{1,9},... | collective-permute-start | bytes 491528 | tf_op jit(solution)/shard_map/ppermute | solution.py:216
  24.2 1.0 collective-permute-done.2.y1
  25.2 2.0 %shard_map.43.field.rest_0_ = f32[320,128]{1,0:T(8,128)S(1)} custom-call(s32[5]{0:T(128)S(1)} %stack.31.flags, f32[16,128]{1,0:T(8,128)S(1)} %bitcast.11, f32[8,128]{1,0:T(8,128)S(1)} %get-tuple-element.12.edge_potential, f32[320,128]{1,0:T(8,128)S(1)} %get-tuple-element.13.field.rest_0_, f32[320,128]{1,0:T(8,128)S(1)} %collective-permute-done.2.y1, ...), custom_call_target="tpu_custom_call" | custom-call | tf_op jit(solution)/shard_map/pallas_call | solution.py:259
  27.2 3.6 %collective-permute-start.9 = (f32[320,128]{1,0:T(8,128)S(1)}, f32[320,128]{1,0:T(8,128)S(1)}, u32[]{:S(2)}, u32[]{:S(2)}) collective-permute-start(f32[320,128]{1,0:T(8,128)S(1)} %shard_map.43.field.rest_0_), channel_id=1, source_target_pairs={{0,64},{64,0},{128,192},{192,128},{256,320},{320,256},{384,448},{4... | collective-permute-start | bytes 491528 | tf_op jit(solution)/shard_map/ppermute | solution.py:225
  31.5 0.7 collective-permute-start.7
  32.2 7.2 %collective-permute-start.6 = (f32[320,128]{1,0:T(8,128)S(1)}, f32[320,128]{1,0:T(8,128)S(1)}, u32[]{:S(2)}, u32[]{:S(2)}) collective-permute-start(f32[320,128]{1,0:T(8,128)S(1)} %shard_map.43.field.rest_0_), channel_id=1, source_target_pairs={{0,8},{8,0},{16,24},{24,16},{32,40},{40,32},{48,56},{56,48},{1,9},... | collective-permute-start | bytes 491528 | tf_op jit(solution)/shard_map/ppermute | solution.py:216
  39.4 1.0 collective-permute-done.6.y1
  40.4 2.0 %shard_map.44.field = f32[320,128]{1,0:T(8,128)S(1)} custom-call(s32[5]{0:T(128)S(1)} %stack.31.flags, f32[16,128]{1,0:T(8,128)S(1)} %bitcast.12, f32[8,128]{1,0:T(8,128)S(1)} %get-tuple-element.12.edge_potential, f32[320,128]{1,0:T(8,128)S(1)} %shard_map.43.field.rest_0_, f32[320,128]{1,0:T(8,128)S(1)} %collective-permute-done.6.y1, ...), custom_call_target="tpu_custom_call" | custom-call | tf_op jit(solution)/shard_map/pallas_call | solution.py:259
  42.4 3.4 %collective-permute-start.13 = (f32[320,128]{1,0:T(8,128)S(1)}, f32[320,128]{1,0:T(8,128)S(1)}, u32[]{:S(2)}, u32[]{:S(2)}) collective-permute-start(f32[320,128]{1,0:T(8,128)S(1)} %shard_map.44.field), channel_id=1, source_target_pairs={{0,64},{64,0},{128,192},{192,128},{256,320},{320,256},{384,448},{4... | collective-permute-start | bytes 491528 | tf_op jit(solution)/shard_map/ppermute | solution.py:225
  46.4 0.7 collective-permute-start.11
  47.1 8.4 %collective-permute-start.10 = (f32[320,128]{1,0:T(8,128)S(1)}, f32[320,128]{1,0:T(8,128)S(1)}, u32[]{:S(2)}, u32[]{:S(2)}) collective-permute-start(f32[320,128]{1,0:T(8,128)S(1)} %shard_map.44.field), channel_id=1, source_target_pairs={{0,8},{8,0},{16,24},{24,16},{32,40},{40,32},{48,56},{56,48},{1,9},... | collective-permute-start | bytes 491528 | tf_op jit(solution)/shard_map/ppermute | solution.py:216
  55.5 1.0 collective-permute-done.10.y1
  56.5 2.0 %shard_map.45 = (f32[256,128]{1,0:T(8,128)S(1)}, f32[64,128]{1,0:T(8,128)S(1)}) custom-call(s32[5]{0:T(128)S(1)} %stack.31.flags, f32[16,128]{1,0:T(8,128)S(1)} %bitcast.13, f32[8,128]{1,0:T(8,128)S(1)} %get-tuple-element.12.edge_potential, f32[320,128]{1,0:T(8,128)S(1)} %shard_map.44.field, f32[320,128]{1,0:T(8,128)S(1)} %collective-permute-done.10.y1, ...), custom_call_target="tpu_custom_call" | custom-call | tf_op jit(solution)/shard_map/pallas_call | solution.py:259
  58.5 1.3 collective-permute-start.15
  59.8 1.3 collective-permute-start.14
  61.1 4.3 %collective-permute-done.15.beside_x = f32[256,128]{1,0:T(8,128)S(1)} collective-permute-done((f32[256,128]{1,0:T(8,128)S(1)}, f32[256,128]{1,0:T(8,128)S(1)}, u32[]{:S(2)}, u32[]{:S(2)}) %collective-permute-start.15) | collective-permute-done | bytes 131104 | tf_op jit(solution)/shard_map/ppermute | solution.py:235
  65.4 1.2 shard_map.46
  66.5 4.8 %collective-permute-start.16 = (f32[16,128]{1,0:T(8,128)S(1)}, f32[16,128]{1,0:T(8,128)S(1)}, u32[]{:S(2)}, u32[]{:S(2)}) collective-permute-start(f32[16,128]{1,0:T(8,128)S(1)} %shard_map.46), channel_id=1, source_target_pairs={{0,8},{8,0},{16,24},{24,16},{32,40},{40,32},{48,56},{56,48},{1,9},... | collective-permute-start | bytes 24584 | tf_op jit(solution)/shard_map/ppermute | solution.py:245
  71.3 0.8 collective-permute-done.16
  72.1 12.2 %psum.28 = f32[16,128]{1,0:T(8,128)S(1)} all-reduce(f32[16,128]{1,0:T(8,128)S(1)} %add.28), channel_id=1, replica_groups={{0,16,32,48},{8,24,40,56},{1,17,33,49},{9,25,41,57},{2,18,34,50},{10,26..., use_global_device_ids=true, to_apply=%region_0.1 | all-reduce | flops 2048 | bytes 16384 | tf_op jit(solution)/shard_map/psum | solution.py:246
  84.3 15.4 %psum.29 = f32[16,128]{1,0:T(8,128)S(1)} all-reduce(f32[16,128]{1,0:T(8,128)S(1)} %psum.28), channel_id=1, replica_groups={{0,1,2,3},{4,5,6,7},{8,9,10,11},{12,13,14,15},{16,17,18,19},{20,21,22,2..., use_global_device_ids=true, to_apply=%region_1.2 | all-reduce | flops 2048 | bytes 16384 | tf_op jit(solution)/shard_map/psum | solution.py:247
  99.8 12.8 %psum.30 = f32[16,128]{1,0:T(8,128)S(1)} all-reduce(f32[16,128]{1,0:T(8,128)S(1)} %psum.29), channel_id=1, replica_groups={{0,64,128,192},{256,320,384,448},{1,65,129,193},{257,321,385,449},{2,66..., use_global_device_ids=true, to_apply=%region_2.3 | all-reduce | flops 2048 | bytes 16384 | tf_op jit(solution)/shard_map/psum | solution.py:248
  112.5 15.7 %psum.31.sums = f32[16,128]{1,0:T(8,128)S(1)} all-reduce(f32[16,128]{1,0:T(8,128)S(1)} %psum.30), channel_id=1, replica_groups={{0,256,4,260},{1,257,5,261},{2,258,6,262},{3,259,7,263},{64,320,68,324}..., use_global_device_ids=true, to_apply=%region_3.4 | all-reduce | flops 2048 | bytes 16384 | tf_op jit(solution)/shard_map/psum | solution.py:250
  128.2 2.5 %shard_map.47 = (f32[256,128]{1,0:T(8,128)}, f32[16,16]{1,0:T(8,128)}) custom-call(f32[16,128]{1,0:T(8,128)S(1)} %psum.31.sums, f32[256,128]{1,0:T(8,128)S(1)} %get-tuple-element.14.field), custom_call_target="tpu_custom_call" | custom-call | tf_op jit(solution)/shard_map/pallas_call | solution.py:259
  (19 shorter events, 2.7 us)
Async XLA Ops:
  0.7 0.7 copy-start.1
  1.4 0.9 copy-start
  3.0 8.5 %collective-permute-start = (f32[40,128]{1,0:T(8,128)S(1)}, f32[40,128]{1,0:T(8,128)S(1)}, u32[]{:S(2)}, u32[]{:S(2)}) collective-permute-start(f32[40,128]{1,0:T(8,128)S(1)} %get-tuple-element.10), channel_id=1, source_target_pairs={{1,2},{2,1},{3,4},{4,3},{5,6},{6,5},{9,10},{10,9},{11,12},{12,11},... | collective-permute-start | bytes 61448 | tf_op jit(solution)/shard_map/ppermute | solution.py:216
  6.4 6.8 %collective-permute-start.1 = (f32[40,128]{1,0:T(8,128)S(1)}, f32[40,128]{1,0:T(8,128)S(1)}, u32[]{:S(2)}, u32[]{:S(2)}) collective-permute-start(f32[40,128]{1,0:T(8,128)S(1)} %get-tuple-element.11), channel_id=1, source_target_pairs={{0,1},{1,0},{2,3},{3,2},{4,5},{5,4},{6,7},{7,6},{8,9},{9,8},{10,11... | collective-permute-start | bytes 61448 | tf_op jit(solution)/shard_map/ppermute | solution.py:216
  14.0 10.1 %collective-permute-start.5 = (f32[320,128]{1,0:T(8,128)S(1)}, f32[320,128]{1,0:T(8,128)S(1)}, u32[]{:S(2)}, u32[]{:S(2)}) collective-permute-start(f32[320,128]{1,0:T(8,128)S(1)} %get-tuple-element.13.field.rest_0_), channel_id=1, source_target_pairs={{0,64},{64,0},{128,192},{192,128},{256,320},{320,256},{384,448},{4... | collective-permute-start | bytes 491528 | tf_op jit(solution)/shard_map/ppermute | solution.py:225
  16.7 7.5 %collective-permute-start.4 = (f32[320,128]{1,0:T(8,128)S(1)}, f32[320,128]{1,0:T(8,128)S(1)}, u32[]{:S(2)}, u32[]{:S(2)}) collective-permute-start(f32[320,128]{1,0:T(8,128)S(1)} %get-tuple-element.13.field.rest_0_), channel_id=1, source_target_pairs={{8,16},{16,8},{24,32},{32,24},{40,48},{48,40},{9,17},{17,9},{25,33... | collective-permute-start | bytes 491528 | tf_op jit(solution)/shard_map/ppermute | solution.py:216
  17.4 6.8 %collective-permute-start.3 = (f32[320,128]{1,0:T(8,128)S(1)}, f32[320,128]{1,0:T(8,128)S(1)}, u32[]{:S(2)}, u32[]{:S(2)}) collective-permute-start(f32[320,128]{1,0:T(8,128)S(1)} %get-tuple-element.13.field.rest_0_), channel_id=1, source_target_pairs={{64,128},{128,64},{192,256},{256,192},{320,384},{384,320},{8,72},{... | collective-permute-start | bytes 491528 | tf_op jit(solution)/shard_map/ppermute | solution.py:225
  18.1 7.1 %collective-permute-start.2 = (f32[320,128]{1,0:T(8,128)S(1)}, f32[320,128]{1,0:T(8,128)S(1)}, u32[]{:S(2)}, u32[]{:S(2)}) collective-permute-start(f32[320,128]{1,0:T(8,128)S(1)} %get-tuple-element.13.field.rest_0_), channel_id=1, source_target_pairs={{0,8},{8,0},{16,24},{24,16},{32,40},{40,32},{48,56},{56,48},{1,9},... | collective-permute-start | bytes 491528 | tf_op jit(solution)/shard_map/ppermute | solution.py:216
  27.2 12.2 %collective-permute-start.9 = (f32[320,128]{1,0:T(8,128)S(1)}, f32[320,128]{1,0:T(8,128)S(1)}, u32[]{:S(2)}, u32[]{:S(2)}) collective-permute-start(f32[320,128]{1,0:T(8,128)S(1)} %shard_map.43.field.rest_0_), channel_id=1, source_target_pairs={{0,64},{64,0},{128,192},{192,128},{256,320},{320,256},{384,448},{4... | collective-permute-start | bytes 491528 | tf_op jit(solution)/shard_map/ppermute | solution.py:225
  30.8 8.5 %collective-permute-start.8 = (f32[320,128]{1,0:T(8,128)S(1)}, f32[320,128]{1,0:T(8,128)S(1)}, u32[]{:S(2)}, u32[]{:S(2)}) collective-permute-start(f32[320,128]{1,0:T(8,128)S(1)} %shard_map.43.field.rest_0_), channel_id=1, source_target_pairs={{8,16},{16,8},{24,32},{32,24},{40,48},{48,40},{9,17},{17,9},{25,33... | collective-permute-start | bytes 491528 | tf_op jit(solution)/shard_map/ppermute | solution.py:216
  31.5 7.9 %collective-permute-start.7 = (f32[320,128]{1,0:T(8,128)S(1)}, f32[320,128]{1,0:T(8,128)S(1)}, u32[]{:S(2)}, u32[]{:S(2)}) collective-permute-start(f32[320,128]{1,0:T(8,128)S(1)} %shard_map.43.field.rest_0_), channel_id=1, source_target_pairs={{64,128},{128,64},{192,256},{256,192},{320,384},{384,320},{8,72},{... | collective-permute-start | bytes 491528 | tf_op jit(solution)/shard_map/ppermute | solution.py:225
  32.2 8.2 %collective-permute-start.6 = (f32[320,128]{1,0:T(8,128)S(1)}, f32[320,128]{1,0:T(8,128)S(1)}, u32[]{:S(2)}, u32[]{:S(2)}) collective-permute-start(f32[320,128]{1,0:T(8,128)S(1)} %shard_map.43.field.rest_0_), channel_id=1, source_target_pairs={{0,8},{8,0},{16,24},{24,16},{32,40},{40,32},{48,56},{56,48},{1,9},... | collective-permute-start | bytes 491528 | tf_op jit(solution)/shard_map/ppermute | solution.py:216
  42.4 13.1 %collective-permute-start.13 = (f32[320,128]{1,0:T(8,128)S(1)}, f32[320,128]{1,0:T(8,128)S(1)}, u32[]{:S(2)}, u32[]{:S(2)}) collective-permute-start(f32[320,128]{1,0:T(8,128)S(1)} %shard_map.44.field), channel_id=1, source_target_pairs={{0,64},{64,0},{128,192},{192,128},{256,320},{320,256},{384,448},{4... | collective-permute-start | bytes 491528 | tf_op jit(solution)/shard_map/ppermute | solution.py:225
  45.7 9.7 %collective-permute-start.12 = (f32[320,128]{1,0:T(8,128)S(1)}, f32[320,128]{1,0:T(8,128)S(1)}, u32[]{:S(2)}, u32[]{:S(2)}) collective-permute-start(f32[320,128]{1,0:T(8,128)S(1)} %shard_map.44.field), channel_id=1, source_target_pairs={{8,16},{16,8},{24,32},{32,24},{40,48},{48,40},{9,17},{17,9},{25,33... | collective-permute-start | bytes 491528 | tf_op jit(solution)/shard_map/ppermute | solution.py:216
  46.4 9.1 %collective-permute-start.11 = (f32[320,128]{1,0:T(8,128)S(1)}, f32[320,128]{1,0:T(8,128)S(1)}, u32[]{:S(2)}, u32[]{:S(2)}) collective-permute-start(f32[320,128]{1,0:T(8,128)S(1)} %shard_map.44.field), channel_id=1, source_target_pairs={{64,128},{128,64},{192,256},{256,192},{320,384},{384,320},{8,72},{... | collective-permute-start | bytes 491528 | tf_op jit(solution)/shard_map/ppermute | solution.py:225
  47.1 9.4 %collective-permute-start.10 = (f32[320,128]{1,0:T(8,128)S(1)}, f32[320,128]{1,0:T(8,128)S(1)}, u32[]{:S(2)}, u32[]{:S(2)}) collective-permute-start(f32[320,128]{1,0:T(8,128)S(1)} %shard_map.44.field), channel_id=1, source_target_pairs={{0,8},{8,0},{16,24},{24,16},{32,40},{40,32},{48,56},{56,48},{1,9},... | collective-permute-start | bytes 491528 | tf_op jit(solution)/shard_map/ppermute | solution.py:216
  58.5 6.9 %collective-permute-start.15 = (f32[256,128]{1,0:T(8,128)S(1)}, f32[256,128]{1,0:T(8,128)S(1)}, u32[]{:S(2)}, u32[]{:S(2)}) collective-permute-start(f32[256,128]{1,0:T(8,128)S(1)} %get-tuple-element.14.field), channel_id=1, source_target_pairs={{64,0},{128,64},{192,128},{256,192},{320,256},{384,320},{448,384},... | collective-permute-start | bytes 393224 | tf_op jit(solution)/shard_map/ppermute | solution.py:235
  59.8 5.6 %collective-permute-start.14 = (f32[256,128]{1,0:T(8,128)S(1)}, f32[256,128]{1,0:T(8,128)S(1)}, u32[]{:S(2)}, u32[]{:S(2)}) collective-permute-start(f32[256,128]{1,0:T(8,128)S(1)} %get-tuple-element.14.field), channel_id=1, source_target_pairs={{8,0},{16,8},{24,16},{32,24},{40,32},{48,40},{56,48},{9,1},{17,9},... | collective-permute-start | bytes 393224 | tf_op jit(solution)/shard_map/ppermute | solution.py:239
  66.5 5.6 %collective-permute-start.16 = (f32[16,128]{1,0:T(8,128)S(1)}, f32[16,128]{1,0:T(8,128)S(1)}, u32[]{:S(2)}, u32[]{:S(2)}) collective-permute-start(f32[16,128]{1,0:T(8,128)S(1)} %shard_map.46), channel_id=1, source_target_pairs={{0,8},{8,0},{16,24},{24,16},{32,40},{40,32},{48,56},{56,48},{1,9},... | collective-permute-start | bytes 24584 | tf_op jit(solution)/shard_map/ppermute | solution.py:245

commit v2 on v1

--- a/solution.py
+++ b/solution.py
@@ -91,26 +91,20 @@
     return ref[x * ORB : (x + 1) * ORB, :]
 
 
-def step_kernel(scale, with_previous, split, flags, potential, edge_potential, field, y1, x2, y2, x1, *rest):
+def sides(is_above, get):
+    layers = [get(i) for i in range(SIDE)]
+    return [jnp.where(is_above, 0.0, v) for v in layers], [jnp.where(is_above, v, 0.0) for v in layers]
+
+
+def block_kernel(scale, with_previous, flags, potential, field, *rest):
     previous = rest[0] if with_previous else None
-    out = rest[-2] if split else rest[-1]
+    y2, x1, out = rest[-3:]
     lane = lane_index(ORB)
-    place = lane % (2 * EXT)
-    lane_y = ((lane + EXT) // (2 * EXT)) % SIDE
-    inside = ((place < EXT) & (flags[4] != 0)) | ((place >= EXT) & (flags[3] != 0))
-    window = (lane < EXT) | (lane >= LANES - EXT)
-    even_x, even_y = flags[0] == 0, flags[1] == 0
     weight = [-0.5 * scale * w for w in WEIGHTS]
     shift = MIDDLE + 1.5 * WEIGHTS[0]
-
-    def line(get, one, two, even):
-        pairs = [(get(one, i), get(two, i)) for i in range(SIDE)]
-        below = [jnp.where(even, b, a) for a, b in pairs]
-        above = [jnp.where(even, a, b) for a, b in pairs]
-        return below + [get(field, i) for i in range(SIDE)] + above
-
     for y in range(SIDE):
-        along = line(lambda ref, x: rows_of(ref, x * SIDE + y), x1, x2, even_x)
+        below, above = sides(flags[0] == 0, lambda x: rows_of(x1, x * SIDE + y))
+        along = below + [rows_of(field, x * SIDE + y) for x in range(SIDE)] + above
         for x in range(SIDE):
             cell = x * SIDE + y
             here = along[SIDE + x]
@@ -125,14 +119,45 @@
                 total = total - rows_of(previous, cell)
             out[cell * ORB : (cell + 1) * ORB, :] = total
     for x in range(SIDE):
-        along = line(lambda ref, y: rows_of(ref, x * SIDE + y), y1, y2, even_y)
+        below, above = sides(flags[1] != 0, lambda y: rows_of(y2, x * SIDE + y))
+        along = below + [rows_of(field, x * SIDE + y) for y in range(SIDE)] + above
         for y in range(SIDE):
             cell = x * SIDE + y
             total = rows_of(out, cell)
             for k in range(1, 5):
                 total = total + weight[k] * (along[SIDE + y + k] + along[SIDE + y - k])
             out[cell * ORB : (cell + 1) * ORB, :] = total
-    along = line(lambda ref, x: edge_of(ref, CELLS + x), x1, x2, even_x)
+
+
+def join_kernel(scale, with_previous, split, flags, edge_potential, part, field, y1, x2, y2, x1, *rest):
+    previous = rest[0] if with_previous else None
+    out = rest[-2] if split else rest[-1]
+    lane = lane_index(ORB)
+    place = lane % (2 * EXT)
+    lane_y = ((lane + EXT) // (2 * EXT)) % SIDE
+    inside = ((place < EXT) & (flags[4] != 0)) | ((place >= EXT) & (flags[3] != 0))
+    window = (lane < EXT) | (lane >= LANES - EXT)
+    even_x, even_y = flags[0] == 0, flags[1] == 0
+    weight = [-0.5 * scale * w for w in WEIGHTS]
+    shift = MIDDLE + 1.5 * WEIGHTS[0]
+
+    def face_terms(below, above, i):
+        terms = [weight[k] * above[i + k - SIDE] for k in range(SIDE - i, 5)]
+        return sum(terms + [weight[k] * below[i - k + SIDE] for k in range(i + 1, 5)])
+
+    for y in range(SIDE):
+        below, above = sides(flags[0] != 0, lambda x: rows_of(x2, x * SIDE + y))
+        for x in range(SIDE):
+            cell = x * SIDE + y
+            out[cell * ORB : (cell + 1) * ORB, :] = rows_of(part, cell) + face_terms(below, above, x)
+    for x in range(SIDE):
+        below, above = sides(even_y, lambda y: rows_of(y1, x * SIDE + y))
+        for y in range(SIDE):
+            cell = x * SIDE + y
+            out[cell * ORB : (cell + 1) * ORB, :] = rows_of(out, cell) + face_terms(below, above, y)
+    pairs = [(edge_of(x1, CELLS + x), edge_of(x2, CELLS + x)) for x in range(SIDE)]
+    along = [jnp.where(even_x, b, a) for a, b in pairs]
+    along = along + [edge_of(field, CELLS + x) for x in range(SIDE)] + [jnp.where(even_x, a, b) for a, b in pairs]
     for x in range(SIDE):
         here = along[SIDE + x]
         one, two = edge_of(y1, CELLS + x), edge_of(y2, CELLS + x)
@@ -142,12 +167,12 @@
             there = there + rolled(jnp.where(window, rows_of(field, x * SIDE + y), 0.0), 2 * EXT * y)
         total = (edge_potential[x : x + 1, :] - shift) * scale * here
         for k in range(1, 5):
-            pairs = along[SIDE + x + k] + along[SIDE + x - k]
-            pairs = pairs + rolled(jnp.where(lane_y < k, above, here), -2 * EXT * k)
-            pairs = pairs + rolled(jnp.where(lane_y >= SIDE - k, below, here), 2 * EXT * k)
-            pairs = pairs + rolled(jnp.where(place < k, there, here), -k)
-            pairs = pairs + rolled(jnp.where(place >= 2 * EXT - k, there, here), k)
-            total = total + weight[k] * pairs
+            terms = along[SIDE + x + k] + along[SIDE + x - k]
+            terms = terms + rolled(jnp.where(lane_y < k, above, here), -2 * EXT * k)
+            terms = terms + rolled(jnp.where(lane_y >= SIDE - k, below, here), 2 * EXT * k)
+            terms = terms + rolled(jnp.where(place < k, there, here), -k)
+            terms = terms + rolled(jnp.where(place >= 2 * EXT - k, there, here), k)
+            total = total + weight[k] * terms
         if with_previous:
             total = total - edge_of(previous, CELLS + x)
         total = jnp.where(inside, total, 0.0)
@@ -284,9 +309,11 @@
 
     def advance(field, scale, previous, split):
         y2, y1, x2, x1 = swap(field, "gy", 1), swap(field, "gy", 0), swap_x(field, 1), swap_x(field, 0)
-        kernel = functools.partial(step_kernel, scale, bool(previous), split)
+        kernel = functools.partial(block_kernel, scale, bool(previous))
+        (part,) = call(kernel, (block,))(flags, potential, field, *previous, y2, x1)
+        kernel = functools.partial(join_kernel, scale, bool(previous), split)
         outs = (block, edge) if split else (sent,)
-        return call(kernel, outs)(flags, potential, edge_potential, field, y1, x2, y2, x1, *previous)
+        return call(kernel, outs)(flags, edge_potential, part, field, y1, x2, y2, x1, *previous)
 
     (field1,) = advance(field, 1.0 / HALF, (), False)
     (field2,) = advance(field1, 2.0 / HALF, (field,), False)

time: 131 us -> 128 us (0.977)
  waiting for transfers between devices: 9.76 us -> 6.84 us
    ppermute x8, waiting for transfers between devices: 4.67 us -> 1.75 us  [swap(): return lax.ppermute(value, axis, pairs)]
    pallas_call x7 -> x10, Pallas kernels: 11.2 us -> 12.1 us  [run(): pl.pallas_call(kernel, out_shape=[jax.ShapeDtypeStruct(shape, jnp.float32...]
  transfers between devices with their start and end apart: 17 -> 17, of which waited for: 6 -> 3; matrix products, arithmetic and copies ran while one was open for 0% -> 0% of each run, Pallas kernels for 0% -> 4%
where the time goes in v2:
time: 128 us; the launch traced here: 127 us
  blocking collectives  55.7 us (44%)
  starting transfers between devices  50.1 us (39%)
  Pallas kernels  12.1 us (9%)
  waiting for transfers between devices  6.84 us (5%)
  local copies, waits for them, and re-layouts  1.59 us (1%)
    ppermute x8, starting transfers between devices, swap(): return lax.ppermute(value, axis, pairs)  31 us
    psum x1, blocking collectives, sum_everywhere(): return lax.psum(value, ('gx', 'gz'), axis_index_groups=rings)  15.7 us
    psum x1, blocking collectives, sum_everywhere(): value = lax.psum(value, 'gz', axis_index_groups=fours)  15.4 us
    psum x1, blocking collectives, sum_everywhere(): value = lax.psum(value, 'gx', axis_index_groups=fours)  12.4 us
    psum x1, blocking collectives, sum_everywhere(): lax.psum(value, 'gy', axis_index_groups=[[0, 2, 4, 6], [1, 3, 5, 7]])  12.2 us
    pallas_call x10, Pallas kernels, run(): pl.pallas_call(kernel, out_shape=[jax.ShapeDtypeStruct(shape, jnp.float32...  12.1 us
    ppermute x6, starting transfers between devices, swap_x(): return lax.ppermute(value, ('gx', 'gy'), pairs)  11.9 us
    ppermute x1, starting transfers between devices, sum_everywhere(): value = value + lax.ppermute(value, 'gy', [(i, i ^ 1) for i in range(8)])  4.61 us
  transfers between devices with their start and end apart: 17, of which 3 were waited for; matrix products, arithmetic and copies ran while one was open for 0% of the time, Pallas kernels for 4%

profile of v2, /device:TPU:2, one launch (start us, length us, event | category | flops | bytes accessed | tf_op | source)
XLA Modules:
  0.0 127.3 jit_solution(17161739427220356554)
XLA Ops:
  1.4 0.9 copy-done
  2.3 0.7 shard_map.41
  3.0 3.4 %collective-permute-start = (f32[40,128]{1,0:T(8,128)S(1)}, f32[40,128]{1,0:T(8,128)S(1)}, u32[]{:S(2)}, u32[]{:S(2)}) collective-permute-start(f32[40,128]{1,0:T(8,128)S(1)} %get-tuple-element.10), channel_id=1, source_target_pairs={{1,2},{2,1},{3,4},{4,3},{5,6},{6,5},{9,10},{10,9},{11,12},{12,11},... | collective-permute-start | bytes 61448 | tf_op jit(solution)/shard_map/ppermute | solution.py:241
  6.4 5.1 %collective-permute-start.1 = (f32[40,128]{1,0:T(8,128)S(1)}, f32[40,128]{1,0:T(8,128)S(1)}, u32[]{:S(2)}, u32[]{:S(2)}) collective-permute-start(f32[40,128]{1,0:T(8,128)S(1)} %get-tuple-element.11), channel_id=1, source_target_pairs={{0,1},{1,0},{2,3},{3,2},{4,5},{5,4},{6,7},{7,6},{8,9},{9,8},{10,11... | collective-permute-start | bytes 61448 | tf_op jit(solution)/shard_map/ppermute | solution.py:241
  11.5 1.7 %collective-permute-done.1.first = f32[40,128]{1,0:T(8,128)S(1)} collective-permute-done((f32[40,128]{1,0:T(8,128)S(1)}, f32[40,128]{1,0:T(8,128)S(1)}, u32[]{:S(2)}, u32[]{:S(2)}) %collective-permute-start.1) | collective-permute-done | bytes 20512 | tf_op jit(solution)/shard_map/ppermute | solution.py:241
  13.2 0.8 shard_map.42
  14.0 2.7 %collective-permute-start.3 = (f32[320,128]{1,0:T(8,128)S(1)}, f32[320,128]{1,0:T(8,128)S(1)}, u32[]{:S(2)}, u32[]{:S(2)}) collective-permute-start(f32[320,128]{1,0:T(8,128)S(1)} %get-tuple-element.13.field.rest_0_), channel_id=1, source_target_pairs={{0,64},{64,0},{128,192},{192,128},{256,320},{320,256},{384,448},{4... | collective-permute-start | bytes 491528 | tf_op jit(solution)/shard_map/ppermute | solution.py:250
  16.7 0.7 collective-permute-start.2
  17.4 0.7 collective-permute-start.5
  18.1 6.1 %collective-permute-start.4 = (f32[320,128]{1,0:T(8,128)S(1)}, f32[320,128]{1,0:T(8,128)S(1)}, u32[]{:S(2)}, u32[]{:S(2)}) collective-permute-start(f32[320,128]{1,0:T(8,128)S(1)} %get-tuple-element.13.field.rest_0_), channel_id=1, source_target_pairs={{0,8},{8,0},{16,24},{24,16},{32,40},{40,32},{48,56},{56,48},{1,9},... | collective-permute-start | bytes 491528 | tf_op jit(solution)/shard_map/ppermute | solution.py:241
  24.2 1.5 %shard_map.43.part = f32[256,128]{1,0:T(8,128)S(1)} custom-call(s32[5]{0:T(128)S(1)} %stack.31.flags, f32[16,128]{1,0:T(8,128)S(1)} %bitcast.11, f32[320,128]{1,0:T(8,128)S(1)} %get-tuple-element.13.field.rest_0_, f32[320,128]{1,0:T(8,128)S(1)} %collective-permute-done.2.rest_0_.y2, f32[320,128]{1,0:T(8,128)S(1)} %collective-permute-done.3.rest_1_.x1), custom_call_target="tpu_custom_call" | custom-call | tf_op jit(solution)/shard_map/pallas_call | solution.py:284
  25.7 0.8 shard_map.44.field.rest_0_
  26.5 3.6 %collective-permute-start.7 = (f32[320,128]{1,0:T(8,128)S(1)}, f32[320,128]{1,0:T(8,128)S(1)}, u32[]{:S(2)}, u32[]{:S(2)}) collective-permute-start(f32[320,128]{1,0:T(8,128)S(1)} %shard_map.44.field.rest_0_), channel_id=1, source_target_pairs={{0,64},{64,0},{128,192},{192,128},{256,320},{320,256},{384,448},{4... | collective-permute-start | bytes 491528 | tf_op jit(solution)/shard_map/ppermute | solution.py:250
  30.2 0.7 collective-permute-start.6
  31.5 6.6 %collective-permute-start.8 = (f32[320,128]{1,0:T(8,128)S(1)}, f32[320,128]{1,0:T(8,128)S(1)}, u32[]{:S(2)}, u32[]{:S(2)}) collective-permute-start(f32[320,128]{1,0:T(8,128)S(1)} %shard_map.44.field.rest_0_), channel_id=1, source_target_pairs={{0,8},{8,0},{16,24},{24,16},{32,40},{40,32},{48,56},{56,48},{1,9},... | collective-permute-start | bytes 491528 | tf_op jit(solution)/shard_map/ppermute | solution.py:241
  38.2 1.5 %shard_map.45.part = f32[256,128]{1,0:T(8,128)S(1)} custom-call(s32[5]{0:T(128)S(1)} %stack.31.flags, f32[16,128]{1,0:T(8,128)S(1)} %bitcast.12, f32[320,128]{1,0:T(8,128)S(1)} %shard_map.44.field.rest_0_, f32[320,128]{1,0:T(8,128)S(1)} %get-tuple-element.13.field.rest_0_, f32[320,128]{1,0:T(8,128)S(1)} %collective-permute-done.6.rest_1_.y2, ...), custom_call_target="tpu_custom_call" | custom-call | tf_op jit(solution)/shard_map/pallas_call | solution.py:284
  39.7 0.8 shard_map.46.field
  40.5 3.5 %collective-permute-start.11 = (f32[320,128]{1,0:T(8,128)S(1)}, f32[320,128]{1,0:T(8,128)S(1)}, u32[]{:S(2)}, u32[]{:S(2)}) collective-permute-start(f32[320,128]{1,0:T(8,128)S(1)} %shard_map.46.field), channel_id=1, source_target_pairs={{0,64},{64,0},{128,192},{192,128},{256,320},{320,256},{384,448},{4... | collective-permute-start | bytes 491528 | tf_op jit(solution)/shard_map/ppermute | solution.py:250
  45.4 7.8 %collective-permute-start.12 = (f32[320,128]{1,0:T(8,128)S(1)}, f32[320,128]{1,0:T(8,128)S(1)}, u32[]{:S(2)}, u32[]{:S(2)}) collective-permute-start(f32[320,128]{1,0:T(8,128)S(1)} %shard_map.46.field), channel_id=1, source_target_pairs={{0,8},{8,0},{16,24},{24,16},{32,40},{40,32},{48,56},{56,48},{1,9},... | collective-permute-start | bytes 491528 | tf_op jit(solution)/shard_map/ppermute | solution.py:241
  53.3 1.5 %shard_map.47.part = f32[256,128]{1,0:T(8,128)S(1)} custom-call(s32[5]{0:T(128)S(1)} %stack.31.flags, f32[16,128]{1,0:T(8,128)S(1)} %bitcast.13, f32[320,128]{1,0:T(8,128)S(1)} %shard_map.46.field, f32[320,128]{1,0:T(8,128)S(1)} %shard_map.44.field.rest_0_, f32[320,128]{1,0:T(8,128)S(1)} %collective-permute-done.10.rest_1_.y2, ...), custom_call_target="tpu_custom_call" | custom-call | tf_op jit(solution)/shard_map/pallas_call | solution.py:284
  54.8 0.8 shard_map.48
  55.6 1.3 %collective-permute-start.15 = (f32[256,128]{1,0:T(8,128)S(1)}, f32[256,128]{1,0:T(8,128)S(1)}, u32[]{:S(2)}, u32[]{:S(2)}) collective-permute-start(f32[256,128]{1,0:T(8,128)S(1)} %get-tuple-element.14.field), channel_id=1, source_target_pairs={{64,0},{128,64},{192,128},{256,192},{320,256},{384,320},{448,384},... | collective-permute-start | bytes 393224 | tf_op jit(solution)/shard_map/ppermute | solution.py:260
  56.9 1.3 %collective-permute-start.14 = (f32[256,128]{1,0:T(8,128)S(1)}, f32[256,128]{1,0:T(8,128)S(1)}, u32[]{:S(2)}, u32[]{:S(2)}) collective-permute-start(f32[256,128]{1,0:T(8,128)S(1)} %get-tuple-element.14.field), channel_id=1, source_target_pairs={{8,0},{16,8},{24,16},{32,24},{40,32},{48,40},{56,48},{9,1},{17,9},... | collective-permute-start | bytes 393224 | tf_op jit(solution)/shard_map/ppermute | solution.py:264
  58.2 4.3 %collective-permute-done.15.beside_x = f32[256,128]{1,0:T(8,128)S(1)} collective-permute-done((f32[256,128]{1,0:T(8,128)S(1)}, f32[256,128]{1,0:T(8,128)S(1)}, u32[]{:S(2)}, u32[]{:S(2)}) %collective-permute-start.15) | collective-permute-done | bytes 131104 | tf_op jit(solution)/shard_map/ppermute | solution.py:260
  62.5 1.2 shard_map.49
  63.6 4.6 %collective-permute-start.16 = (f32[16,128]{1,0:T(8,128)S(1)}, f32[16,128]{1,0:T(8,128)S(1)}, u32[]{:S(2)}, u32[]{:S(2)}) collective-permute-start(f32[16,128]{1,0:T(8,128)S(1)} %shard_map.49), channel_id=1, source_target_pairs={{0,8},{8,0},{16,24},{24,16},{32,40},{40,32},{48,56},{56,48},{1,9},... | collective-permute-start | bytes 24584 | tf_op jit(solution)/shard_map/ppermute | solution.py:270
  68.3 0.8 collective-permute-done.16
  69.1 12.2 %psum.28 = f32[16,128]{1,0:T(8,128)S(1)} all-reduce(f32[16,128]{1,0:T(8,128)S(1)} %add.28), channel_id=1, replica_groups={{0,16,32,48},{8,24,40,56},{1,17,33,49},{9,25,41,57},{2,18,34,50},{10,26..., use_global_device_ids=true, to_apply=%region_0.1 | all-reduce | flops 2048 | bytes 16384 | tf_op jit(solution)/shard_map/psum | solution.py:271
  81.3 15.4 %psum.29 = f32[16,128]{1,0:T(8,128)S(1)} all-reduce(f32[16,128]{1,0:T(8,128)S(1)} %psum.28), channel_id=1, replica_groups={{0,1,2,3},{4,5,6,7},{8,9,10,11},{12,13,14,15},{16,17,18,19},{20,21,22,2..., use_global_device_ids=true, to_apply=%region_1.2 | all-reduce | flops 2048 | bytes 16384 | tf_op jit(solution)/shard_map/psum | solution.py:272
  96.7 12.4 %psum.30 = f32[16,128]{1,0:T(8,128)S(1)} all-reduce(f32[16,128]{1,0:T(8,128)S(1)} %psum.29), channel_id=1, replica_groups={{0,64,128,192},{256,320,384,448},{1,65,129,193},{257,321,385,449},{2,66..., use_global_device_ids=true, to_apply=%region_2.3 | all-reduce | flops 2048 | bytes 16384 | tf_op jit(solution)/shard_map/psum | solution.py:273
  109.1 15.7 %psum.31.sums = f32[16,128]{1,0:T(8,128)S(1)} all-reduce(f32[16,128]{1,0:T(8,128)S(1)} %psum.30), channel_id=1, replica_groups={{0,256,4,260},{1,257,5,261},{2,258,6,262},{3,259,7,263},{64,320,68,324}..., use_global_device_ids=true, to_apply=%region_3.4 | all-reduce | flops 2048 | bytes 16384 | tf_op jit(solution)/shard_map/psum | solution.py:275
  124.8 2.5 %shard_map.50 = (f32[256,128]{1,0:T(8,128)}, f32[16,16]{1,0:T(8,128)}) custom-call(f32[16,128]{1,0:T(8,128)S(1)} %psum.31.sums, f32[256,128]{1,0:T(8,128)S(1)} %get-tuple-element.14.field), custom_call_target="tpu_custom_call" | custom-call | tf_op jit(solution)/shard_map/pallas_call | solution.py:284
  (22 shorter events, 2.7 us)
Async XLA Ops:
  0.7 0.7 copy-start.1
  1.4 0.9 copy-start
  3.0 8.5 %collective-permute-start = (f32[40,128]{1,0:T(8,128)S(1)}, f32[40,128]{1,0:T(8,128)S(1)}, u32[]{:S(2)}, u32[]{:S(2)}) collective-permute-start(f32[40,128]{1,0:T(8,128)S(1)} %get-tuple-element.10), channel_id=1, source_target_pairs={{1,2},{2,1},{3,4},{4,3},{5,6},{6,5},{9,10},{10,9},{11,12},{12,11},... | collective-permute-start | bytes 61448 | tf_op jit(solution)/shard_map/ppermute | solution.py:241
  6.4 6.8 %collective-permute-start.1 = (f32[40,128]{1,0:T(8,128)S(1)}, f32[40,128]{1,0:T(8,128)S(1)}, u32[]{:S(2)}, u32[]{:S(2)}) collective-permute-start(f32[40,128]{1,0:T(8,128)S(1)} %get-tuple-element.11), channel_id=1, source_target_pairs={{0,1},{1,0},{2,3},{3,2},{4,5},{5,4},{6,7},{7,6},{8,9},{9,8},{10,11... | collective-permute-start | bytes 61448 | tf_op jit(solution)/shard_map/ppermute | solution.py:241
  14.0 10.1 %collective-permute-start.3 = (f32[320,128]{1,0:T(8,128)S(1)}, f32[320,128]{1,0:T(8,128)S(1)}, u32[]{:S(2)}, u32[]{:S(2)}) collective-permute-start(f32[320,128]{1,0:T(8,128)S(1)} %get-tuple-element.13.field.rest_0_), channel_id=1, source_target_pairs={{0,64},{64,0},{128,192},{192,128},{256,320},{320,256},{384,448},{4... | collective-permute-start | bytes 491528 | tf_op jit(solution)/shard_map/ppermute | solution.py:250
  16.7 7.5 %collective-permute-start.2 = (f32[320,128]{1,0:T(8,128)S(1)}, f32[320,128]{1,0:T(8,128)S(1)}, u32[]{:S(2)}, u32[]{:S(2)}) collective-permute-start(f32[320,128]{1,0:T(8,128)S(1)} %get-tuple-element.13.field.rest_0_), channel_id=1, source_target_pairs={{8,16},{16,8},{24,32},{32,24},{40,48},{48,40},{9,17},{17,9},{25,33... | collective-permute-start | bytes 491528 | tf_op jit(solution)/shard_map/ppermute | solution.py:241
  17.4 8.3 %collective-permute-start.5 = (f32[320,128]{1,0:T(8,128)S(1)}, f32[320,128]{1,0:T(8,128)S(1)}, u32[]{:S(2)}, u32[]{:S(2)}) collective-permute-start(f32[320,128]{1,0:T(8,128)S(1)} %get-tuple-element.13.field.rest_0_), channel_id=1, source_target_pairs={{64,128},{128,64},{192,256},{256,192},{320,384},{384,320},{8,72},{... | collective-permute-start | bytes 491528 | tf_op jit(solution)/shard_map/ppermute | solution.py:250
  18.1 7.6 %collective-permute-start.4 = (f32[320,128]{1,0:T(8,128)S(1)}, f32[320,128]{1,0:T(8,128)S(1)}, u32[]{:S(2)}, u32[]{:S(2)}) collective-permute-start(f32[320,128]{1,0:T(8,128)S(1)} %get-tuple-element.13.field.rest_0_), channel_id=1, source_target_pairs={{0,8},{8,0},{16,24},{24,16},{32,40},{40,32},{48,56},{56,48},{1,9},... | collective-permute-start | bytes 491528 | tf_op jit(solution)/shard_map/ppermute | solution.py:241
  26.5 11.6 %collective-permute-start.7 = (f32[320,128]{1,0:T(8,128)S(1)}, f32[320,128]{1,0:T(8,128)S(1)}, u32[]{:S(2)}, u32[]{:S(2)}) collective-permute-start(f32[320,128]{1,0:T(8,128)S(1)} %shard_map.44.field.rest_0_), channel_id=1, source_target_pairs={{0,64},{64,0},{128,192},{192,128},{256,320},{320,256},{384,448},{4... | collective-permute-start | bytes 491528 | tf_op jit(solution)/shard_map/ppermute | solution.py:250
  30.2 8.0 %collective-permute-start.6 = (f32[320,128]{1,0:T(8,128)S(1)}, f32[320,128]{1,0:T(8,128)S(1)}, u32[]{:S(2)}, u32[]{:S(2)}) collective-permute-start(f32[320,128]{1,0:T(8,128)S(1)} %shard_map.44.field.rest_0_), channel_id=1, source_target_pairs={{8,16},{16,8},{24,32},{32,24},{40,48},{48,40},{9,17},{17,9},{25,33... | collective-permute-start | bytes 491528 | tf_op jit(solution)/shard_map/ppermute | solution.py:241
  30.8 8.8 %collective-permute-start.9 = (f32[320,128]{1,0:T(8,128)S(1)}, f32[320,128]{1,0:T(8,128)S(1)}, u32[]{:S(2)}, u32[]{:S(2)}) collective-permute-start(f32[320,128]{1,0:T(8,128)S(1)} %shard_map.44.field.rest_0_), channel_id=1, source_target_pairs={{64,128},{128,64},{192,256},{256,192},{320,384},{384,320},{8,72},{... | collective-permute-start | bytes 491528 | tf_op jit(solution)/shard_map/ppermute | solution.py:250
  31.5 8.2 %collective-permute-start.8 = (f32[320,128]{1,0:T(8,128)S(1)}, f32[320,128]{1,0:T(8,128)S(1)}, u32[]{:S(2)}, u32[]{:S(2)}) collective-permute-start(f32[320,128]{1,0:T(8,128)S(1)} %shard_map.44.field.rest_0_), channel_id=1, source_target_pairs={{0,8},{8,0},{16,24},{24,16},{32,40},{40,32},{48,56},{56,48},{1,9},... | collective-permute-start | bytes 491528 | tf_op jit(solution)/shard_map/ppermute | solution.py:241
  40.5 12.7 %collective-permute-start.11 = (f32[320,128]{1,0:T(8,128)S(1)}, f32[320,128]{1,0:T(8,128)S(1)}, u32[]{:S(2)}, u32[]{:S(2)}) collective-permute-start(f32[320,128]{1,0:T(8,128)S(1)} %shard_map.46.field), channel_id=1, source_target_pairs={{0,64},{64,0},{128,192},{192,128},{256,320},{320,256},{384,448},{4... | collective-permute-start | bytes 491528 | tf_op jit(solution)/shard_map/ppermute | solution.py:250
  44.1 9.2 %collective-permute-start.10 = (f32[320,128]{1,0:T(8,128)S(1)}, f32[320,128]{1,0:T(8,128)S(1)}, u32[]{:S(2)}, u32[]{:S(2)}) collective-permute-start(f32[320,128]{1,0:T(8,128)S(1)} %shard_map.46.field), channel_id=1, source_target_pairs={{8,16},{16,8},{24,32},{32,24},{40,48},{48,40},{9,17},{17,9},{25,33... | collective-permute-start | bytes 491528 | tf_op jit(solution)/shard_map/ppermute | solution.py:241
  44.7 10.0 %collective-permute-start.13 = (f32[320,128]{1,0:T(8,128)S(1)}, f32[320,128]{1,0:T(8,128)S(1)}, u32[]{:S(2)}, u32[]{:S(2)}) collective-permute-start(f32[320,128]{1,0:T(8,128)S(1)} %shard_map.46.field), channel_id=1, source_target_pairs={{64,128},{128,64},{192,256},{256,192},{320,384},{384,320},{8,72},{... | collective-permute-start | bytes 491528 | tf_op jit(solution)/shard_map/ppermute | solution.py:250
  45.4 9.4 %collective-permute-start.12 = (f32[320,128]{1,0:T(8,128)S(1)}, f32[320,128]{1,0:T(8,128)S(1)}, u32[]{:S(2)}, u32[]{:S(2)}) collective-permute-start(f32[320,128]{1,0:T(8,128)S(1)} %shard_map.46.field), channel_id=1, source_target_pairs={{0,8},{8,0},{16,24},{24,16},{32,40},{40,32},{48,56},{56,48},{1,9},... | collective-permute-start | bytes 491528 | tf_op jit(solution)/shard_map/ppermute | solution.py:241
  55.6 6.9 %collective-permute-start.15 = (f32[256,128]{1,0:T(8,128)S(1)}, f32[256,128]{1,0:T(8,128)S(1)}, u32[]{:S(2)}, u32[]{:S(2)}) collective-permute-start(f32[256,128]{1,0:T(8,128)S(1)} %get-tuple-element.14.field), channel_id=1, source_target_pairs={{64,0},{128,64},{192,128},{256,192},{320,256},{384,320},{448,384},... | collective-permute-start | bytes 393224 | tf_op jit(solution)/shard_map/ppermute | solution.py:260
  56.9 5.6 %collective-permute-start.14 = (f32[256,128]{1,0:T(8,128)S(1)}, f32[256,128]{1,0:T(8,128)S(1)}, u32[]{:S(2)}, u32[]{:S(2)}) collective-permute-start(f32[256,128]{1,0:T(8,128)S(1)} %get-tuple-element.14.field), channel_id=1, source_target_pairs={{8,0},{16,8},{24,16},{32,24},{40,32},{48,40},{56,48},{9,1},{17,9},... | collective-permute-start | bytes 393224 | tf_op jit(solution)/shard_map/ppermute | solution.py:264
  63.6 5.4 %collective-permute-start.16 = (f32[16,128]{1,0:T(8,128)S(1)}, f32[16,128]{1,0:T(8,128)S(1)}, u32[]{:S(2)}, u32[]{:S(2)}) collective-permute-start(f32[16,128]{1,0:T(8,128)S(1)} %shard_map.49), channel_id=1, source_target_pairs={{0,8},{8,0},{16,24},{24,16},{32,40},{40,32},{48,56},{56,48},{1,9},... | collective-permute-start | bytes 24584 | tf_op jit(solution)/shard_map/ppermute | solution.py:270

commit v3 on v2

--- a/solution.py
+++ b/solution.py
@@ -188,36 +188,57 @@
     )
 
 
-def sums_kernel(flags, potential, field, edge, after_y, beside_x, sums):
+def image_kernel(flags, potential, field, edge, out):
     lane = lane_index(ORB)
     up = flags[1] == 0
-    along_x = {}
-    for y in range(SIDE):
-        rows = [rows_of(ref, x * SIDE + y) for ref in (field, beside_x) for x in range(SIDE)]
-        line = [jnp.where(up, rows[start + i], rows[start + SIDE - 1 - i]) for start in (0, SIDE) for i in range(SIDE)]
-        terms = [sum(-0.5 * WEIGHTS[k] * line[i + k] for k in range(1, 5)) for i in range(SIDE)]
-        for x in range(SIDE):
-            along_x[x, y] = jnp.where(up, terms[x], terms[SIDE - 1 - x])
+    weight = [-0.5 * w for w in WEIGHTS]
+    for x in range(SIDE):
+        for y in range(SIDE):
+            cell = x * SIDE + y
+            here, there = rows_of(field, cell), rolled(edge_of(edge, x), -2 * EXT * y)
+            total = (0.5 * potential[cell : cell + 1, :] + 1.5 * weight[0]) * here
+            above = sum([weight[k] * rows_of(field, cell + k * SIDE) for k in range(1, SIDE - x)], jnp.zeros_like(here))
+            below = sum([weight[k] * rows_of(field, cell - k * SIDE) for k in range(1, x + 1)], jnp.zeros_like(here))
+            total = total + jnp.where(up, above, below)
+            for k in range(1, 5):
+                pair = rolled(jnp.where(lane < k, there, here), -k)
+                if y + k < SIDE:
+                    pair = pair + rows_of(field, cell + k)
+                total = total + weight[k] * pair
+            out[cell * ORB : (cell + 1) * ORB, :] = total
+
+
+def group_of(rows):
+    return lax.broadcasted_iota(jnp.int32, (rows, LANES), 0) // 4
+
+
+def sums_kernel(flags, part, field, after_y, beside_x, sums, wide):
+    up = flags[1] == 0
+    weight = [-0.5 * w for w in WEIGHTS]
     here_all, image_all = [], []
     for x in range(SIDE):
         for y in range(SIDE):
             cell = x * SIDE + y
-            here, there = rows_of(field, cell), rolled(edge_of(edge, x), -2 * EXT * y)
-            image = (0.5 * potential[cell : cell + 1, :] - 0.75 * WEIGHTS[0]) * here + along_x[x, y]
-            for k in range(1, 5):
-                above = rows_of(field, cell + k) if y + k < SIDE else rows_of(after_y, cell + k - SIDE)
-                above = above + rolled(jnp.where(lane < k, there, here), -k)
-                image = image + (-0.5 * WEIGHTS[k]) * above
-            here_all.append(here)
+            above = sum(weight[k] * rows_of(beside_x, cell + (k - SIDE) * SIDE) for k in range(SIDE - x, 5))
+            below = sum(weight[k] * rows_of(beside_x, cell + (SIDE - k) * SIDE) for k in range(x + 1, 5))
+            image = rows_of(part, cell) + jnp.where(up, above, below)
+            image = image + sum(weight[k] * rows_of(after_y, cell + k - SIDE) for k in range(SIDE - y, 5))
+            here_all.append(rows_of(field, cell))
             image_all.append(image)
     here = jnp.concatenate(here_all, axis=1)
     image = jnp.concatenate(image_all, axis=1)
-    sums[...] = jnp.zeros_like(sums)
-    sums[:, : 2 * ORB] = dot(here, jnp.concatenate([here, image], axis=0), (1, 1))
-
-
-def finish_kernel(cell_total, sums, field, q_block, ritz):
-    sums = sums[...] * (1.0 / cell_total)
+    wide[...] = jnp.zeros_like(wide)
+    wide[:, : 2 * ORB] = dot(here, jnp.concatenate([here, image], axis=0), (1, 1))
+    value, group = wide[...], group_of(ORB)
+    wide[...] = sum(jnp.where(group == g, rolled(value, 2 * ORB * g), 0.0) for g in range(4))
+    sums[...] = (wide[0:4, :] + wide[4:8, :]) + (wide[8:12, :] + wide[12:16, :])
+
+
+def finish_kernel(cell_total, sums, field, q_block, ritz, wide):
+    for g in range(4):
+        wide[4 * g : 4 * g + 4, :] = sums[...]
+    value, group = wide[...], group_of(ORB)
+    sums = sum(jnp.where(group == g, rolled(value, -2 * ORB * g), 0.0) for g in range(4)) * (1.0 / cell_total)
     row = lax.broadcasted_iota(jnp.int32, (ORB, LANES), 0)
     lane = lane_index(ORB)
     work = jnp.where(lane < ORB, sums, jnp.where(lane == row + ORB, 1.0, 0.0))
@@ -276,7 +297,7 @@
     return lax.psum(value, ("gx", "gy", "gz"))
 
 
-def call(kernel, outs, smem=True):
+def call(kernel, outs, smem=True, scratch=()):
     def run(*operands):
         specs = [pl.BlockSpec(memory_space=pltpu.VMEM)] * len(operands)
         if smem:
@@ -286,6 +307,7 @@
             out_shape=[jax.ShapeDtypeStruct(shape, jnp.float32) for shape in outs],
             in_specs=specs,
             out_specs=[pl.BlockSpec(memory_space=pltpu.VMEM)] * len(outs),
+            scratch_shapes=[pltpu.VMEM(shape, jnp.float32) for shape in scratch],
             compiler_params=pltpu.CompilerParams(vmem_limit_bytes=8 * 1024 * 1024),
         )(*operands)
 
@@ -319,9 +341,11 @@
     (field2,) = advance(field1, 2.0 / HALF, (field,), False)
     field, edge = advance(field2, 2.0 / HALF, (field1,), True)
     after_y, beside_x = from_above(field, "gy"), one_side_x(field)
-    sums = call(sums_kernel, ((ORB, LANES),))(flags, potential, field, edge, after_y, beside_x)[0]
+    (part,) = call(image_kernel, (block,))(flags, potential, field, edge)
+    wide = (ORB, LANES)
+    (sums,) = call(sums_kernel, ((4, LANES),), scratch=(wide,))(flags, part, field, after_y, beside_x)
     sums = sum_everywhere(sums)
-    q_block, ritz = call(functools.partial(finish_kernel, cell_total), (block, (ORB, ORB)), smem=False)(sums, field)
+    q_block, ritz = call(functools.partial(finish_kernel, cell_total), (block, (ORB, ORB)), False, (wide,))(sums, field)
     return q_block.reshape(shape), ritz
 
 

time: 128 us -> 127 us (level)
    pallas_call x10 -> x11, Pallas kernels: 12.1 us -> 12.9 us  [run(): pl.pallas_call(kernel, out_shape=[jax.ShapeDtypeStruct(shape, jnp.float32...]
where the time goes in v3:
time: 127 us
  blocking collectives  55.2 us (43%)
  starting transfers between devices  50.1 us (39%)
  Pallas kernels  12.9 us (10%)
  waiting for transfers between devices  5.89 us (5%)
  local copies, waits for them, and re-layouts  1.59 us (1%)
    ppermute x8, starting transfers between devices, swap(): return lax.ppermute(value, axis, pairs)  31 us
    psum x1, blocking collectives, sum_everywhere(): return lax.psum(value, ('gx', 'gz'), axis_index_groups=rings)  15.6 us
    psum x1, blocking collectives, sum_everywhere(): value = lax.psum(value, 'gz', axis_index_groups=fours)  15.3 us
    pallas_call x11, Pallas kernels, run(): pl.pallas_call(kernel, out_shape=[jax.ShapeDtypeStruct(shape, jnp.float32...  12.9 us
    psum x1, blocking collectives, sum_everywhere(): value = lax.psum(value, 'gx', axis_index_groups=fours)  12.2 us
    psum x1, blocking collectives, sum_everywhere(): lax.psum(value, 'gy', axis_index_groups=[[0, 2, 4, 6], [1, 3, 5, 7]])  12.1 us
    ppermute x6, starting transfers between devices, swap_x(): return lax.ppermute(value, ('gx', 'gy'), pairs)  11.9 us
    ppermute x1, starting transfers between devices, sum_everywhere(): value = value + lax.ppermute(value, 'gy', [(i, i ^ 1) for i in range(8)])  4.61 us
  transfers between devices with their start and end apart: 17, of which 3 were waited for; matrix products, arithmetic and copies ran while one was open for 0% of the time, Pallas kernels for 4%

profile of v3, /device:TPU:2, one launch (start us, length us, event | category | flops | bytes accessed | tf_op | source)
XLA Modules:
  0.0 126.6 jit_solution(1985267627026848097)
XLA Ops:
  1.4 0.9 copy-done
  2.3 0.7 shard_map.41
  3.0 3.4 %collective-permute-start = (f32[40,128]{1,0:T(8,128)S(1)}, f32[40,128]{1,0:T(8,128)S(1)}, u32[]{:S(2)}, u32[]{:S(2)}) collective-permute-start(f32[40,128]{1,0:T(8,128)S(1)} %get-tuple-element.10), channel_id=1, source_target_pairs={{1,2},{2,1},{3,4},{4,3},{5,6},{6,5},{9,10},{10,9},{11,12},{12,11},... | collective-permute-start | bytes 61448 | tf_op jit(solution)/shard_map/ppermute | solution.py:262
  6.4 5.1 %collective-permute-start.1 = (f32[40,128]{1,0:T(8,128)S(1)}, f32[40,128]{1,0:T(8,128)S(1)}, u32[]{:S(2)}, u32[]{:S(2)}) collective-permute-start(f32[40,128]{1,0:T(8,128)S(1)} %get-tuple-element.11), channel_id=1, source_target_pairs={{0,1},{1,0},{2,3},{3,2},{4,5},{5,4},{6,7},{7,6},{8,9},{9,8},{10,11... | collective-permute-start | bytes 61448 | tf_op jit(solution)/shard_map/ppermute | solution.py:262
  11.5 1.7 %collective-permute-done.1.first = f32[40,128]{1,0:T(8,128)S(1)} collective-permute-done((f32[40,128]{1,0:T(8,128)S(1)}, f32[40,128]{1,0:T(8,128)S(1)}, u32[]{:S(2)}, u32[]{:S(2)}) %collective-permute-start.1) | collective-permute-done | bytes 20512 | tf_op jit(solution)/shard_map/ppermute | solution.py:262
  13.2 0.8 shard_map.42
  14.0 2.7 %collective-permute-start.3 = (f32[320,128]{1,0:T(8,128)S(1)}, f32[320,128]{1,0:T(8,128)S(1)}, u32[]{:S(2)}, u32[]{:S(2)}) collective-permute-start(f32[320,128]{1,0:T(8,128)S(1)} %get-tuple-element.13.field.rest_0_), channel_id=1, source_target_pairs={{0,64},{64,0},{128,192},{192,128},{256,320},{320,256},{384,448},{4... | collective-permute-start | bytes 491528 | tf_op jit(solution)/shard_map/ppermute | solution.py:271
  16.7 0.7 collective-permute-start.2
  17.4 0.7 collective-permute-start.5
  18.1 6.1 %collective-permute-start.4 = (f32[320,128]{1,0:T(8,128)S(1)}, f32[320,128]{1,0:T(8,128)S(1)}, u32[]{:S(2)}, u32[]{:S(2)}) collective-permute-start(f32[320,128]{1,0:T(8,128)S(1)} %get-tuple-element.13.field.rest_0_), channel_id=1, source_target_pairs={{0,8},{8,0},{16,24},{24,16},{32,40},{40,32},{48,56},{56,48},{1,9},... | collective-permute-start | bytes 491528 | tf_op jit(solution)/shard_map/ppermute | solution.py:262
  24.2 1.5 %shard_map.43.part = f32[256,128]{1,0:T(8,128)S(1)} custom-call(s32[5]{0:T(128)S(1)} %stack.31.flags, f32[16,128]{1,0:T(8,128)S(1)} %bitcast.11, f32[320,128]{1,0:T(8,128)S(1)} %get-tuple-element.13.field.rest_0_, f32[320,128]{1,0:T(8,128)S(1)} %collective-permute-done.2.rest_0_.y2, f32[320,128]{1,0:T(8,128)S(1)} %collective-permute-done.3.rest_1_.x1), custom_call_target="tpu_custom_call" | custom-call | tf_op jit(solution)/shard_map/pallas_call | solution.py:305
  25.7 0.8 shard_map.44.field.rest_0_
  26.5 3.6 %collective-permute-start.7 = (f32[320,128]{1,0:T(8,128)S(1)}, f32[320,128]{1,0:T(8,128)S(1)}, u32[]{:S(2)}, u32[]{:S(2)}) collective-permute-start(f32[320,128]{1,0:T(8,128)S(1)} %shard_map.44.field.rest_0_), channel_id=1, source_target_pairs={{0,64},{64,0},{128,192},{192,128},{256,320},{320,256},{384,448},{4... | collective-permute-start | bytes 491528 | tf_op jit(solution)/shard_map/ppermute | solution.py:271
  31.5 6.6 %collective-permute-start.8 = (f32[320,128]{1,0:T(8,128)S(1)}, f32[320,128]{1,0:T(8,128)S(1)}, u32[]{:S(2)}, u32[]{:S(2)}) collective-permute-start(f32[320,128]{1,0:T(8,128)S(1)} %shard_map.44.field.rest_0_), channel_id=1, source_target_pairs={{0,8},{8,0},{16,24},{24,16},{32,40},{40,32},{48,56},{56,48},{1,9},... | collective-permute-start | bytes 491528 | tf_op jit(solution)/shard_map/ppermute | solution.py:262
  38.2 1.5 %shard_map.45.part = f32[256,128]{1,0:T(8,128)S(1)} custom-call(s32[5]{0:T(128)S(1)} %stack.31.flags, f32[16,128]{1,0:T(8,128)S(1)} %bitcast.12, f32[320,128]{1,0:T(8,128)S(1)} %shard_map.44.field.rest_0_, f32[320,128]{1,0:T(8,128)S(1)} %get-tuple-element.13.field.rest_0_, f32[320,128]{1,0:T(8,128)S(1)} %collective-permute-done.6.rest_1_.y2, ...), custom_call_target="tpu_custom_call" | custom-call | tf_op jit(solution)/shard_map/pallas_call | solution.py:305
  39.7 0.8 shard_map.46.field
  40.5 3.5 %collective-permute-start.11 = (f32[320,128]{1,0:T(8,128)S(1)}, f32[320,128]{1,0:T(8,128)S(1)}, u32[]{:S(2)}, u32[]{:S(2)}) collective-permute-start(f32[320,128]{1,0:T(8,128)S(1)} %shard_map.46.field), channel_id=1, source_target_pairs={{0,64},{64,0},{128,192},{192,128},{256,320},{320,256},{384,448},{4... | collective-permute-start | bytes 491528 | tf_op jit(solution)/shard_map/ppermute | solution.py:271
  45.4 7.8 %collective-permute-start.12 = (f32[320,128]{1,0:T(8,128)S(1)}, f32[320,128]{1,0:T(8,128)S(1)}, u32[]{:S(2)}, u32[]{:S(2)}) collective-permute-start(f32[320,128]{1,0:T(8,128)S(1)} %shard_map.46.field), channel_id=1, source_target_pairs={{0,8},{8,0},{16,24},{24,16},{32,40},{40,32},{48,56},{56,48},{1,9},... | collective-permute-start | bytes 491528 | tf_op jit(solution)/shard_map/ppermute | solution.py:262
  53.3 1.5 %shard_map.47.part = f32[256,128]{1,0:T(8,128)S(1)} custom-call(s32[5]{0:T(128)S(1)} %stack.31.flags, f32[16,128]{1,0:T(8,128)S(1)} %bitcast.13, f32[320,128]{1,0:T(8,128)S(1)} %shard_map.46.field, f32[320,128]{1,0:T(8,128)S(1)} %shard_map.44.field.rest_0_, f32[320,128]{1,0:T(8,128)S(1)} %collective-permute-done.10.rest_1_.y2, ...), custom_call_target="tpu_custom_call" | custom-call | tf_op jit(solution)/shard_map/pallas_call | solution.py:305
  54.8 0.8 shard_map.48
  55.6 1.3 %collective-permute-start.15 = (f32[256,128]{1,0:T(8,128)S(1)}, f32[256,128]{1,0:T(8,128)S(1)}, u32[]{:S(2)}, u32[]{:S(2)}) collective-permute-start(f32[256,128]{1,0:T(8,128)S(1)} %get-tuple-element.14.field), channel_id=1, source_target_pairs={{64,0},{128,64},{192,128},{256,192},{320,256},{384,320},{448,384},... | collective-permute-start | bytes 393224 | tf_op jit(solution)/shard_map/ppermute | solution.py:281
  56.9 1.3 %collective-permute-start.14 = (f32[256,128]{1,0:T(8,128)S(1)}, f32[256,128]{1,0:T(8,128)S(1)}, u32[]{:S(2)}, u32[]{:S(2)}) collective-permute-start(f32[256,128]{1,0:T(8,128)S(1)} %get-tuple-element.14.field), channel_id=1, source_target_pairs={{8,0},{16,8},{24,16},{32,24},{40,32},{48,40},{56,48},{9,1},{17,9},... | collective-permute-start | bytes 393224 | tf_op jit(solution)/shard_map/ppermute | solution.py:285
  58.2 0.9 shard_map.49.part
  59.2 3.3 %collective-permute-done.15.beside_x = f32[256,128]{1,0:T(8,128)S(1)} collective-permute-done((f32[256,128]{1,0:T(8,128)S(1)}, f32[256,128]{1,0:T(8,128)S(1)}, u32[]{:S(2)}, u32[]{:S(2)}) %collective-permute-start.15) | collective-permute-done | bytes 131104 | tf_op jit(solution)/shard_map/ppermute | solution.py:281
  62.5 1.0 shard_map.50
  63.4 4.6 %collective-permute-start.16 = (f32[4,128]{1,0:T(4,128)S(1)}, f32[4,128]{1,0:T(4,128)S(1)}, u32[]{:S(2)}, u32[]{:S(2)}) collective-permute-start(f32[4,128]{1,0:T(4,128)S(1)} %shard_map.50), channel_id=1, source_target_pairs={{0,8},{8,0},{16,24},{24,16},{32,40},{40,32},{48,56},{56,48},{1,9},... | collective-permute-start | bytes 6152 | tf_op jit(solution)/shard_map/ppermute | solution.py:291
  68.1 0.8 collective-permute-done.16
  68.9 12.1 %psum.28 = f32[4,128]{1,0:T(4,128)S(1)} all-reduce(f32[4,128]{1,0:T(4,128)S(1)} %add.28), channel_id=1, replica_groups={{0,16,32,48},{8,24,40,56},{1,17,33,49},{9,25,41,57},{2,18,34,50},{10,26..., use_global_device_ids=true, to_apply=%region_0.1 | all-reduce | flops 512 | bytes 4096 | tf_op jit(solution)/shard_map/psum | solution.py:292
  80.9 15.3 %psum.29 = f32[4,128]{1,0:T(4,128)S(1)} all-reduce(f32[4,128]{1,0:T(4,128)S(1)} %psum.28), channel_id=1, replica_groups={{0,1,2,3},{4,5,6,7},{8,9,10,11},{12,13,14,15},{16,17,18,19},{20,21,22,2..., use_global_device_ids=true, to_apply=%region_1.2 | all-reduce | flops 512 | bytes 4096 | tf_op jit(solution)/shard_map/psum | solution.py:293
  96.2 12.2 %psum.30 = f32[4,128]{1,0:T(4,128)S(1)} all-reduce(f32[4,128]{1,0:T(4,128)S(1)} %psum.29), channel_id=1, replica_groups={{0,64,128,192},{256,320,384,448},{1,65,129,193},{257,321,385,449},{2,66..., use_global_device_ids=true, to_apply=%region_2.3 | all-reduce | flops 512 | bytes 4096 | tf_op jit(solution)/shard_map/psum | solution.py:294
  108.4 15.6 %psum.31.sums = f32[4,128]{1,0:T(4,128)S(1)} all-reduce(f32[4,128]{1,0:T(4,128)S(1)} %psum.30), channel_id=1, replica_groups={{0,256,4,260},{1,257,5,261},{2,258,6,262},{3,259,7,263},{64,320,68,324}..., use_global_device_ids=true, to_apply=%region_3.4 | all-reduce | flops 512 | bytes 4096 | tf_op jit(solution)/shard_map/psum | solution.py:296
  124.0 2.6 %shard_map.51 = (f32[256,128]{1,0:T(8,128)}, f32[16,16]{1,0:T(8,128)}) custom-call(f32[4,128]{1,0:T(4,128)S(1)} %psum.31.sums, f32[256,128]{1,0:T(8,128)S(1)} %get-tuple-element.14.field), custom_call_target="tpu_custom_call" | custom-call | tf_op jit(solution)/shard_map/pallas_call | solution.py:305
  (23 shorter events, 3.4 us)
Async XLA Ops:
  0.7 0.7 copy-start.1
  1.4 0.9 copy-start
  3.0 8.5 %collective-permute-start = (f32[40,128]{1,0:T(8,128)S(1)}, f32[40,128]{1,0:T(8,128)S(1)}, u32[]{:S(2)}, u32[]{:S(2)}) collective-permute-start(f32[40,128]{1,0:T(8,128)S(1)} %get-tuple-element.10), channel_id=1, source_target_pairs={{1,2},{2,1},{3,4},{4,3},{5,6},{6,5},{9,10},{10,9},{11,12},{12,11},... | collective-permute-start | bytes 61448 | tf_op jit(solution)/shard_map/ppermute | solution.py:262
  6.4 6.8 %collective-permute-start.1 = (f32[40,128]{1,0:T(8,128)S(1)}, f32[40,128]{1,0:T(8,128)S(1)}, u32[]{:S(2)}, u32[]{:S(2)}) collective-permute-start(f32[40,128]{1,0:T(8,128)S(1)} %get-tuple-element.11), channel_id=1, source_target_pairs={{0,1},{1,0},{2,3},{3,2},{4,5},{5,4},{6,7},{7,6},{8,9},{9,8},{10,11... | collective-permute-start | bytes 61448 | tf_op jit(solution)/shard_map/ppermute | solution.py:262
  14.0 10.1 %collective-permute-start.3 = (f32[320,128]{1,0:T(8,128)S(1)}, f32[320,128]{1,0:T(8,128)S(1)}, u32[]{:S(2)}, u32[]{:S(2)}) collective-permute-start(f32[320,128]{1,0:T(8,128)S(1)} %get-tuple-element.13.field.rest_0_), channel_id=1, source_target_pairs={{0,64},{64,0},{128,192},{192,128},{256,320},{320,256},{384,448},{4... | collective-permute-start | bytes 491528 | tf_op jit(solution)/shard_map/ppermute | solution.py:271
  16.7 7.5 %collective-permute-start.2 = (f32[320,128]{1,0:T(8,128)S(1)}, f32[320,128]{1,0:T(8,128)S(1)}, u32[]{:S(2)}, u32[]{:S(2)}) collective-permute-start(f32[320,128]{1,0:T(8,128)S(1)} %get-tuple-element.13.field.rest_0_), channel_id=1, source_target_pairs={{8,16},{16,8},{24,32},{32,24},{40,48},{48,40},{9,17},{17,9},{25,33... | collective-permute-start | bytes 491528 | tf_op jit(solution)/shard_map/ppermute | solution.py:262
  17.4 8.3 %collective-permute-start.5 = (f32[320,128]{1,0:T(8,128)S(1)}, f32[320,128]{1,0:T(8,128)S(1)}, u32[]{:S(2)}, u32[]{:S(2)}) collective-permute-start(f32[320,128]{1,0:T(8,128)S(1)} %get-tuple-element.13.field.rest_0_), channel_id=1, source_target_pairs={{64,128},{128,64},{192,256},{256,192},{320,384},{384,320},{8,72},{... | collective-permute-start | bytes 491528 | tf_op jit(solution)/shard_map/ppermute | solution.py:271
  18.1 7.6 %collective-permute-start.4 = (f32[320,128]{1,0:T(8,128)S(1)}, f32[320,128]{1,0:T(8,128)S(1)}, u32[]{:S(2)}, u32[]{:S(2)}) collective-permute-start(f32[320,128]{1,0:T(8,128)S(1)} %get-tuple-element.13.field.rest_0_), channel_id=1, source_target_pairs={{0,8},{8,0},{16,24},{24,16},{32,40},{40,32},{48,56},{56,48},{1,9},... | collective-permute-start | bytes 491528 | tf_op jit(solution)/shard_map/ppermute | solution.py:262
  26.5 11.6 %collective-permute-start.7 = (f32[320,128]{1,0:T(8,128)S(1)}, f32[320,128]{1,0:T(8,128)S(1)}, u32[]{:S(2)}, u32[]{:S(2)}) collective-permute-start(f32[320,128]{1,0:T(8,128)S(1)} %shard_map.44.field.rest_0_), channel_id=1, source_target_pairs={{0,64},{64,0},{128,192},{192,128},{256,320},{320,256},{384,448},{4... | collective-permute-start | bytes 491528 | tf_op jit(solution)/shard_map/ppermute | solution.py:271
  30.2 8.0 %collective-permute-start.6 = (f32[320,128]{1,0:T(8,128)S(1)}, f32[320,128]{1,0:T(8,128)S(1)}, u32[]{:S(2)}, u32[]{:S(2)}) collective-permute-start(f32[320,128]{1,0:T(8,128)S(1)} %shard_map.44.field.rest_0_), channel_id=1, source_target_pairs={{8,16},{16,8},{24,32},{32,24},{40,48},{48,40},{9,17},{17,9},{25,33... | collective-permute-start | bytes 491528 | tf_op jit(solution)/shard_map/ppermute | solution.py:262
  30.8 8.8 %collective-permute-start.9 = (f32[320,128]{1,0:T(8,128)S(1)}, f32[320,128]{1,0:T(8,128)S(1)}, u32[]{:S(2)}, u32[]{:S(2)}) collective-permute-start(f32[320,128]{1,0:T(8,128)S(1)} %shard_map.44.field.rest_0_), channel_id=1, source_target_pairs={{64,128},{128,64},{192,256},{256,192},{320,384},{384,320},{8,72},{... | collective-permute-start | bytes 491528 | tf_op jit(solution)/shard_map/ppermute | solution.py:271
  31.5 8.2 %collective-permute-start.8 = (f32[320,128]{1,0:T(8,128)S(1)}, f32[320,128]{1,0:T(8,128)S(1)}, u32[]{:S(2)}, u32[]{:S(2)}) collective-permute-start(f32[320,128]{1,0:T(8,128)S(1)} %shard_map.44.field.rest_0_), channel_id=1, source_target_pairs={{0,8},{8,0},{16,24},{24,16},{32,40},{40,32},{48,56},{56,48},{1,9},... | collective-permute-start | bytes 491528 | tf_op jit(solution)/shard_map/ppermute | solution.py:262
  40.5 12.7 %collective-permute-start.11 = (f32[320,128]{1,0:T(8,128)S(1)}, f32[320,128]{1,0:T(8,128)S(1)}, u32[]{:S(2)}, u32[]{:S(2)}) collective-permute-start(f32[320,128]{1,0:T(8,128)S(1)} %shard_map.46.field), channel_id=1, source_target_pairs={{0,64},{64,0},{128,192},{192,128},{256,320},{320,256},{384,448},{4... | collective-permute-start | bytes 491528 | tf_op jit(solution)/shard_map/ppermute | solution.py:271
  44.1 9.2 %collective-permute-start.10 = (f32[320,128]{1,0:T(8,128)S(1)}, f32[320,128]{1,0:T(8,128)S(1)}, u32[]{:S(2)}, u32[]{:S(2)}) collective-permute-start(f32[320,128]{1,0:T(8,128)S(1)} %shard_map.46.field), channel_id=1, source_target_pairs={{8,16},{16,8},{24,32},{32,24},{40,48},{48,40},{9,17},{17,9},{25,33... | collective-permute-start | bytes 491528 | tf_op jit(solution)/shard_map/ppermute | solution.py:262
  44.7 10.0 %collective-permute-start.13 = (f32[320,128]{1,0:T(8,128)S(1)}, f32[320,128]{1,0:T(8,128)S(1)}, u32[]{:S(2)}, u32[]{:S(2)}) collective-permute-start(f32[320,128]{1,0:T(8,128)S(1)} %shard_map.46.field), channel_id=1, source_target_pairs={{64,128},{128,64},{192,256},{256,192},{320,384},{384,320},{8,72},{... | collective-permute-start | bytes 491528 | tf_op jit(solution)/shard_map/ppermute | solution.py:271
  45.4 9.4 %collective-permute-start.12 = (f32[320,128]{1,0:T(8,128)S(1)}, f32[320,128]{1,0:T(8,128)S(1)}, u32[]{:S(2)}, u32[]{:S(2)}) collective-permute-start(f32[320,128]{1,0:T(8,128)S(1)} %shard_map.46.field), channel_id=1, source_target_pairs={{0,8},{8,0},{16,24},{24,16},{32,40},{40,32},{48,56},{56,48},{1,9},... | collective-permute-start | bytes 491528 | tf_op jit(solution)/shard_map/ppermute | solution.py:262
  55.6 6.9 %collective-permute-start.15 = (f32[256,128]{1,0:T(8,128)S(1)}, f32[256,128]{1,0:T(8,128)S(1)}, u32[]{:S(2)}, u32[]{:S(2)}) collective-permute-start(f32[256,128]{1,0:T(8,128)S(1)} %get-tuple-element.14.field), channel_id=1, source_target_pairs={{64,0},{128,64},{192,128},{256,192},{320,256},{384,320},{448,384},... | collective-permute-start | bytes 393224 | tf_op jit(solution)/shard_map/ppermute | solution.py:281
  56.9 5.6 %collective-permute-start.14 = (f32[256,128]{1,0:T(8,128)S(1)}, f32[256,128]{1,0:T(8,128)S(1)}, u32[]{:S(2)}, u32[]{:S(2)}) collective-permute-start(f32[256,128]{1,0:T(8,128)S(1)} %get-tuple-element.14.field), channel_id=1, source_target_pairs={{8,0},{16,8},{24,16},{32,24},{40,32},{48,40},{56,48},{9,1},{17,9},... | collective-permute-start | bytes 393224 | tf_op jit(solution)/shard_map/ppermute | solution.py:285
  63.4 5.4 %collective-permute-start.16 = (f32[4,128]{1,0:T(4,128)S(1)}, f32[4,128]{1,0:T(4,128)S(1)}, u32[]{:S(2)}, u32[]{:S(2)}) collective-permute-start(f32[4,128]{1,0:T(4,128)S(1)} %shard_map.50), channel_id=1, source_target_pairs={{0,8},{8,0},{16,24},{24,16},{32,40},{40,32},{48,56},{56,48},{1,9},... | collective-permute-start | bytes 6152 | tf_op jit(solution)/shard_map/ppermute | solution.py:291

commit v4 on v3

--- a/solution.py
+++ b/solution.py
@@ -285,16 +285,27 @@
     return lax.ppermute(value, axis, [(i + 1, i) for i in range(lax.axis_size(axis) - 1)])
 
 
+def ring_groups(odd_core, stage):
+    at = lambda gx, gy, gz: (gx * 8 + gy) * 8 + gz
+    four, eight, cores = range(4), range(8), range(odd_core, 8, 2)
+    if stage == "y":
+        return [[at(gx, 2 * i + odd_core, gz) for i in four] for gx in eight for gz in eight]
+    if stage == "x":
+        return [[at(gx, gy, 4 * h + i) for i in four] for gx in eight for gy in cores for h in range(2)]
+    if stage == "z":
+        return [[at(4 * h + i, gy, gz) for i in four] for gy in cores for gz in eight for h in range(2)]
+    return [[at(gx + 4 * j, gy, gz + 4 * h) for h in range(2) for j in range(2)] for gx in four for gy in cores for gz in four]
+
+
 def sum_everywhere(value):
-    if all(lax.axis_size(axis) == 8 for axis in ("gx", "gy", "gz")):
-        fours = [[0, 1, 2, 3], [4, 5, 6, 7]]
+    axes = ("gx", "gy", "gz")
+    if all(lax.axis_size(axis) == 8 for axis in axes):
         value = value + lax.ppermute(value, "gy", [(i, i ^ 1) for i in range(8)])
-        value = lax.psum(value, "gy", axis_index_groups=[[0, 2, 4, 6], [1, 3, 5, 7]])
-        value = lax.psum(value, "gz", axis_index_groups=fours)
-        value = lax.psum(value, "gx", axis_index_groups=fours)
-        rings = [[8 * gx + gz, 8 * gx + 32 + gz, 8 * gx + gz + 4, 8 * gx + 32 + gz + 4] for gx in range(4) for gz in range(4)]
-        return lax.psum(value, ("gx", "gz"), axis_index_groups=rings)
-    return lax.psum(value, ("gx", "gy", "gz"))
+        for stages in (("y", "x"), ("x", "y"), ("z", "apart"), ("apart", "z")):
+            groups = [group for core in range(2) for group in ring_groups(core, stages[core])]
+            value = lax.psum(value, axes, axis_index_groups=groups)
+        return value
+    return lax.psum(value, axes)
 
 
 def call(kernel, outs, smem=True, scratch=()):

time: 127 us -> 127 us (level)
  no operation moved by 1% of the time
where the time goes in v4:
time: 127 us
  blocking collectives  55.2 us (43%)
  starting transfers between devices  50.1 us (39%)
  Pallas kernels  12.9 us (10%)
  waiting for transfers between devices  5.89 us (5%)
  local copies, waits for them, and re-layouts  1.59 us (1%)
    psum x4, blocking collectives, sum_everywhere(): value = lax.psum(value, axes, axis_index_groups=groups)  55.2 us
    ppermute x8, starting transfers between devices, swap(): return lax.ppermute(value, axis, pairs)  31 us
    pallas_call x11, Pallas kernels, run(): pl.pallas_call(kernel, out_shape=[jax.ShapeDtypeStruct(shape, jnp.float32...  12.9 us
    ppermute x6, starting transfers between devices, swap_x(): return lax.ppermute(value, ('gx', 'gy'), pairs)  11.9 us
    ppermute x1, starting transfers between devices, sum_everywhere(): value = value + lax.ppermute(value, 'gy', [(i, i ^ 1) for i in range(8)])  4.61 us
    ppermute x1, waiting for transfers between devices, one_side_x(): return lax.ppermute(value, ('gx', 'gy'), pairs)  3.32 us
  transfers between devices with their start and end apart: 17, of which 3 were waited for; matrix products, arithmetic and copies ran while one was open for 0% of the time, Pallas kernels for 4%

profile of v4, /device:TPU:2, one launch (start us, length us, event | category | flops | bytes accessed | tf_op | source)
XLA Modules:
  0.0 126.6 jit_solution(3405550108780763162)
XLA Ops:
  1.4 0.9 copy-done
  2.3 0.7 shard_map.41
  3.0 3.4 %collective-permute-start = (f32[40,128]{1,0:T(8,128)S(1)}, f32[40,128]{1,0:T(8,128)S(1)}, u32[]{:S(2)}, u32[]{:S(2)}) collective-permute-start(f32[40,128]{1,0:T(8,128)S(1)} %get-tuple-element.10), channel_id=1, source_target_pairs={{1,2},{2,1},{3,4},{4,3},{5,6},{6,5},{9,10},{10,9},{11,12},{12,11},... | collective-permute-start | bytes 61448 | tf_op jit(solution)/shard_map/ppermute | solution.py:262
  6.4 5.1 %collective-permute-start.1 = (f32[40,128]{1,0:T(8,128)S(1)}, f32[40,128]{1,0:T(8,128)S(1)}, u32[]{:S(2)}, u32[]{:S(2)}) collective-permute-start(f32[40,128]{1,0:T(8,128)S(1)} %get-tuple-element.11), channel_id=1, source_target_pairs={{0,1},{1,0},{2,3},{3,2},{4,5},{5,4},{6,7},{7,6},{8,9},{9,8},{10,11... | collective-permute-start | bytes 61448 | tf_op jit(solution)/shard_map/ppermute | solution.py:262
  11.5 1.7 %collective-permute-done.1.first = f32[40,128]{1,0:T(8,128)S(1)} collective-permute-done((f32[40,128]{1,0:T(8,128)S(1)}, f32[40,128]{1,0:T(8,128)S(1)}, u32[]{:S(2)}, u32[]{:S(2)}) %collective-permute-start.1) | collective-permute-done | bytes 20512 | tf_op jit(solution)/shard_map/ppermute | solution.py:262
  13.2 0.8 shard_map.42
  14.0 2.7 %collective-permute-start.3 = (f32[320,128]{1,0:T(8,128)S(1)}, f32[320,128]{1,0:T(8,128)S(1)}, u32[]{:S(2)}, u32[]{:S(2)}) collective-permute-start(f32[320,128]{1,0:T(8,128)S(1)} %get-tuple-element.13.field.rest_0_), channel_id=1, source_target_pairs={{0,64},{64,0},{128,192},{192,128},{256,320},{320,256},{384,448},{4... | collective-permute-start | bytes 491528 | tf_op jit(solution)/shard_map/ppermute | solution.py:271
  16.7 0.7 collective-permute-start.2
  17.4 0.7 collective-permute-start.5
  18.1 6.1 %collective-permute-start.4 = (f32[320,128]{1,0:T(8,128)S(1)}, f32[320,128]{1,0:T(8,128)S(1)}, u32[]{:S(2)}, u32[]{:S(2)}) collective-permute-start(f32[320,128]{1,0:T(8,128)S(1)} %get-tuple-element.13.field.rest_0_), channel_id=1, source_target_pairs={{0,8},{8,0},{16,24},{24,16},{32,40},{40,32},{48,56},{56,48},{1,9},... | collective-permute-start | bytes 491528 | tf_op jit(solution)/shard_map/ppermute | solution.py:262
  24.2 1.5 %shard_map.43.part = f32[256,128]{1,0:T(8,128)S(1)} custom-call(s32[5]{0:T(128)S(1)} %stack.31.flags, f32[16,128]{1,0:T(8,128)S(1)} %bitcast.11, f32[320,128]{1,0:T(8,128)S(1)} %get-tuple-element.13.field.rest_0_, f32[320,128]{1,0:T(8,128)S(1)} %collective-permute-done.2.rest_0_.y2, f32[320,128]{1,0:T(8,128)S(1)} %collective-permute-done.3.rest_1_.x1), custom_call_target="tpu_custom_call" | custom-call | tf_op jit(solution)/shard_map/pallas_call | solution.py:316
  25.7 0.8 shard_map.44.field.rest_0_
  26.5 3.6 %collective-permute-start.7 = (f32[320,128]{1,0:T(8,128)S(1)}, f32[320,128]{1,0:T(8,128)S(1)}, u32[]{:S(2)}, u32[]{:S(2)}) collective-permute-start(f32[320,128]{1,0:T(8,128)S(1)} %shard_map.44.field.rest_0_), channel_id=1, source_target_pairs={{0,64},{64,0},{128,192},{192,128},{256,320},{320,256},{384,448},{4... | collective-permute-start | bytes 491528 | tf_op jit(solution)/shard_map/ppermute | solution.py:271
  31.5 6.6 %collective-permute-start.8 = (f32[320,128]{1,0:T(8,128)S(1)}, f32[320,128]{1,0:T(8,128)S(1)}, u32[]{:S(2)}, u32[]{:S(2)}) collective-permute-start(f32[320,128]{1,0:T(8,128)S(1)} %shard_map.44.field.rest_0_), channel_id=1, source_target_pairs={{0,8},{8,0},{16,24},{24,16},{32,40},{40,32},{48,56},{56,48},{1,9},... | collective-permute-start | bytes 491528 | tf_op jit(solution)/shard_map/ppermute | solution.py:262
  38.2 1.5 %shard_map.45.part = f32[256,128]{1,0:T(8,128)S(1)} custom-call(s32[5]{0:T(128)S(1)} %stack.31.flags, f32[16,128]{1,0:T(8,128)S(1)} %bitcast.12, f32[320,128]{1,0:T(8,128)S(1)} %shard_map.44.field.rest_0_, f32[320,128]{1,0:T(8,128)S(1)} %get-tuple-element.13.field.rest_0_, f32[320,128]{1,0:T(8,128)S(1)} %collective-permute-done.6.rest_1_.y2, ...), custom_call_target="tpu_custom_call" | custom-call | tf_op jit(solution)/shard_map/pallas_call | solution.py:316
  39.7 0.8 shard_map.46.field
  40.5 3.5 %collective-permute-start.11 = (f32[320,128]{1,0:T(8,128)S(1)}, f32[320,128]{1,0:T(8,128)S(1)}, u32[]{:S(2)}, u32[]{:S(2)}) collective-permute-start(f32[320,128]{1,0:T(8,128)S(1)} %shard_map.46.field), channel_id=1, source_target_pairs={{0,64},{64,0},{128,192},{192,128},{256,320},{320,256},{384,448},{4... | collective-permute-start | bytes 491528 | tf_op jit(solution)/shard_map/ppermute | solution.py:271
  45.4 7.8 %collective-permute-start.12 = (f32[320,128]{1,0:T(8,128)S(1)}, f32[320,128]{1,0:T(8,128)S(1)}, u32[]{:S(2)}, u32[]{:S(2)}) collective-permute-start(f32[320,128]{1,0:T(8,128)S(1)} %shard_map.46.field), channel_id=1, source_target_pairs={{0,8},{8,0},{16,24},{24,16},{32,40},{40,32},{48,56},{56,48},{1,9},... | collective-permute-start | bytes 491528 | tf_op jit(solution)/shard_map/ppermute | solution.py:262
  53.3 1.5 %shard_map.47.part = f32[256,128]{1,0:T(8,128)S(1)} custom-call(s32[5]{0:T(128)S(1)} %stack.31.flags, f32[16,128]{1,0:T(8,128)S(1)} %bitcast.13, f32[320,128]{1,0:T(8,128)S(1)} %shard_map.46.field, f32[320,128]{1,0:T(8,128)S(1)} %shard_map.44.field.rest_0_, f32[320,128]{1,0:T(8,128)S(1)} %collective-permute-done.10.rest_1_.y2, ...), custom_call_target="tpu_custom_call" | custom-call | tf_op jit(solution)/shard_map/pallas_call | solution.py:316
  54.8 0.8 shard_map.48
  55.6 1.3 %collective-permute-start.15 = (f32[256,128]{1,0:T(8,128)S(1)}, f32[256,128]{1,0:T(8,128)S(1)}, u32[]{:S(2)}, u32[]{:S(2)}) collective-permute-start(f32[256,128]{1,0:T(8,128)S(1)} %get-tuple-element.14.field), channel_id=1, source_target_pairs={{64,0},{128,64},{192,128},{256,192},{320,256},{384,320},{448,384},... | collective-permute-start | bytes 393224 | tf_op jit(solution)/shard_map/ppermute | solution.py:281
  56.9 1.3 %collective-permute-start.14 = (f32[256,128]{1,0:T(8,128)S(1)}, f32[256,128]{1,0:T(8,128)S(1)}, u32[]{:S(2)}, u32[]{:S(2)}) collective-permute-start(f32[256,128]{1,0:T(8,128)S(1)} %get-tuple-element.14.field), channel_id=1, source_target_pairs={{8,0},{16,8},{24,16},{32,24},{40,32},{48,40},{56,48},{9,1},{17,9},... | collective-permute-start | bytes 393224 | tf_op jit(solution)/shard_map/ppermute | solution.py:285
  58.2 0.9 shard_map.49.part
  59.2 3.3 %collective-permute-done.15.beside_x = f32[256,128]{1,0:T(8,128)S(1)} collective-permute-done((f32[256,128]{1,0:T(8,128)S(1)}, f32[256,128]{1,0:T(8,128)S(1)}, u32[]{:S(2)}, u32[]{:S(2)}) %collective-permute-start.15) | collective-permute-done | bytes 131104 | tf_op jit(solution)/shard_map/ppermute | solution.py:281
  62.5 1.0 shard_map.50
  63.4 4.6 %collective-permute-start.16 = (f32[4,128]{1,0:T(4,128)S(1)}, f32[4,128]{1,0:T(4,128)S(1)}, u32[]{:S(2)}, u32[]{:S(2)}) collective-permute-start(f32[4,128]{1,0:T(4,128)S(1)} %shard_map.50), channel_id=1, source_target_pairs={{0,8},{8,0},{16,24},{24,16},{32,40},{40,32},{48,56},{56,48},{1,9},... | collective-permute-start | bytes 6152 | tf_op jit(solution)/shard_map/ppermute | solution.py:303
  68.1 0.8 collective-permute-done.16
  68.9 12.1 %psum.28 = f32[4,128]{1,0:T(4,128)S(1)} all-reduce(f32[4,128]{1,0:T(4,128)S(1)} %add.28), channel_id=1, replica_groups={{0,16,32,48},{1,17,33,49},{2,18,34,50},{3,19,35,51},{4,20,36,52},{5,21,..., use_global_device_ids=true, to_apply=%region_0.1 | all-reduce | flops 512 | bytes 4096 | tf_op jit(solution)/shard_map/psum | solution.py:306
  80.9 15.3 %psum.29 = f32[4,128]{1,0:T(4,128)S(1)} all-reduce(f32[4,128]{1,0:T(4,128)S(1)} %psum.28), channel_id=1, replica_groups={{0,1,2,3},{4,5,6,7},{16,17,18,19},{20,21,22,23},{32,33,34,35},{36,37,38..., use_global_device_ids=true, to_apply=%region_1.2 | all-reduce | flops 512 | bytes 4096 | tf_op jit(solution)/shard_map/psum | solution.py:306
  96.2 12.2 %psum.30 = f32[4,128]{1,0:T(4,128)S(1)} all-reduce(f32[4,128]{1,0:T(4,128)S(1)} %psum.29), channel_id=1, replica_groups={{0,64,128,192},{256,320,384,448},{1,65,129,193},{257,321,385,449},{2,66..., use_global_device_ids=true, to_apply=%region_2.3 | all-reduce | flops 512 | bytes 4096 | tf_op jit(solution)/shard_map/psum | solution.py:306
  108.4 15.6 %psum.31.sums = f32[4,128]{1,0:T(4,128)S(1)} all-reduce(f32[4,128]{1,0:T(4,128)S(1)} %psum.30), channel_id=1, replica_groups={{0,256,4,260},{1,257,5,261},{2,258,6,262},{3,259,7,263},{16,272,20,276}..., use_global_device_ids=true, to_apply=%region_3.4 | all-reduce | flops 512 | bytes 4096 | tf_op jit(solution)/shard_map/psum | solution.py:306
  124.0 2.6 %shard_map.51 = (f32[256,128]{1,0:T(8,128)}, f32[16,16]{1,0:T(8,128)}) custom-call(f32[4,128]{1,0:T(4,128)S(1)} %psum.31.sums, f32[256,128]{1,0:T(8,128)S(1)} %get-tuple-element.14.field), custom_call_target="tpu_custom_call" | custom-call | tf_op jit(solution)/shard_map/pallas_call | solution.py:316
  (23 shorter events, 3.4 us)
Async XLA Ops:
  0.7 0.7 copy-start.1
  1.4 0.9 copy-start
  3.0 8.5 %collective-permute-start = (f32[40,128]{1,0:T(8,128)S(1)}, f32[40,128]{1,0:T(8,128)S(1)}, u32[]{:S(2)}, u32[]{:S(2)}) collective-permute-start(f32[40,128]{1,0:T(8,128)S(1)} %get-tuple-element.10), channel_id=1, source_target_pairs={{1,2},{2,1},{3,4},{4,3},{5,6},{6,5},{9,10},{10,9},{11,12},{12,11},... | collective-permute-start | bytes 61448 | tf_op jit(solution)/shard_map/ppermute | solution.py:262
  6.4 6.8 %collective-permute-start.1 = (f32[40,128]{1,0:T(8,128)S(1)}, f32[40,128]{1,0:T(8,128)S(1)}, u32[]{:S(2)}, u32[]{:S(2)}) collective-permute-start(f32[40,128]{1,0:T(8,128)S(1)} %get-tuple-element.11), channel_id=1, source_target_pairs={{0,1},{1,0},{2,3},{3,2},{4,5},{5,4},{6,7},{7,6},{8,9},{9,8},{10,11... | collective-permute-start | bytes 61448 | tf_op jit(solution)/shard_map/ppermute | solution.py:262
  14.0 10.1 %collective-permute-start.3 = (f32[320,128]{1,0:T(8,128)S(1)}, f32[320,128]{1,0:T(8,128)S(1)}, u32[]{:S(2)}, u32[]{:S(2)}) collective-permute-start(f32[320,128]{1,0:T(8,128)S(1)} %get-tuple-element.13.field.rest_0_), channel_id=1, source_target_pairs={{0,64},{64,0},{128,192},{192,128},{256,320},{320,256},{384,448},{4... | collective-permute-start | bytes 491528 | tf_op jit(solution)/shard_map/ppermute | solution.py:271
  16.7 7.5 %collective-permute-start.2 = (f32[320,128]{1,0:T(8,128)S(1)}, f32[320,128]{1,0:T(8,128)S(1)}, u32[]{:S(2)}, u32[]{:S(2)}) collective-permute-start(f32[320,128]{1,0:T(8,128)S(1)} %get-tuple-element.13.field.rest_0_), channel_id=1, source_target_pairs={{8,16},{16,8},{24,32},{32,24},{40,48},{48,40},{9,17},{17,9},{25,33... | collective-permute-start | bytes 491528 | tf_op jit(solution)/shard_map/ppermute | solution.py:262
  17.4 8.3 %collective-permute-start.5 = (f32[320,128]{1,0:T(8,128)S(1)}, f32[320,128]{1,0:T(8,128)S(1)}, u32[]{:S(2)}, u32[]{:S(2)}) collective-permute-start(f32[320,128]{1,0:T(8,128)S(1)} %get-tuple-element.13.field.rest_0_), channel_id=1, source_target_pairs={{64,128},{128,64},{192,256},{256,192},{320,384},{384,320},{8,72},{... | collective-permute-start | bytes 491528 | tf_op jit(solution)/shard_map/ppermute | solution.py:271
  18.1 7.6 %collective-permute-start.4 = (f32[320,128]{1,0:T(8,128)S(1)}, f32[320,128]{1,0:T(8,128)S(1)}, u32[]{:S(2)}, u32[]{:S(2)}) collective-permute-start(f32[320,128]{1,0:T(8,128)S(1)} %get-tuple-element.13.field.rest_0_), channel_id=1, source_target_pairs={{0,8},{8,0},{16,24},{24,16},{32,40},{40,32},{48,56},{56,48},{1,9},... | collective-permute-start | bytes 491528 | tf_op jit(solution)/shard_map/ppermute | solution.py:262
  26.5 11.6 %collective-permute-start.7 = (f32[320,128]{1,0:T(8,128)S(1)}, f32[320,128]{1,0:T(8,128)S(1)}, u32[]{:S(2)}, u32[]{:S(2)}) collective-permute-start(f32[320,128]{1,0:T(8,128)S(1)} %shard_map.44.field.rest_0_), channel_id=1, source_target_pairs={{0,64},{64,0},{128,192},{192,128},{256,320},{320,256},{384,448},{4... | collective-permute-start | bytes 491528 | tf_op jit(solution)/shard_map/ppermute | solution.py:271
  30.2 8.0 %collective-permute-start.6 = (f32[320,128]{1,0:T(8,128)S(1)}, f32[320,128]{1,0:T(8,128)S(1)}, u32[]{:S(2)}, u32[]{:S(2)}) collective-permute-start(f32[320,128]{1,0:T(8,128)S(1)} %shard_map.44.field.rest_0_), channel_id=1, source_target_pairs={{8,16},{16,8},{24,32},{32,24},{40,48},{48,40},{9,17},{17,9},{25,33... | collective-permute-start | bytes 491528 | tf_op jit(solution)/shard_map/ppermute | solution.py:262
  30.8 8.8 %collective-permute-start.9 = (f32[320,128]{1,0:T(8,128)S(1)}, f32[320,128]{1,0:T(8,128)S(1)}, u32[]{:S(2)}, u32[]{:S(2)}) collective-permute-start(f32[320,128]{1,0:T(8,128)S(1)} %shard_map.44.field.rest_0_), channel_id=1, source_target_pairs={{64,128},{128,64},{192,256},{256,192},{320,384},{384,320},{8,72},{... | collective-permute-start | bytes 491528 | tf_op jit(solution)/shard_map/ppermute | solution.py:271
  31.5 8.2 %collective-permute-start.8 = (f32[320,128]{1,0:T(8,128)S(1)}, f32[320,128]{1,0:T(8,128)S(1)}, u32[]{:S(2)}, u32[]{:S(2)}) collective-permute-start(f32[320,128]{1,0:T(8,128)S(1)} %shard_map.44.field.rest_0_), channel_id=1, source_target_pairs={{0,8},{8,0},{16,24},{24,16},{32,40},{40,32},{48,56},{56,48},{1,9},... | collective-permute-start | bytes 491528 | tf_op jit(solution)/shard_map/ppermute | solution.py:262
  40.5 12.7 %collective-permute-start.11 = (f32[320,128]{1,0:T(8,128)S(1)}, f32[320,128]{1,0:T(8,128)S(1)}, u32[]{:S(2)}, u32[]{:S(2)}) collective-permute-start(f32[320,128]{1,0:T(8,128)S(1)} %shard_map.46.field), channel_id=1, source_target_pairs={{0,64},{64,0},{128,192},{192,128},{256,320},{320,256},{384,448},{4... | collective-permute-start | bytes 491528 | tf_op jit(solution)/shard_map/ppermute | solution.py:271
  44.1 9.2 %collective-permute-start.10 = (f32[320,128]{1,0:T(8,128)S(1)}, f32[320,128]{1,0:T(8,128)S(1)}, u32[]{:S(2)}, u32[]{:S(2)}) collective-permute-start(f32[320,128]{1,0:T(8,128)S(1)} %shard_map.46.field), channel_id=1, source_target_pairs={{8,16},{16,8},{24,32},{32,24},{40,48},{48,40},{9,17},{17,9},{25,33... | collective-permute-start | bytes 491528 | tf_op jit(solution)/shard_map/ppermute | solution.py:262
  44.7 10.0 %collective-permute-start.13 = (f32[320,128]{1,0:T(8,128)S(1)}, f32[320,128]{1,0:T(8,128)S(1)}, u32[]{:S(2)}, u32[]{:S(2)}) collective-permute-start(f32[320,128]{1,0:T(8,128)S(1)} %shard_map.46.field), channel_id=1, source_target_pairs={{64,128},{128,64},{192,256},{256,192},{320,384},{384,320},{8,72},{... | collective-permute-start | bytes 491528 | tf_op jit(solution)/shard_map/ppermute | solution.py:271
  45.4 9.4 %collective-permute-start.12 = (f32[320,128]{1,0:T(8,128)S(1)}, f32[320,128]{1,0:T(8,128)S(1)}, u32[]{:S(2)}, u32[]{:S(2)}) collective-permute-start(f32[320,128]{1,0:T(8,128)S(1)} %shard_map.46.field), channel_id=1, source_target_pairs={{0,8},{8,0},{16,24},{24,16},{32,40},{40,32},{48,56},{56,48},{1,9},... | collective-permute-start | bytes 491528 | tf_op jit(solution)/shard_map/ppermute | solution.py:262
  55.6 6.9 %collective-permute-start.15 = (f32[256,128]{1,0:T(8,128)S(1)}, f32[256,128]{1,0:T(8,128)S(1)}, u32[]{:S(2)}, u32[]{:S(2)}) collective-permute-start(f32[256,128]{1,0:T(8,128)S(1)} %get-tuple-element.14.field), channel_id=1, source_target_pairs={{64,0},{128,64},{192,128},{256,192},{320,256},{384,320},{448,384},... | collective-permute-start | bytes 393224 | tf_op jit(solution)/shard_map/ppermute | solution.py:281
  56.9 5.6 %collective-permute-start.14 = (f32[256,128]{1,0:T(8,128)S(1)}, f32[256,128]{1,0:T(8,128)S(1)}, u32[]{:S(2)}, u32[]{:S(2)}) collective-permute-start(f32[256,128]{1,0:T(8,128)S(1)} %get-tuple-element.14.field), channel_id=1, source_target_pairs={{8,0},{16,8},{24,16},{32,24},{40,32},{48,40},{56,48},{9,1},{17,9},... | collective-permute-start | bytes 393224 | tf_op jit(solution)/shard_map/ppermute | solution.py:285
  63.4 5.4 %collective-permute-start.16 = (f32[4,128]{1,0:T(4,128)S(1)}, f32[4,128]{1,0:T(4,128)S(1)}, u32[]{:S(2)}, u32[]{:S(2)}) collective-permute-start(f32[4,128]{1,0:T(4,128)S(1)} %shard_map.50), channel_id=1, source_target_pairs={{0,8},{8,0},{16,24},{24,16},{32,40},{40,32},{48,56},{56,48},{1,9},... | collective-permute-start | bytes 6152 | tf_op jit(solution)/shard_map/ppermute | solution.py:303

commit v5 on v3

--- a/solution.py
+++ b/solution.py
@@ -98,7 +98,7 @@
 
 def block_kernel(scale, with_previous, flags, potential, field, *rest):
     previous = rest[0] if with_previous else None
-    y2, x1, out = rest[-3:]
+    x1, y2, out = rest[-3:]
     lane = lane_index(ORB)
     weight = [-0.5 * scale * w for w in WEIGHTS]
     shift = MIDDLE + 1.5 * WEIGHTS[0]
@@ -129,7 +129,7 @@
             out[cell * ORB : (cell + 1) * ORB, :] = total
 
 
-def join_kernel(scale, with_previous, split, flags, edge_potential, part, field, y1, x2, y2, x1, *rest):
+def join_kernel(scale, with_previous, split, flags, edge_potential, part, field, y1, x2, x1, y2, *rest):
     previous = rest[0] if with_previous else None
     out = rest[-2] if split else rest[-1]
     lane = lane_index(ORB)
@@ -332,10 +332,10 @@
     def advance(field, scale, previous, split):
         y2, y1, x2, x1 = swap(field, "gy", 1), swap(field, "gy", 0), swap_x(field, 1), swap_x(field, 0)
         kernel = functools.partial(block_kernel, scale, bool(previous))
-        (part,) = call(kernel, (block,))(flags, potential, field, *previous, y2, x1)
+        (part,) = call(kernel, (block,))(flags, potential, field, *previous, x1, y2)
         kernel = functools.partial(join_kernel, scale, bool(previous), split)
         outs = (block, edge) if split else (sent,)
-        return call(kernel, outs)(flags, edge_potential, part, field, y1, x2, y2, x1, *previous)
+        return call(kernel, outs)(flags, edge_potential, part, field, y1, x2, x1, y2, *previous)
 
     (field1,) = advance(field, 1.0 / HALF, (), False)
     (field2,) = advance(field1, 2.0 / HALF, (field,), False)

time: 127 us -> 127 us (level)
  blocking collectives: 55.2 us -> 52.1 us
  starting transfers between devices: 50.1 us -> 53 us
    ppermute x8, starting transfers between devices: 31 us -> 37.3 us  [swap(): return lax.ppermute(value, axis, pairs)]
    psum x1, blocking collectives: 12.1 us -> 8.85 us  [sum_everywhere(): lax.psum(value, 'gy', axis_index_groups=[[0, 2, 4, 6], [1, 3, 5, 7]])]
    ppermute x6, starting transfers between devices: 11.9 us -> 9.08 us  [swap_x(): return lax.ppermute(value, ('gx', 'gy'), pairs)]
where the time goes in v5:
time: 127 us
  starting transfers between devices  53 us (42%)
  blocking collectives  52.1 us (41%)
  Pallas kernels  12.9 us (10%)
  waiting for transfers between devices  5.89 us (5%)
  local copies, waits for them, and re-layouts  1.59 us (1%)
    ppermute x8, starting transfers between devices, swap(): return lax.ppermute(value, axis, pairs)  37.3 us
    psum x1, blocking collectives, sum_everywhere(): value = lax.psum(value, 'gz', axis_index_groups=fours)  16.1 us
    psum x1, blocking collectives, sum_everywhere(): return lax.psum(value, ('gx', 'gz'), axis_index_groups=rings)  15.6 us
    pallas_call x11, Pallas kernels, run(): pl.pallas_call(kernel, out_shape=[jax.ShapeDtypeStruct(shape, jnp.float32...  12.9 us
    psum x1, blocking collectives, sum_everywhere(): value = lax.psum(value, 'gx', axis_index_groups=fours)  11.6 us
    ppermute x6, starting transfers between devices, swap_x(): return lax.ppermute(value, ('gx', 'gy'), pairs)  9.08 us
    psum x1, blocking collectives, sum_everywhere(): lax.psum(value, 'gy', axis_index_groups=[[0, 2, 4, 6], [1, 3, 5, 7]])  8.85 us
    ppermute x1, starting transfers between devices, sum_everywhere(): value = value + lax.ppermute(value, 'gy', [(i, i ^ 1) for i in range(8)])  4.07 us
  transfers between devices with their start and end apart: 17, of which 3 were waited for; matrix products, arithmetic and copies ran while one was open for 0% of the time, Pallas kernels for 4%

profile of v5, /device:TPU:2, one launch (start us, length us, event | category | flops | bytes accessed | tf_op | source)
XLA Modules:
  0.0 126.5 jit_solution(9292573130095959838)
XLA Ops:
  1.4 0.9 copy-done
  2.3 0.7 shard_map.41
  3.0 3.4 %collective-permute-start = (f32[40,128]{1,0:T(8,128)S(1)}, f32[40,128]{1,0:T(8,128)S(1)}, u32[]{:S(2)}, u32[]{:S(2)}) collective-permute-start(f32[40,128]{1,0:T(8,128)S(1)} %get-tuple-element.10), channel_id=1, source_target_pairs={{1,2},{2,1},{3,4},{4,3},{5,6},{6,5},{9,10},{10,9},{11,12},{12,11},... | collective-permute-start | bytes 61448 | tf_op jit(solution)/shard_map/ppermute | solution.py:262
  6.4 5.1 %collective-permute-start.1 = (f32[40,128]{1,0:T(8,128)S(1)}, f32[40,128]{1,0:T(8,128)S(1)}, u32[]{:S(2)}, u32[]{:S(2)}) collective-permute-start(f32[40,128]{1,0:T(8,128)S(1)} %get-tuple-element.11), channel_id=1, source_target_pairs={{0,1},{1,0},{2,3},{3,2},{4,5},{5,4},{6,7},{7,6},{8,9},{9,8},{10,11... | collective-permute-start | bytes 61448 | tf_op jit(solution)/shard_map/ppermute | solution.py:262
  11.5 1.7 %collective-permute-done.1.first = f32[40,128]{1,0:T(8,128)S(1)} collective-permute-done((f32[40,128]{1,0:T(8,128)S(1)}, f32[40,128]{1,0:T(8,128)S(1)}, u32[]{:S(2)}, u32[]{:S(2)}) %collective-permute-start.1) | collective-permute-done | bytes 20512 | tf_op jit(solution)/shard_map/ppermute | solution.py:262
  13.2 0.8 shard_map.42
  14.0 0.7 collective-permute-start.3
  14.7 2.7 %collective-permute-start.2 = (f32[320,128]{1,0:T(8,128)S(1)}, f32[320,128]{1,0:T(8,128)S(1)}, u32[]{:S(2)}, u32[]{:S(2)}) collective-permute-start(f32[320,128]{1,0:T(8,128)S(1)} %get-tuple-element.13.field.rest_0_), channel_id=1, source_target_pairs={{0,64},{64,0},{128,192},{192,128},{256,320},{320,256},{384,448},{4... | collective-permute-start | bytes 491528 | tf_op jit(solution)/shard_map/ppermute | solution.py:271
  17.4 0.7 collective-permute-start.5
  18.1 7.4 %collective-permute-start.4 = (f32[320,128]{1,0:T(8,128)S(1)}, f32[320,128]{1,0:T(8,128)S(1)}, u32[]{:S(2)}, u32[]{:S(2)}) collective-permute-start(f32[320,128]{1,0:T(8,128)S(1)} %get-tuple-element.13.field.rest_0_), channel_id=1, source_target_pairs={{0,8},{8,0},{16,24},{24,16},{32,40},{40,32},{48,56},{56,48},{1,9},... | collective-permute-start | bytes 491528 | tf_op jit(solution)/shard_map/ppermute | solution.py:262
  25.5 1.5 %shard_map.43.part = f32[256,128]{1,0:T(8,128)S(1)} custom-call(s32[5]{0:T(128)S(1)} %stack.31.flags, f32[16,128]{1,0:T(8,128)S(1)} %bitcast.11, f32[320,128]{1,0:T(8,128)S(1)} %get-tuple-element.13.field.rest_0_, f32[320,128]{1,0:T(8,128)S(1)} %collective-permute-done.2.rest_0_.x1, f32[320,128]{1,0:T(8,128)S(1)} %collective-permute-done.3.rest_1_.y2), custom_call_target="tpu_custom_call" | custom-call | tf_op jit(solution)/shard_map/pallas_call | solution.py:305
  27.0 0.8 shard_map.44.field.rest_0_
  28.5 2.2 %collective-permute-start.6 = (f32[320,128]{1,0:T(8,128)S(1)}, f32[320,128]{1,0:T(8,128)S(1)}, u32[]{:S(2)}, u32[]{:S(2)}) collective-permute-start(f32[320,128]{1,0:T(8,128)S(1)} %shard_map.44.field.rest_0_), channel_id=1, source_target_pairs={{0,64},{64,0},{128,192},{192,128},{256,320},{320,256},{384,448},{4... | collective-permute-start | bytes 491528 | tf_op jit(solution)/shard_map/ppermute | solution.py:271
  31.4 10.3 %collective-permute-start.8 = (f32[320,128]{1,0:T(8,128)S(1)}, f32[320,128]{1,0:T(8,128)S(1)}, u32[]{:S(2)}, u32[]{:S(2)}) collective-permute-start(f32[320,128]{1,0:T(8,128)S(1)} %shard_map.44.field.rest_0_), channel_id=1, source_target_pairs={{0,8},{8,0},{16,24},{24,16},{32,40},{40,32},{48,56},{56,48},{1,9},... | collective-permute-start | bytes 491528 | tf_op jit(solution)/shard_map/ppermute | solution.py:262
  41.7 1.5 %shard_map.45.part = f32[256,128]{1,0:T(8,128)S(1)} custom-call(s32[5]{0:T(128)S(1)} %stack.31.flags, f32[16,128]{1,0:T(8,128)S(1)} %bitcast.12, f32[320,128]{1,0:T(8,128)S(1)} %shard_map.44.field.rest_0_, f32[320,128]{1,0:T(8,128)S(1)} %get-tuple-element.13.field.rest_0_, f32[320,128]{1,0:T(8,128)S(1)} %collective-permute-done.6.rest_1_.x1, ...), custom_call_target="tpu_custom_call" | custom-call | tf_op jit(solution)/shard_map/pallas_call | solution.py:305
  43.2 0.8 shard_map.46.field
  44.7 2.2 %collective-permute-start.10 = (f32[320,128]{1,0:T(8,128)S(1)}, f32[320,128]{1,0:T(8,128)S(1)}, u32[]{:S(2)}, u32[]{:S(2)}) collective-permute-start(f32[320,128]{1,0:T(8,128)S(1)} %shard_map.46.field), channel_id=1, source_target_pairs={{0,64},{64,0},{128,192},{192,128},{256,320},{320,256},{384,448},{4... | collective-permute-start | bytes 491528 | tf_op jit(solution)/shard_map/ppermute | solution.py:271
  47.6 9.1 %collective-permute-start.12 = (f32[320,128]{1,0:T(8,128)S(1)}, f32[320,128]{1,0:T(8,128)S(1)}, u32[]{:S(2)}, u32[]{:S(2)}) collective-permute-start(f32[320,128]{1,0:T(8,128)S(1)} %shard_map.46.field), channel_id=1, source_target_pairs={{0,8},{8,0},{16,24},{24,16},{32,40},{40,32},{48,56},{56,48},{1,9},... | collective-permute-start | bytes 491528 | tf_op jit(solution)/shard_map/ppermute | solution.py:262
  56.7 1.5 %shard_map.47.part = f32[256,128]{1,0:T(8,128)S(1)} custom-call(s32[5]{0:T(128)S(1)} %stack.31.flags, f32[16,128]{1,0:T(8,128)S(1)} %bitcast.13, f32[320,128]{1,0:T(8,128)S(1)} %shard_map.46.field, f32[320,128]{1,0:T(8,128)S(1)} %shard_map.44.field.rest_0_, f32[320,128]{1,0:T(8,128)S(1)} %collective-permute-done.10.rest_1_.x1, ...), custom_call_target="tpu_custom_call" | custom-call | tf_op jit(solution)/shard_map/pallas_call | solution.py:305
  58.3 0.8 shard_map.48
  59.1 1.3 %collective-permute-start.15 = (f32[256,128]{1,0:T(8,128)S(1)}, f32[256,128]{1,0:T(8,128)S(1)}, u32[]{:S(2)}, u32[]{:S(2)}) collective-permute-start(f32[256,128]{1,0:T(8,128)S(1)} %get-tuple-element.14.field), channel_id=1, source_target_pairs={{64,0},{128,64},{192,128},{256,192},{320,256},{384,320},{448,384},... | collective-permute-start | bytes 393224 | tf_op jit(solution)/shard_map/ppermute | solution.py:281
  60.4 1.3 %collective-permute-start.14 = (f32[256,128]{1,0:T(8,128)S(1)}, f32[256,128]{1,0:T(8,128)S(1)}, u32[]{:S(2)}, u32[]{:S(2)}) collective-permute-start(f32[256,128]{1,0:T(8,128)S(1)} %get-tuple-element.14.field), channel_id=1, source_target_pairs={{8,0},{16,8},{24,16},{32,24},{40,32},{48,40},{56,48},{9,1},{17,9},... | collective-permute-start | bytes 393224 | tf_op jit(solution)/shard_map/ppermute | solution.py:285
  61.7 0.9 shard_map.49.part
  62.6 3.3 %collective-permute-done.15.beside_x = f32[256,128]{1,0:T(8,128)S(1)} collective-permute-done((f32[256,128]{1,0:T(8,128)S(1)}, f32[256,128]{1,0:T(8,128)S(1)}, u32[]{:S(2)}, u32[]{:S(2)}) %collective-permute-start.15) | collective-permute-done | bytes 131104 | tf_op jit(solution)/shard_map/ppermute | solution.py:281
  65.9 1.0 shard_map.50
  66.9 4.1 %collective-permute-start.16 = (f32[4,128]{1,0:T(4,128)S(1)}, f32[4,128]{1,0:T(4,128)S(1)}, u32[]{:S(2)}, u32[]{:S(2)}) collective-permute-start(f32[4,128]{1,0:T(4,128)S(1)} %shard_map.50), channel_id=1, source_target_pairs={{0,8},{8,0},{16,24},{24,16},{32,40},{40,32},{48,56},{56,48},{1,9},... | collective-permute-start | bytes 6152 | tf_op jit(solution)/shard_map/ppermute | solution.py:291
  71.0 0.8 collective-permute-done.16
  71.8 8.9 %psum.28 = f32[4,128]{1,0:T(4,128)S(1)} all-reduce(f32[4,128]{1,0:T(4,128)S(1)} %add.28), channel_id=1, replica_groups={{0,16,32,48},{8,24,40,56},{1,17,33,49},{9,25,41,57},{2,18,34,50},{10,26..., use_global_device_ids=true, to_apply=%region_0.1 | all-reduce | flops 512 | bytes 4096 | tf_op jit(solution)/shard_map/psum | solution.py:292
  80.6 16.1 %psum.29 = f32[4,128]{1,0:T(4,128)S(1)} all-reduce(f32[4,128]{1,0:T(4,128)S(1)} %psum.28), channel_id=1, replica_groups={{0,1,2,3},{4,5,6,7},{8,9,10,11},{12,13,14,15},{16,17,18,19},{20,21,22,2..., use_global_device_ids=true, to_apply=%region_1.2 | all-reduce | flops 512 | bytes 4096 | tf_op jit(solution)/shard_map/psum | solution.py:293
  96.7 11.6 %psum.30 = f32[4,128]{1,0:T(4,128)S(1)} all-reduce(f32[4,128]{1,0:T(4,128)S(1)} %psum.29), channel_id=1, replica_groups={{0,64,128,192},{256,320,384,448},{1,65,129,193},{257,321,385,449},{2,66..., use_global_device_ids=true, to_apply=%region_2.3 | all-reduce | flops 512 | bytes 4096 | tf_op jit(solution)/shard_map/psum | solution.py:294
  108.4 15.6 %psum.31.sums = f32[4,128]{1,0:T(4,128)S(1)} all-reduce(f32[4,128]{1,0:T(4,128)S(1)} %psum.30), channel_id=1, replica_groups={{0,256,4,260},{1,257,5,261},{2,258,6,262},{3,259,7,263},{64,320,68,324}..., use_global_device_ids=true, to_apply=%region_3.4 | all-reduce | flops 512 | bytes 4096 | tf_op jit(solution)/shard_map/psum | solution.py:296
  123.9 2.6 %shard_map.51 = (f32[256,128]{1,0:T(8,128)}, f32[16,16]{1,0:T(8,128)}) custom-call(f32[4,128]{1,0:T(4,128)S(1)} %psum.31.sums, f32[256,128]{1,0:T(8,128)S(1)} %get-tuple-element.14.field), custom_call_target="tpu_custom_call" | custom-call | tf_op jit(solution)/shard_map/pallas_call | solution.py:305
  (23 shorter events, 3.4 us)
Async XLA Ops:
  0.7 0.7 copy-start.1
  1.4 0.9 copy-start
  3.0 8.5 %collective-permute-start = (f32[40,128]{1,0:T(8,128)S(1)}, f32[40,128]{1,0:T(8,128)S(1)}, u32[]{:S(2)}, u32[]{:S(2)}) collective-permute-start(f32[40,128]{1,0:T(8,128)S(1)} %get-tuple-element.10), channel_id=1, source_target_pairs={{1,2},{2,1},{3,4},{4,3},{5,6},{6,5},{9,10},{10,9},{11,12},{12,11},... | collective-permute-start | bytes 61448 | tf_op jit(solution)/shard_map/ppermute | solution.py:262
  6.4 6.8 %collective-permute-start.1 = (f32[40,128]{1,0:T(8,128)S(1)}, f32[40,128]{1,0:T(8,128)S(1)}, u32[]{:S(2)}, u32[]{:S(2)}) collective-permute-start(f32[40,128]{1,0:T(8,128)S(1)} %get-tuple-element.11), channel_id=1, source_target_pairs={{0,1},{1,0},{2,3},{3,2},{4,5},{5,4},{6,7},{7,6},{8,9},{9,8},{10,11... | collective-permute-start | bytes 61448 | tf_op jit(solution)/shard_map/ppermute | solution.py:262
  14.0 11.5 %collective-permute-start.3 = (f32[320,128]{1,0:T(8,128)S(1)}, f32[320,128]{1,0:T(8,128)S(1)}, u32[]{:S(2)}, u32[]{:S(2)}) collective-permute-start(f32[320,128]{1,0:T(8,128)S(1)} %get-tuple-element.13.field.rest_0_), channel_id=1, source_target_pairs={{8,16},{16,8},{24,32},{32,24},{40,48},{48,40},{9,17},{17,9},{25,33... | collective-permute-start | bytes 491528 | tf_op jit(solution)/shard_map/ppermute | solution.py:262
  14.7 10.8 %collective-permute-start.2 = (f32[320,128]{1,0:T(8,128)S(1)}, f32[320,128]{1,0:T(8,128)S(1)}, u32[]{:S(2)}, u32[]{:S(2)}) collective-permute-start(f32[320,128]{1,0:T(8,128)S(1)} %get-tuple-element.13.field.rest_0_), channel_id=1, source_target_pairs={{0,64},{64,0},{128,192},{192,128},{256,320},{320,256},{384,448},{4... | collective-permute-start | bytes 491528 | tf_op jit(solution)/shard_map/ppermute | solution.py:271
  17.4 9.6 %collective-permute-start.5 = (f32[320,128]{1,0:T(8,128)S(1)}, f32[320,128]{1,0:T(8,128)S(1)}, u32[]{:S(2)}, u32[]{:S(2)}) collective-permute-start(f32[320,128]{1,0:T(8,128)S(1)} %get-tuple-element.13.field.rest_0_), channel_id=1, source_target_pairs={{64,128},{128,64},{192,256},{256,192},{320,384},{384,320},{8,72},{... | collective-permute-start | bytes 491528 | tf_op jit(solution)/shard_map/ppermute | solution.py:271
  18.1 9.0 %collective-permute-start.4 = (f32[320,128]{1,0:T(8,128)S(1)}, f32[320,128]{1,0:T(8,128)S(1)}, u32[]{:S(2)}, u32[]{:S(2)}) collective-permute-start(f32[320,128]{1,0:T(8,128)S(1)} %get-tuple-element.13.field.rest_0_), channel_id=1, source_target_pairs={{0,8},{8,0},{16,24},{24,16},{32,40},{40,32},{48,56},{56,48},{1,9},... | collective-permute-start | bytes 491528 | tf_op jit(solution)/shard_map/ppermute | solution.py:262
  27.9 13.8 %collective-permute-start.7 = (f32[320,128]{1,0:T(8,128)S(1)}, f32[320,128]{1,0:T(8,128)S(1)}, u32[]{:S(2)}, u32[]{:S(2)}) collective-permute-start(f32[320,128]{1,0:T(8,128)S(1)} %shard_map.44.field.rest_0_), channel_id=1, source_target_pairs={{8,16},{16,8},{24,32},{32,24},{40,48},{48,40},{9,17},{17,9},{25,33... | collective-permute-start | bytes 491528 | tf_op jit(solution)/shard_map/ppermute | solution.py:262
  28.5 13.2 %collective-permute-start.6 = (f32[320,128]{1,0:T(8,128)S(1)}, f32[320,128]{1,0:T(8,128)S(1)}, u32[]{:S(2)}, u32[]{:S(2)}) collective-permute-start(f32[320,128]{1,0:T(8,128)S(1)} %shard_map.44.field.rest_0_), channel_id=1, source_target_pairs={{0,64},{64,0},{128,192},{192,128},{256,320},{320,256},{384,448},{4... | collective-permute-start | bytes 491528 | tf_op jit(solution)/shard_map/ppermute | solution.py:271
  30.7 12.5 %collective-permute-start.9 = (f32[320,128]{1,0:T(8,128)S(1)}, f32[320,128]{1,0:T(8,128)S(1)}, u32[]{:S(2)}, u32[]{:S(2)}) collective-permute-start(f32[320,128]{1,0:T(8,128)S(1)} %shard_map.44.field.rest_0_), channel_id=1, source_target_pairs={{64,128},{128,64},{192,256},{256,192},{320,384},{384,320},{8,72},{... | collective-permute-start | bytes 491528 | tf_op jit(solution)/shard_map/ppermute | solution.py:271
  31.4 11.8 %collective-permute-start.8 = (f32[320,128]{1,0:T(8,128)S(1)}, f32[320,128]{1,0:T(8,128)S(1)}, u32[]{:S(2)}, u32[]{:S(2)}) collective-permute-start(f32[320,128]{1,0:T(8,128)S(1)} %shard_map.44.field.rest_0_), channel_id=1, source_target_pairs={{0,8},{8,0},{16,24},{24,16},{32,40},{40,32},{48,56},{56,48},{1,9},... | collective-permute-start | bytes 491528 | tf_op jit(solution)/shard_map/ppermute | solution.py:262
  44.1 12.6 %collective-permute-start.11 = (f32[320,128]{1,0:T(8,128)S(1)}, f32[320,128]{1,0:T(8,128)S(1)}, u32[]{:S(2)}, u32[]{:S(2)}) collective-permute-start(f32[320,128]{1,0:T(8,128)S(1)} %shard_map.46.field), channel_id=1, source_target_pairs={{8,16},{16,8},{24,32},{32,24},{40,48},{48,40},{9,17},{17,9},{25,33... | collective-permute-start | bytes 491528 | tf_op jit(solution)/shard_map/ppermute | solution.py:262
  44.7 12.0 %collective-permute-start.10 = (f32[320,128]{1,0:T(8,128)S(1)}, f32[320,128]{1,0:T(8,128)S(1)}, u32[]{:S(2)}, u32[]{:S(2)}) collective-permute-start(f32[320,128]{1,0:T(8,128)S(1)} %shard_map.46.field), channel_id=1, source_target_pairs={{0,64},{64,0},{128,192},{192,128},{256,320},{320,256},{384,448},{4... | collective-permute-start | bytes 491528 | tf_op jit(solution)/shard_map/ppermute | solution.py:271
  47.0 11.3 %collective-permute-start.13 = (f32[320,128]{1,0:T(8,128)S(1)}, f32[320,128]{1,0:T(8,128)S(1)}, u32[]{:S(2)}, u32[]{:S(2)}) collective-permute-start(f32[320,128]{1,0:T(8,128)S(1)} %shard_map.46.field), channel_id=1, source_target_pairs={{64,128},{128,64},{192,256},{256,192},{320,384},{384,320},{8,72},{... | collective-permute-start | bytes 491528 | tf_op jit(solution)/shard_map/ppermute | solution.py:271
  47.6 10.6 %collective-permute-start.12 = (f32[320,128]{1,0:T(8,128)S(1)}, f32[320,128]{1,0:T(8,128)S(1)}, u32[]{:S(2)}, u32[]{:S(2)}) collective-permute-start(f32[320,128]{1,0:T(8,128)S(1)} %shard_map.46.field), channel_id=1, source_target_pairs={{0,8},{8,0},{16,24},{24,16},{32,40},{40,32},{48,56},{56,48},{1,9},... | collective-permute-start | bytes 491528 | tf_op jit(solution)/shard_map/ppermute | solution.py:262
  59.1 6.9 %collective-permute-start.15 = (f32[256,128]{1,0:T(8,128)S(1)}, f32[256,128]{1,0:T(8,128)S(1)}, u32[]{:S(2)}, u32[]{:S(2)}) collective-permute-start(f32[256,128]{1,0:T(8,128)S(1)} %get-tuple-element.14.field), channel_id=1, source_target_pairs={{64,0},{128,64},{192,128},{256,192},{320,256},{384,320},{448,384},... | collective-permute-start | bytes 393224 | tf_op jit(solution)/shard_map/ppermute | solution.py:281
  60.4 5.6 %collective-permute-start.14 = (f32[256,128]{1,0:T(8,128)S(1)}, f32[256,128]{1,0:T(8,128)S(1)}, u32[]{:S(2)}, u32[]{:S(2)}) collective-permute-start(f32[256,128]{1,0:T(8,128)S(1)} %get-tuple-element.14.field), channel_id=1, source_target_pairs={{8,0},{16,8},{24,16},{32,24},{40,32},{48,40},{56,48},{9,1},{17,9},... | collective-permute-start | bytes 393224 | tf_op jit(solution)/shard_map/ppermute | solution.py:285
  66.9 4.9 %collective-permute-start.16 = (f32[4,128]{1,0:T(4,128)S(1)}, f32[4,128]{1,0:T(4,128)S(1)}, u32[]{:S(2)}, u32[]{:S(2)}) collective-permute-start(f32[4,128]{1,0:T(4,128)S(1)} %shard_map.50), channel_id=1, source_target_pairs={{0,8},{8,0},{16,24},{24,16},{32,40},{40,32},{48,56},{56,48},{1,9},... | collective-permute-start | bytes 6152 | tf_op jit(solution)/shard_map/ppermute | solution.py:291

commit v6 on v3

--- a/solution.py
+++ b/solution.py
@@ -242,17 +242,25 @@
     row = lax.broadcasted_iota(jnp.int32, (ORB, LANES), 0)
     lane = lane_index(ORB)
     work = jnp.where(lane < ORB, sums, jnp.where(lane == row + ORB, 1.0, 0.0))
-    for k in range(ORB - 1):
-        pivot = work[k : k + 1, :]
-        factor = work[:, k : k + 1] / pivot[:, k : k + 1]
-        work = work - jnp.where(row > k, factor, 0.0) * pivot
+    for k in range(0, ORB, 2):
+        top, next_row = work[k : k + 1, :], work[k + 1 : k + 2, :]
+        left, right = work[:, k : k + 1], work[:, k + 1 : k + 2]
+        corner, beside = top[:, k : k + 1], top[:, k + 1 : k + 2]
+        ratio = next_row[:, k : k + 1] / corner
+        low = next_row - ratio * top
+        pivot = next_row[:, k + 1 : k + 2] - ratio * beside
+        first = left / corner
+        second = (right - first * beside) / pivot
+        changed = work - first * top - second * low
+        work = jnp.where(row > k + 1, changed, jnp.where(row == k + 1, low, work))
     diagonal = jnp.sum(jnp.where(lane == row, work, 0.0), axis=1, keepdims=True)
     inverse = (work * (1.0 / jnp.sqrt(diagonal)))[:, ORB : 2 * ORB]
     half = sums[:, ORB : 2 * ORB]
     part = dot(dot(inverse, half, (1, 0)), inverse, (1, 1))
     ritz[...] = part + part.T
+    product = dot(inverse, jnp.concatenate([rows_of(field, cell) for cell in range(CELLS)], axis=1), (1, 0))
     for cell in range(CELLS):
-        q_block[pl.ds(cell, ORB, stride=CELLS), :] = dot(inverse, rows_of(field, cell), (1, 0))
+        q_block[pl.ds(cell, ORB, stride=CELLS), :] = product[:, cell * LANES : (cell + 1) * LANES]
 
 
 def swap(value, axis, first):

time: 127 us -> 128 us (level)
  no operation moved by 1% of the time
where the time goes in v6:
time: 128 us; the launch traced here: 127 us
  blocking collectives  55.2 us (43%)
  starting transfers between devices  50.1 us (39%)
  Pallas kernels  13.3 us (10%)
  waiting for transfers between devices  5.89 us (5%)
  local copies, waits for them, and re-layouts  1.59 us (1%)
    ppermute x8, starting transfers between devices, swap(): return lax.ppermute(value, axis, pairs)  31 us
    psum x1, blocking collectives, sum_everywhere(): return lax.psum(value, ('gx', 'gz'), axis_index_groups=rings)  15.6 us
    psum x1, blocking collectives, sum_everywhere(): value = lax.psum(value, 'gz', axis_index_groups=fours)  15.3 us
    pallas_call x11, Pallas kernels, run(): pl.pallas_call(kernel, out_shape=[jax.ShapeDtypeStruct(shape, jnp.float32...  13.3 us
    psum x1, blocking collectives, sum_everywhere(): value = lax.psum(value, 'gx', axis_index_groups=fours)  12.2 us
    psum x1, blocking collectives, sum_everywhere(): lax.psum(value, 'gy', axis_index_groups=[[0, 2, 4, 6], [1, 3, 5, 7]])  12.1 us
    ppermute x6, starting transfers between devices, swap_x(): return lax.ppermute(value, ('gx', 'gy'), pairs)  11.9 us
    ppermute x1, starting transfers between devices, sum_everywhere(): value = value + lax.ppermute(value, 'gy', [(i, i ^ 1) for i in range(8)])  4.61 us
  transfers between devices with their start and end apart: 17, of which 3 were waited for; matrix products, arithmetic and copies ran while one was open for 0% of the time, Pallas kernels for 4%

profile of v6, /device:TPU:2, one launch (start us, length us, event | category | flops | bytes accessed | tf_op | source)
XLA Modules:
  0.0 127.0 jit_solution(4029894797857725741)
XLA Ops:
  1.4 0.9 copy-done
  2.3 0.7 shard_map.41
  3.0 3.4 %collective-permute-start = (f32[40,128]{1,0:T(8,128)S(1)}, f32[40,128]{1,0:T(8,128)S(1)}, u32[]{:S(2)}, u32[]{:S(2)}) collective-permute-start(f32[40,128]{1,0:T(8,128)S(1)} %get-tuple-element.10), channel_id=1, source_target_pairs={{1,2},{2,1},{3,4},{4,3},{5,6},{6,5},{9,10},{10,9},{11,12},{12,11},... | collective-permute-start | bytes 61448 | tf_op jit(solution)/shard_map/ppermute | solution.py:270
  6.4 5.1 %collective-permute-start.1 = (f32[40,128]{1,0:T(8,128)S(1)}, f32[40,128]{1,0:T(8,128)S(1)}, u32[]{:S(2)}, u32[]{:S(2)}) collective-permute-start(f32[40,128]{1,0:T(8,128)S(1)} %get-tuple-element.11), channel_id=1, source_target_pairs={{0,1},{1,0},{2,3},{3,2},{4,5},{5,4},{6,7},{7,6},{8,9},{9,8},{10,11... | collective-permute-start | bytes 61448 | tf_op jit(solution)/shard_map/ppermute | solution.py:270
  11.5 1.7 %collective-permute-done.1.first = f32[40,128]{1,0:T(8,128)S(1)} collective-permute-done((f32[40,128]{1,0:T(8,128)S(1)}, f32[40,128]{1,0:T(8,128)S(1)}, u32[]{:S(2)}, u32[]{:S(2)}) %collective-permute-start.1) | collective-permute-done | bytes 20512 | tf_op jit(solution)/shard_map/ppermute | solution.py:270
  13.2 0.8 shard_map.42
  14.0 2.7 %collective-permute-start.3 = (f32[320,128]{1,0:T(8,128)S(1)}, f32[320,128]{1,0:T(8,128)S(1)}, u32[]{:S(2)}, u32[]{:S(2)}) collective-permute-start(f32[320,128]{1,0:T(8,128)S(1)} %get-tuple-element.13.field.rest_0_), channel_id=1, source_target_pairs={{0,64},{64,0},{128,192},{192,128},{256,320},{320,256},{384,448},{4... | collective-permute-start | bytes 491528 | tf_op jit(solution)/shard_map/ppermute | solution.py:279
  16.7 0.7 collective-permute-start.2
  17.4 0.7 collective-permute-start.5
  18.1 6.1 %collective-permute-start.4 = (f32[320,128]{1,0:T(8,128)S(1)}, f32[320,128]{1,0:T(8,128)S(1)}, u32[]{:S(2)}, u32[]{:S(2)}) collective-permute-start(f32[320,128]{1,0:T(8,128)S(1)} %get-tuple-element.13.field.rest_0_), channel_id=1, source_target_pairs={{0,8},{8,0},{16,24},{24,16},{32,40},{40,32},{48,56},{56,48},{1,9},... | collective-permute-start | bytes 491528 | tf_op jit(solution)/shard_map/ppermute | solution.py:270
  24.2 1.5 %shard_map.43.part = f32[256,128]{1,0:T(8,128)S(1)} custom-call(s32[5]{0:T(128)S(1)} %stack.31.flags, f32[16,128]{1,0:T(8,128)S(1)} %bitcast.11, f32[320,128]{1,0:T(8,128)S(1)} %get-tuple-element.13.field.rest_0_, f32[320,128]{1,0:T(8,128)S(1)} %collective-permute-done.2.rest_0_.y2, f32[320,128]{1,0:T(8,128)S(1)} %collective-permute-done.3.rest_1_.x1), custom_call_target="tpu_custom_call" | custom-call | tf_op jit(solution)/shard_map/pallas_call | solution.py:313
  25.7 0.8 shard_map.44.field.rest_0_
  26.5 3.6 %collective-permute-start.7 = (f32[320,128]{1,0:T(8,128)S(1)}, f32[320,128]{1,0:T(8,128)S(1)}, u32[]{:S(2)}, u32[]{:S(2)}) collective-permute-start(f32[320,128]{1,0:T(8,128)S(1)} %shard_map.44.field.rest_0_), channel_id=1, source_target_pairs={{0,64},{64,0},{128,192},{192,128},{256,320},{320,256},{384,448},{4... | collective-permute-start | bytes 491528 | tf_op jit(solution)/shard_map/ppermute | solution.py:279
  31.5 6.6 %collective-permute-start.8 = (f32[320,128]{1,0:T(8,128)S(1)}, f32[320,128]{1,0:T(8,128)S(1)}, u32[]{:S(2)}, u32[]{:S(2)}) collective-permute-start(f32[320,128]{1,0:T(8,128)S(1)} %shard_map.44.field.rest_0_), channel_id=1, source_target_pairs={{0,8},{8,0},{16,24},{24,16},{32,40},{40,32},{48,56},{56,48},{1,9},... | collective-permute-start | bytes 491528 | tf_op jit(solution)/shard_map/ppermute | solution.py:270
  38.2 1.5 %shard_map.45.part = f32[256,128]{1,0:T(8,128)S(1)} custom-call(s32[5]{0:T(128)S(1)} %stack.31.flags, f32[16,128]{1,0:T(8,128)S(1)} %bitcast.12, f32[320,128]{1,0:T(8,128)S(1)} %shard_map.44.field.rest_0_, f32[320,128]{1,0:T(8,128)S(1)} %get-tuple-element.13.field.rest_0_, f32[320,128]{1,0:T(8,128)S(1)} %collective-permute-done.6.rest_1_.y2, ...), custom_call_target="tpu_custom_call" | custom-call | tf_op jit(solution)/shard_map/pallas_call | solution.py:313
  39.7 0.8 shard_map.46.field
  40.5 3.5 %collective-permute-start.11 = (f32[320,128]{1,0:T(8,128)S(1)}, f32[320,128]{1,0:T(8,128)S(1)}, u32[]{:S(2)}, u32[]{:S(2)}) collective-permute-start(f32[320,128]{1,0:T(8,128)S(1)} %shard_map.46.field), channel_id=1, source_target_pairs={{0,64},{64,0},{128,192},{192,128},{256,320},{320,256},{384,448},{4... | collective-permute-start | bytes 491528 | tf_op jit(solution)/shard_map/ppermute | solution.py:279
  45.4 7.8 %collective-permute-start.12 = (f32[320,128]{1,0:T(8,128)S(1)}, f32[320,128]{1,0:T(8,128)S(1)}, u32[]{:S(2)}, u32[]{:S(2)}) collective-permute-start(f32[320,128]{1,0:T(8,128)S(1)} %shard_map.46.field), channel_id=1, source_target_pairs={{0,8},{8,0},{16,24},{24,16},{32,40},{40,32},{48,56},{56,48},{1,9},... | collective-permute-start | bytes 491528 | tf_op jit(solution)/shard_map/ppermute | solution.py:270
  53.3 1.5 %shard_map.47.part = f32[256,128]{1,0:T(8,128)S(1)} custom-call(s32[5]{0:T(128)S(1)} %stack.31.flags, f32[16,128]{1,0:T(8,128)S(1)} %bitcast.13, f32[320,128]{1,0:T(8,128)S(1)} %shard_map.46.field, f32[320,128]{1,0:T(8,128)S(1)} %shard_map.44.field.rest_0_, f32[320,128]{1,0:T(8,128)S(1)} %collective-permute-done.10.rest_1_.y2, ...), custom_call_target="tpu_custom_call" | custom-call | tf_op jit(solution)/shard_map/pallas_call | solution.py:313
  54.8 0.8 shard_map.48
  55.6 1.3 %collective-permute-start.15 = (f32[256,128]{1,0:T(8,128)S(1)}, f32[256,128]{1,0:T(8,128)S(1)}, u32[]{:S(2)}, u32[]{:S(2)}) collective-permute-start(f32[256,128]{1,0:T(8,128)S(1)} %get-tuple-element.14.field), channel_id=1, source_target_pairs={{64,0},{128,64},{192,128},{256,192},{320,256},{384,320},{448,384},... | collective-permute-start | bytes 393224 | tf_op jit(solution)/shard_map/ppermute | solution.py:289
  56.9 1.3 %collective-permute-start.14 = (f32[256,128]{1,0:T(8,128)S(1)}, f32[256,128]{1,0:T(8,128)S(1)}, u32[]{:S(2)}, u32[]{:S(2)}) collective-permute-start(f32[256,128]{1,0:T(8,128)S(1)} %get-tuple-element.14.field), channel_id=1, source_target_pairs={{8,0},{16,8},{24,16},{32,24},{40,32},{48,40},{56,48},{9,1},{17,9},... | collective-permute-start | bytes 393224 | tf_op jit(solution)/shard_map/ppermute | solution.py:293
  58.2 0.9 shard_map.49.part
  59.2 3.3 %collective-permute-done.15.beside_x = f32[256,128]{1,0:T(8,128)S(1)} collective-permute-done((f32[256,128]{1,0:T(8,128)S(1)}, f32[256,128]{1,0:T(8,128)S(1)}, u32[]{:S(2)}, u32[]{:S(2)}) %collective-permute-start.15) | collective-permute-done | bytes 131104 | tf_op jit(solution)/shard_map/ppermute | solution.py:289
  62.5 1.0 shard_map.50
  63.4 4.6 %collective-permute-start.16 = (f32[4,128]{1,0:T(4,128)S(1)}, f32[4,128]{1,0:T(4,128)S(1)}, u32[]{:S(2)}, u32[]{:S(2)}) collective-permute-start(f32[4,128]{1,0:T(4,128)S(1)} %shard_map.50), channel_id=1, source_target_pairs={{0,8},{8,0},{16,24},{24,16},{32,40},{40,32},{48,56},{56,48},{1,9},... | collective-permute-start | bytes 6152 | tf_op jit(solution)/shard_map/ppermute | solution.py:299
  68.1 0.8 collective-permute-done.16
  68.9 12.1 %psum.28 = f32[4,128]{1,0:T(4,128)S(1)} all-reduce(f32[4,128]{1,0:T(4,128)S(1)} %add.28), channel_id=1, replica_groups={{0,16,32,48},{8,24,40,56},{1,17,33,49},{9,25,41,57},{2,18,34,50},{10,26..., use_global_device_ids=true, to_apply=%region_0.1 | all-reduce | flops 512 | bytes 4096 | tf_op jit(solution)/shard_map/psum | solution.py:300
  80.9 15.3 %psum.29 = f32[4,128]{1,0:T(4,128)S(1)} all-reduce(f32[4,128]{1,0:T(4,128)S(1)} %psum.28), channel_id=1, replica_groups={{0,1,2,3},{4,5,6,7},{8,9,10,11},{12,13,14,15},{16,17,18,19},{20,21,22,2..., use_global_device_ids=true, to_apply=%region_1.2 | all-reduce | flops 512 | bytes 4096 | tf_op jit(solution)/shard_map/psum | solution.py:301
  96.2 12.2 %psum.30 = f32[4,128]{1,0:T(4,128)S(1)} all-reduce(f32[4,128]{1,0:T(4,128)S(1)} %psum.29), channel_id=1, replica_groups={{0,64,128,192},{256,320,384,448},{1,65,129,193},{257,321,385,449},{2,66..., use_global_device_ids=true, to_apply=%region_2.3 | all-reduce | flops 512 | bytes 4096 | tf_op jit(solution)/shard_map/psum | solution.py:302
  108.4 15.6 %psum.31.sums = f32[4,128]{1,0:T(4,128)S(1)} all-reduce(f32[4,128]{1,0:T(4,128)S(1)} %psum.30), channel_id=1, replica_groups={{0,256,4,260},{1,257,5,261},{2,258,6,262},{3,259,7,263},{64,320,68,324}..., use_global_device_ids=true, to_apply=%region_3.4 | all-reduce | flops 512 | bytes 4096 | tf_op jit(solution)/shard_map/psum | solution.py:304
  124.0 2.9 %shard_map.51 = (f32[256,128]{1,0:T(8,128)}, f32[16,16]{1,0:T(8,128)}) custom-call(f32[4,128]{1,0:T(4,128)S(1)} %psum.31.sums, f32[256,128]{1,0:T(8,128)S(1)} %get-tuple-element.14.field), custom_call_target="tpu_custom_call" | custom-call | tf_op jit(solution)/shard_map/pallas_call | solution.py:313
  (23 shorter events, 3.4 us)
Async XLA Ops:
  0.7 0.7 copy-start.1
  1.4 0.9 copy-start
  3.0 8.5 %collective-permute-start = (f32[40,128]{1,0:T(8,128)S(1)}, f32[40,128]{1,0:T(8,128)S(1)}, u32[]{:S(2)}, u32[]{:S(2)}) collective-permute-start(f32[40,128]{1,0:T(8,128)S(1)} %get-tuple-element.10), channel_id=1, source_target_pairs={{1,2},{2,1},{3,4},{4,3},{5,6},{6,5},{9,10},{10,9},{11,12},{12,11},... | collective-permute-start | bytes 61448 | tf_op jit(solution)/shard_map/ppermute | solution.py:270
  6.4 6.8 %collective-permute-start.1 = (f32[40,128]{1,0:T(8,128)S(1)}, f32[40,128]{1,0:T(8,128)S(1)}, u32[]{:S(2)}, u32[]{:S(2)}) collective-permute-start(f32[40,128]{1,0:T(8,128)S(1)} %get-tuple-element.11), channel_id=1, source_target_pairs={{0,1},{1,0},{2,3},{3,2},{4,5},{5,4},{6,7},{7,6},{8,9},{9,8},{10,11... | collective-permute-start | bytes 61448 | tf_op jit(solution)/shard_map/ppermute | solution.py:270
  14.0 10.1 %collective-permute-start.3 = (f32[320,128]{1,0:T(8,128)S(1)}, f32[320,128]{1,0:T(8,128)S(1)}, u32[]{:S(2)}, u32[]{:S(2)}) collective-permute-start(f32[320,128]{1,0:T(8,128)S(1)} %get-tuple-element.13.field.rest_0_), channel_id=1, source_target_pairs={{0,64},{64,0},{128,192},{192,128},{256,320},{320,256},{384,448},{4... | collective-permute-start | bytes 491528 | tf_op jit(solution)/shard_map/ppermute | solution.py:279
  16.7 7.5 %collective-permute-start.2 = (f32[320,128]{1,0:T(8,128)S(1)}, f32[320,128]{1,0:T(8,128)S(1)}, u32[]{:S(2)}, u32[]{:S(2)}) collective-permute-start(f32[320,128]{1,0:T(8,128)S(1)} %get-tuple-element.13.field.rest_0_), channel_id=1, source_target_pairs={{8,16},{16,8},{24,32},{32,24},{40,48},{48,40},{9,17},{17,9},{25,33... | collective-permute-start | bytes 491528 | tf_op jit(solution)/shard_map/ppermute | solution.py:270
  17.4 8.3 %collective-permute-start.5 = (f32[320,128]{1,0:T(8,128)S(1)}, f32[320,128]{1,0:T(8,128)S(1)}, u32[]{:S(2)}, u32[]{:S(2)}) collective-permute-start(f32[320,128]{1,0:T(8,128)S(1)} %get-tuple-element.13.field.rest_0_), channel_id=1, source_target_pairs={{64,128},{128,64},{192,256},{256,192},{320,384},{384,320},{8,72},{... | collective-permute-start | bytes 491528 | tf_op jit(solution)/shard_map/ppermute | solution.py:279
  18.1 7.6 %collective-permute-start.4 = (f32[320,128]{1,0:T(8,128)S(1)}, f32[320,128]{1,0:T(8,128)S(1)}, u32[]{:S(2)}, u32[]{:S(2)}) collective-permute-start(f32[320,128]{1,0:T(8,128)S(1)} %get-tuple-element.13.field.rest_0_), channel_id=1, source_target_pairs={{0,8},{8,0},{16,24},{24,16},{32,40},{40,32},{48,56},{56,48},{1,9},... | collective-permute-start | bytes 491528 | tf_op jit(solution)/shard_map/ppermute | solution.py:270
  26.5 11.6 %collective-permute-start.7 = (f32[320,128]{1,0:T(8,128)S(1)}, f32[320,128]{1,0:T(8,128)S(1)}, u32[]{:S(2)}, u32[]{:S(2)}) collective-permute-start(f32[320,128]{1,0:T(8,128)S(1)} %shard_map.44.field.rest_0_), channel_id=1, source_target_pairs={{0,64},{64,0},{128,192},{192,128},{256,320},{320,256},{384,448},{4... | collective-permute-start | bytes 491528 | tf_op jit(solution)/shard_map/ppermute | solution.py:279
  30.2 8.0 %collective-permute-start.6 = (f32[320,128]{1,0:T(8,128)S(1)}, f32[320,128]{1,0:T(8,128)S(1)}, u32[]{:S(2)}, u32[]{:S(2)}) collective-permute-start(f32[320,128]{1,0:T(8,128)S(1)} %shard_map.44.field.rest_0_), channel_id=1, source_target_pairs={{8,16},{16,8},{24,32},{32,24},{40,48},{48,40},{9,17},{17,9},{25,33... | collective-permute-start | bytes 491528 | tf_op jit(solution)/shard_map/ppermute | solution.py:270
  30.8 8.8 %collective-permute-start.9 = (f32[320,128]{1,0:T(8,128)S(1)}, f32[320,128]{1,0:T(8,128)S(1)}, u32[]{:S(2)}, u32[]{:S(2)}) collective-permute-start(f32[320,128]{1,0:T(8,128)S(1)} %shard_map.44.field.rest_0_), channel_id=1, source_target_pairs={{64,128},{128,64},{192,256},{256,192},{320,384},{384,320},{8,72},{... | collective-permute-start | bytes 491528 | tf_op jit(solution)/shard_map/ppermute | solution.py:279
  31.5 8.2 %collective-permute-start.8 = (f32[320,128]{1,0:T(8,128)S(1)}, f32[320,128]{1,0:T(8,128)S(1)}, u32[]{:S(2)}, u32[]{:S(2)}) collective-permute-start(f32[320,128]{1,0:T(8,128)S(1)} %shard_map.44.field.rest_0_), channel_id=1, source_target_pairs={{0,8},{8,0},{16,24},{24,16},{32,40},{40,32},{48,56},{56,48},{1,9},... | collective-permute-start | bytes 491528 | tf_op jit(solution)/shard_map/ppermute | solution.py:270
  40.5 12.7 %collective-permute-start.11 = (f32[320,128]{1,0:T(8,128)S(1)}, f32[320,128]{1,0:T(8,128)S(1)}, u32[]{:S(2)}, u32[]{:S(2)}) collective-permute-start(f32[320,128]{1,0:T(8,128)S(1)} %shard_map.46.field), channel_id=1, source_target_pairs={{0,64},{64,0},{128,192},{192,128},{256,320},{320,256},{384,448},{4... | collective-permute-start | bytes 491528 | tf_op jit(solution)/shard_map/ppermute | solution.py:279
  44.1 9.2 %collective-permute-start.10 = (f32[320,128]{1,0:T(8,128)S(1)}, f32[320,128]{1,0:T(8,128)S(1)}, u32[]{:S(2)}, u32[]{:S(2)}) collective-permute-start(f32[320,128]{1,0:T(8,128)S(1)} %shard_map.46.field), channel_id=1, source_target_pairs={{8,16},{16,8},{24,32},{32,24},{40,48},{48,40},{9,17},{17,9},{25,33... | collective-permute-start | bytes 491528 | tf_op jit(solution)/shard_map/ppermute | solution.py:270
  44.7 10.0 %collective-permute-start.13 = (f32[320,128]{1,0:T(8,128)S(1)}, f32[320,128]{1,0:T(8,128)S(1)}, u32[]{:S(2)}, u32[]{:S(2)}) collective-permute-start(f32[320,128]{1,0:T(8,128)S(1)} %shard_map.46.field), channel_id=1, source_target_pairs={{64,128},{128,64},{192,256},{256,192},{320,384},{384,320},{8,72},{... | collective-permute-start | bytes 491528 | tf_op jit(solution)/shard_map/ppermute | solution.py:279
  45.4 9.4 %collective-permute-start.12 = (f32[320,128]{1,0:T(8,128)S(1)}, f32[320,128]{1,0:T(8,128)S(1)}, u32[]{:S(2)}, u32[]{:S(2)}) collective-permute-start(f32[320,128]{1,0:T(8,128)S(1)} %shard_map.46.field), channel_id=1, source_target_pairs={{0,8},{8,0},{16,24},{24,16},{32,40},{40,32},{48,56},{56,48},{1,9},... | collective-permute-start | bytes 491528 | tf_op jit(solution)/shard_map/ppermute | solution.py:270
  55.6 6.9 %collective-permute-start.15 = (f32[256,128]{1,0:T(8,128)S(1)}, f32[256,128]{1,0:T(8,128)S(1)}, u32[]{:S(2)}, u32[]{:S(2)}) collective-permute-start(f32[256,128]{1,0:T(8,128)S(1)} %get-tuple-element.14.field), channel_id=1, source_target_pairs={{64,0},{128,64},{192,128},{256,192},{320,256},{384,320},{448,384},... | collective-permute-start | bytes 393224 | tf_op jit(solution)/shard_map/ppermute | solution.py:289
  56.9 5.6 %collective-permute-start.14 = (f32[256,128]{1,0:T(8,128)S(1)}, f32[256,128]{1,0:T(8,128)S(1)}, u32[]{:S(2)}, u32[]{:S(2)}) collective-permute-start(f32[256,128]{1,0:T(8,128)S(1)} %get-tuple-element.14.field), channel_id=1, source_target_pairs={{8,0},{16,8},{24,16},{32,24},{40,32},{48,40},{56,48},{9,1},{17,9},... | collective-permute-start | bytes 393224 | tf_op jit(solution)/shard_map/ppermute | solution.py:293
  63.4 5.4 %collective-permute-start.16 = (f32[4,128]{1,0:T(4,128)S(1)}, f32[4,128]{1,0:T(4,128)S(1)}, u32[]{:S(2)}, u32[]{:S(2)}) collective-permute-start(f32[4,128]{1,0:T(4,128)S(1)} %shard_map.50), channel_id=1, source_target_pairs={{0,8},{8,0},{16,24},{24,16},{32,40},{40,32},{48,56},{56,48},{1,9},... | collective-permute-start | bytes 6152 | tf_op jit(solution)/shard_map/ppermute | solution.py:299

commit v7 on v3

--- a/solution.py
+++ b/solution.py
@@ -288,12 +288,12 @@
 def sum_everywhere(value):
     if all(lax.axis_size(axis) == 8 for axis in ("gx", "gy", "gz")):
         fours = [[0, 1, 2, 3], [4, 5, 6, 7]]
-        value = value + lax.ppermute(value, "gy", [(i, i ^ 1) for i in range(8)])
         value = lax.psum(value, "gy", axis_index_groups=[[0, 2, 4, 6], [1, 3, 5, 7]])
         value = lax.psum(value, "gz", axis_index_groups=fours)
         value = lax.psum(value, "gx", axis_index_groups=fours)
         rings = [[8 * gx + gz, 8 * gx + 32 + gz, 8 * gx + gz + 4, 8 * gx + 32 + gz + 4] for gx in range(4) for gz in range(4)]
-        return lax.psum(value, ("gx", "gz"), axis_index_groups=rings)
+        value = lax.psum(value, ("gx", "gz"), axis_index_groups=rings)
+        return value + lax.ppermute(value, "gy", [(i, i ^ 1) for i in range(8)])
     return lax.psum(value, ("gx", "gy", "gz"))
 
 

time: 127 us -> 128 us (level)
  the two profiles are of different devices: /device:TPU:2 before, /device:TPU:1 now
where the time goes in v7:
time: 128 us; the launch traced here: 127 us
  starting transfers between devices  57.2 us (45%)
  blocking collectives  47.4 us (37%)
  Pallas kernels  12.9 us (10%)
  waiting for transfers between devices  7.22 us (6%)
  local copies, waits for them, and re-layouts  1.59 us (1%)
    ppermute x8, starting transfers between devices, swap(): return lax.ppermute(value, axis, pairs)  34.7 us
    psum x1, blocking collectives, sum_everywhere(): value = lax.psum(value, 'gz', axis_index_groups=fours)  16.5 us
    pallas_call x11, Pallas kernels, run(): pl.pallas_call(kernel, out_shape=[jax.ShapeDtypeStruct(shape, jnp.float32...  12.9 us
    psum x1, blocking collectives, sum_everywhere(): value = lax.psum(value, ('gx', 'gz'), axis_index_groups=rings)  11.5 us
    ppermute x1, starting transfers between devices, sum_everywhere(): return value + lax.ppermute(value, 'gy', [(i, i ^ 1) for i in range(8)])  9.86 us
    psum x1, blocking collectives, sum_everywhere(): value = lax.psum(value, 'gx', axis_index_groups=fours)  9.86 us
    psum x1, blocking collectives, sum_everywhere(): lax.psum(value, 'gy', axis_index_groups=[[0, 2, 4, 6], [1, 3, 5, 7]])  9.51 us
    ppermute x6, starting transfers between devices, swap_x(): return lax.ppermute(value, ('gx', 'gy'), pairs)  7.98 us
  transfers between devices with their start and end apart: 17, of which 6 were waited for; matrix products, arithmetic and copies ran while one was open for 0% of the time, Pallas kernels for 4%

profile of v7, /device:TPU:1, one launch (start us, length us, event | category | flops | bytes accessed | tf_op | source)
XLA Modules:
  0.0 127.3 jit_solution(7487885049555094148)
XLA Ops:
  1.4 0.9 copy-done
  2.3 0.7 shard_map.41
  3.6 6.4 %collective-permute-start.1 = (f32[40,128]{1,0:T(8,128)S(1)}, f32[40,128]{1,0:T(8,128)S(1)}, u32[]{:S(2)}, u32[]{:S(2)}) collective-permute-start(f32[40,128]{1,0:T(8,128)S(1)} %get-tuple-element.11), channel_id=1, source_target_pairs={{0,1},{1,0},{2,3},{3,2},{4,5},{5,4},{6,7},{7,6},{8,9},{9,8},{10,11... | collective-permute-start | bytes 61448 | tf_op jit(solution)/shard_map/ppermute | solution.py:262
  10.1 1.1 collective-permute-done.1.first
  11.2 0.8 shard_map.42
  12.7 8.1 %collective-permute-start.2 = (f32[320,128]{1,0:T(8,128)S(1)}, f32[320,128]{1,0:T(8,128)S(1)}, u32[]{:S(2)}, u32[]{:S(2)}) collective-permute-start(f32[320,128]{1,0:T(8,128)S(1)} %get-tuple-element.13.field.rest_0_), channel_id=1, source_target_pairs={{8,16},{16,8},{24,32},{32,24},{40,48},{48,40},{9,17},{17,9},{25,33... | collective-permute-start | bytes 491528 | tf_op jit(solution)/shard_map/ppermute | solution.py:262
  20.8 1.9 %collective-permute-start.5 = (f32[320,128]{1,0:T(8,128)S(1)}, f32[320,128]{1,0:T(8,128)S(1)}, u32[]{:S(2)}, u32[]{:S(2)}) collective-permute-start(f32[320,128]{1,0:T(8,128)S(1)} %get-tuple-element.13.field.rest_0_), channel_id=1, source_target_pairs={{64,128},{128,64},{192,256},{256,192},{320,384},{384,320},{8,72},{... | collective-permute-start | bytes 491528 | tf_op jit(solution)/shard_map/ppermute | solution.py:271
  22.7 1.9 %collective-permute-start.4 = (f32[320,128]{1,0:T(8,128)S(1)}, f32[320,128]{1,0:T(8,128)S(1)}, u32[]{:S(2)}, u32[]{:S(2)}) collective-permute-start(f32[320,128]{1,0:T(8,128)S(1)} %get-tuple-element.13.field.rest_0_), channel_id=1, source_target_pairs={{0,8},{8,0},{16,24},{24,16},{32,40},{40,32},{48,56},{56,48},{1,9},... | collective-permute-start | bytes 491528 | tf_op jit(solution)/shard_map/ppermute | solution.py:262
  24.7 1.5 %shard_map.43.part = f32[256,128]{1,0:T(8,128)S(1)} custom-call(s32[5]{0:T(128)S(1)} %stack.31.flags, f32[16,128]{1,0:T(8,128)S(1)} %bitcast.11, f32[320,128]{1,0:T(8,128)S(1)} %get-tuple-element.13.field.rest_0_, f32[320,128]{1,0:T(8,128)S(1)} %collective-permute-done.2.rest_0_.y2, f32[320,128]{1,0:T(8,128)S(1)} %collective-permute-done.3.rest_1_.x1), custom_call_target="tpu_custom_call" | custom-call | tf_op jit(solution)/shard_map/pallas_call | solution.py:305
  26.8 0.8 shard_map.44.field.rest_0_
  28.3 6.3 %collective-permute-start.6 = (f32[320,128]{1,0:T(8,128)S(1)}, f32[320,128]{1,0:T(8,128)S(1)}, u32[]{:S(2)}, u32[]{:S(2)}) collective-permute-start(f32[320,128]{1,0:T(8,128)S(1)} %shard_map.44.field.rest_0_), channel_id=1, source_target_pairs={{8,16},{16,8},{24,32},{32,24},{40,48},{48,40},{9,17},{17,9},{25,33... | collective-permute-start | bytes 491528 | tf_op jit(solution)/shard_map/ppermute | solution.py:262
  34.7 2.0 %collective-permute-start.9 = (f32[320,128]{1,0:T(8,128)S(1)}, f32[320,128]{1,0:T(8,128)S(1)}, u32[]{:S(2)}, u32[]{:S(2)}) collective-permute-start(f32[320,128]{1,0:T(8,128)S(1)} %shard_map.44.field.rest_0_), channel_id=1, source_target_pairs={{64,128},{128,64},{192,256},{256,192},{320,384},{384,320},{8,72},{... | collective-permute-start | bytes 491528 | tf_op jit(solution)/shard_map/ppermute | solution.py:271
  36.7 1.9 %collective-permute-start.8 = (f32[320,128]{1,0:T(8,128)S(1)}, f32[320,128]{1,0:T(8,128)S(1)}, u32[]{:S(2)}, u32[]{:S(2)}) collective-permute-start(f32[320,128]{1,0:T(8,128)S(1)} %shard_map.44.field.rest_0_), channel_id=1, source_target_pairs={{0,8},{8,0},{16,24},{24,16},{32,40},{40,32},{48,56},{56,48},{1,9},... | collective-permute-start | bytes 491528 | tf_op jit(solution)/shard_map/ppermute | solution.py:262
  38.6 1.5 %shard_map.45.part = f32[256,128]{1,0:T(8,128)S(1)} custom-call(s32[5]{0:T(128)S(1)} %stack.31.flags, f32[16,128]{1,0:T(8,128)S(1)} %bitcast.12, f32[320,128]{1,0:T(8,128)S(1)} %shard_map.44.field.rest_0_, f32[320,128]{1,0:T(8,128)S(1)} %get-tuple-element.13.field.rest_0_, f32[320,128]{1,0:T(8,128)S(1)} %collective-permute-done.6.rest_1_.y2, ...), custom_call_target="tpu_custom_call" | custom-call | tf_op jit(solution)/shard_map/pallas_call | solution.py:305
  40.7 0.8 shard_map.46.field
  42.2 7.5 %collective-permute-start.10 = (f32[320,128]{1,0:T(8,128)S(1)}, f32[320,128]{1,0:T(8,128)S(1)}, u32[]{:S(2)}, u32[]{:S(2)}) collective-permute-start(f32[320,128]{1,0:T(8,128)S(1)} %shard_map.46.field), channel_id=1, source_target_pairs={{8,16},{16,8},{24,32},{32,24},{40,48},{48,40},{9,17},{17,9},{25,33... | collective-permute-start | bytes 491528 | tf_op jit(solution)/shard_map/ppermute | solution.py:262
  49.8 2.0 %collective-permute-start.13 = (f32[320,128]{1,0:T(8,128)S(1)}, f32[320,128]{1,0:T(8,128)S(1)}, u32[]{:S(2)}, u32[]{:S(2)}) collective-permute-start(f32[320,128]{1,0:T(8,128)S(1)} %shard_map.46.field), channel_id=1, source_target_pairs={{64,128},{128,64},{192,256},{256,192},{320,384},{384,320},{8,72},{... | collective-permute-start | bytes 491528 | tf_op jit(solution)/shard_map/ppermute | solution.py:271
  51.8 1.9 %collective-permute-start.12 = (f32[320,128]{1,0:T(8,128)S(1)}, f32[320,128]{1,0:T(8,128)S(1)}, u32[]{:S(2)}, u32[]{:S(2)}) collective-permute-start(f32[320,128]{1,0:T(8,128)S(1)} %shard_map.46.field), channel_id=1, source_target_pairs={{0,8},{8,0},{16,24},{24,16},{32,40},{40,32},{48,56},{56,48},{1,9},... | collective-permute-start | bytes 491528 | tf_op jit(solution)/shard_map/ppermute | solution.py:262
  53.7 1.5 %shard_map.47.part = f32[256,128]{1,0:T(8,128)S(1)} custom-call(s32[5]{0:T(128)S(1)} %stack.31.flags, f32[16,128]{1,0:T(8,128)S(1)} %bitcast.13, f32[320,128]{1,0:T(8,128)S(1)} %shard_map.46.field, f32[320,128]{1,0:T(8,128)S(1)} %shard_map.44.field.rest_0_, f32[320,128]{1,0:T(8,128)S(1)} %collective-permute-done.10.rest_1_.y2, ...), custom_call_target="tpu_custom_call" | custom-call | tf_op jit(solution)/shard_map/pallas_call | solution.py:305
  55.8 0.8 shard_map.48
  56.7 2.7 %collective-permute-start.15 = (f32[256,128]{1,0:T(8,128)S(1)}, f32[256,128]{1,0:T(8,128)S(1)}, u32[]{:S(2)}, u32[]{:S(2)}) collective-permute-start(f32[256,128]{1,0:T(8,128)S(1)} %get-tuple-element.14.field), channel_id=1, source_target_pairs={{64,0},{128,64},{192,128},{256,192},{320,256},{384,320},{448,384},... | collective-permute-start | bytes 393224 | tf_op jit(solution)/shard_map/ppermute | solution.py:281
  59.4 1.9 %collective-permute-start.14 = (f32[256,128]{1,0:T(8,128)S(1)}, f32[256,128]{1,0:T(8,128)S(1)}, u32[]{:S(2)}, u32[]{:S(2)}) collective-permute-start(f32[256,128]{1,0:T(8,128)S(1)} %get-tuple-element.14.field), channel_id=1, source_target_pairs={{8,0},{16,8},{24,16},{32,24},{40,32},{48,40},{56,48},{9,1},{17,9},... | collective-permute-start | bytes 393224 | tf_op jit(solution)/shard_map/ppermute | solution.py:285
  61.3 0.9 shard_map.49.part
  62.2 3.4 %collective-permute-done.14.after_y = f32[256,128]{1,0:T(8,128)S(1)} collective-permute-done((f32[256,128]{1,0:T(8,128)S(1)}, f32[256,128]{1,0:T(8,128)S(1)}, u32[]{:S(2)}, u32[]{:S(2)}) %collective-permute-start.14) | collective-permute-done | bytes 131104 | tf_op jit(solution)/shard_map/ppermute | solution.py:285
  65.7 1.0 shard_map.50
  66.6 9.5 %psum.28 = f32[4,128]{1,0:T(4,128)S(1)} all-reduce(f32[4,128]{1,0:T(4,128)S(1)} %shard_map.50), channel_id=1, replica_groups={{0,16,32,48},{8,24,40,56},{1,17,33,49},{9,25,41,57},{2,18,34,50},{10,26..., use_global_device_ids=true, to_apply=%region_0.1 | all-reduce | flops 512 | bytes 4096 | tf_op jit(solution)/shard_map/psum | solution.py:291
  76.1 16.5 %psum.29 = f32[4,128]{1,0:T(4,128)S(1)} all-reduce(f32[4,128]{1,0:T(4,128)S(1)} %psum.28), channel_id=1, replica_groups={{0,1,2,3},{4,5,6,7},{8,9,10,11},{12,13,14,15},{16,17,18,19},{20,21,22,2..., use_global_device_ids=true, to_apply=%region_1.2 | all-reduce | flops 512 | bytes 4096 | tf_op jit(solution)/shard_map/psum | solution.py:292
  92.6 9.9 %psum.30 = f32[4,128]{1,0:T(4,128)S(1)} all-reduce(f32[4,128]{1,0:T(4,128)S(1)} %psum.29), channel_id=1, replica_groups={{0,64,128,192},{256,320,384,448},{1,65,129,193},{257,321,385,449},{2,66..., use_global_device_ids=true, to_apply=%region_2.3 | all-reduce | flops 512 | bytes 4096 | tf_op jit(solution)/shard_map/psum | solution.py:293
  102.5 11.5 %psum.31 = f32[4,128]{1,0:T(4,128)S(1)} all-reduce(f32[4,128]{1,0:T(4,128)S(1)} %psum.30), channel_id=1, replica_groups={{0,256,4,260},{1,257,5,261},{2,258,6,262},{3,259,7,263},{64,320,68,324}..., use_global_device_ids=true, to_apply=%region_3.4 | all-reduce | flops 512 | bytes 4096 | tf_op jit(solution)/shard_map/psum | solution.py:295
  114.0 9.9 %collective-permute-start.16 = (f32[4,128]{1,0:T(4,128)S(1)}, f32[4,128]{1,0:T(4,128)S(1)}, u32[]{:S(2)}, u32[]{:S(2)}) collective-permute-start(f32[4,128]{1,0:T(4,128)S(1)} %psum.31), channel_id=1, source_target_pairs={{0,8},{8,0},{16,24},{24,16},{32,40},{40,32},{48,56},{56,48},{1,9},... | collective-permute-start | bytes 6152 | tf_op jit(solution)/shard_map/ppermute | solution.py:296
  123.9 0.8 collective-permute-done.16
  124.7 2.6 %shard_map.51 = (f32[256,128]{1,0:T(8,128)}, f32[16,16]{1,0:T(8,128)}) custom-call(f32[4,128]{1,0:T(4,128)S(1)} %add.28.sums, f32[256,128]{1,0:T(8,128)S(1)} %get-tuple-element.14.field), custom_call_target="tpu_custom_call" | custom-call | tf_op jit(solution)/shard_map/pallas_call | solution.py:305
  (23 shorter events, 5.2 us)
Async XLA Ops:
  0.7 0.7 copy-start.1
  1.4 0.9 copy-start
  3.0 7.1 %collective-permute-start = (f32[40,128]{1,0:T(8,128)S(1)}, f32[40,128]{1,0:T(8,128)S(1)}, u32[]{:S(2)}, u32[]{:S(2)}) collective-permute-start(f32[40,128]{1,0:T(8,128)S(1)} %get-tuple-element.10), channel_id=1, source_target_pairs={{1,2},{2,1},{3,4},{4,3},{5,6},{6,5},{9,10},{10,9},{11,12},{12,11},... | collective-permute-start | bytes 61448 | tf_op jit(solution)/shard_map/ppermute | solution.py:262
  3.6 7.6 %collective-permute-start.1 = (f32[40,128]{1,0:T(8,128)S(1)}, f32[40,128]{1,0:T(8,128)S(1)}, u32[]{:S(2)}, u32[]{:S(2)}) collective-permute-start(f32[40,128]{1,0:T(8,128)S(1)} %get-tuple-element.11), channel_id=1, source_target_pairs={{0,1},{1,0},{2,3},{3,2},{4,5},{5,4},{6,7},{7,6},{8,9},{9,8},{10,11... | collective-permute-start | bytes 61448 | tf_op jit(solution)/shard_map/ppermute | solution.py:262
  12.0 12.6 %collective-permute-start.3 = (f32[320,128]{1,0:T(8,128)S(1)}, f32[320,128]{1,0:T(8,128)S(1)}, u32[]{:S(2)}, u32[]{:S(2)}) collective-permute-start(f32[320,128]{1,0:T(8,128)S(1)} %get-tuple-element.13.field.rest_0_), channel_id=1, source_target_pairs={{0,64},{64,0},{128,192},{192,128},{256,320},{320,256},{384,448},{4... | collective-permute-start | bytes 491528 | tf_op jit(solution)/shard_map/ppermute | solution.py:271
  12.7 11.9 %collective-permute-start.2 = (f32[320,128]{1,0:T(8,128)S(1)}, f32[320,128]{1,0:T(8,128)S(1)}, u32[]{:S(2)}, u32[]{:S(2)}) collective-permute-start(f32[320,128]{1,0:T(8,128)S(1)} %get-tuple-element.13.field.rest_0_), channel_id=1, source_target_pairs={{8,16},{16,8},{24,32},{32,24},{40,48},{48,40},{9,17},{17,9},{25,33... | collective-permute-start | bytes 491528 | tf_op jit(solution)/shard_map/ppermute | solution.py:262
  20.8 6.1 %collective-permute-start.5 = (f32[320,128]{1,0:T(8,128)S(1)}, f32[320,128]{1,0:T(8,128)S(1)}, u32[]{:S(2)}, u32[]{:S(2)}) collective-permute-start(f32[320,128]{1,0:T(8,128)S(1)} %get-tuple-element.13.field.rest_0_), channel_id=1, source_target_pairs={{64,128},{128,64},{192,256},{256,192},{320,384},{384,320},{8,72},{... | collective-permute-start | bytes 491528 | tf_op jit(solution)/shard_map/ppermute | solution.py:271
  22.7 4.1 %collective-permute-start.4 = (f32[320,128]{1,0:T(8,128)S(1)}, f32[320,128]{1,0:T(8,128)S(1)}, u32[]{:S(2)}, u32[]{:S(2)}) collective-permute-start(f32[320,128]{1,0:T(8,128)S(1)} %get-tuple-element.13.field.rest_0_), channel_id=1, source_target_pairs={{0,8},{8,0},{16,24},{24,16},{32,40},{40,32},{48,56},{56,48},{1,9},... | collective-permute-start | bytes 491528 | tf_op jit(solution)/shard_map/ppermute | solution.py:262
  27.7 11.0 %collective-permute-start.7 = (f32[320,128]{1,0:T(8,128)S(1)}, f32[320,128]{1,0:T(8,128)S(1)}, u32[]{:S(2)}, u32[]{:S(2)}) collective-permute-start(f32[320,128]{1,0:T(8,128)S(1)} %shard_map.44.field.rest_0_), channel_id=1, source_target_pairs={{0,64},{64,0},{128,192},{192,128},{256,320},{320,256},{384,448},{4... | collective-permute-start | bytes 491528 | tf_op jit(solution)/shard_map/ppermute | solution.py:271
  28.3 10.3 %collective-permute-start.6 = (f32[320,128]{1,0:T(8,128)S(1)}, f32[320,128]{1,0:T(8,128)S(1)}, u32[]{:S(2)}, u32[]{:S(2)}) collective-permute-start(f32[320,128]{1,0:T(8,128)S(1)} %shard_map.44.field.rest_0_), channel_id=1, source_target_pairs={{8,16},{16,8},{24,32},{32,24},{40,48},{48,40},{9,17},{17,9},{25,33... | collective-permute-start | bytes 491528 | tf_op jit(solution)/shard_map/ppermute | solution.py:262
  34.7 6.1 %collective-permute-start.9 = (f32[320,128]{1,0:T(8,128)S(1)}, f32[320,128]{1,0:T(8,128)S(1)}, u32[]{:S(2)}, u32[]{:S(2)}) collective-permute-start(f32[320,128]{1,0:T(8,128)S(1)} %shard_map.44.field.rest_0_), channel_id=1, source_target_pairs={{64,128},{128,64},{192,256},{256,192},{320,384},{384,320},{8,72},{... | collective-permute-start | bytes 491528 | tf_op jit(solution)/shard_map/ppermute | solution.py:271
  36.7 4.0 %collective-permute-start.8 = (f32[320,128]{1,0:T(8,128)S(1)}, f32[320,128]{1,0:T(8,128)S(1)}, u32[]{:S(2)}, u32[]{:S(2)}) collective-permute-start(f32[320,128]{1,0:T(8,128)S(1)} %shard_map.44.field.rest_0_), channel_id=1, source_target_pairs={{0,8},{8,0},{16,24},{24,16},{32,40},{40,32},{48,56},{56,48},{1,9},... | collective-permute-start | bytes 491528 | tf_op jit(solution)/shard_map/ppermute | solution.py:262
  41.5 12.2 %collective-permute-start.11 = (f32[320,128]{1,0:T(8,128)S(1)}, f32[320,128]{1,0:T(8,128)S(1)}, u32[]{:S(2)}, u32[]{:S(2)}) collective-permute-start(f32[320,128]{1,0:T(8,128)S(1)} %shard_map.46.field), channel_id=1, source_target_pairs={{0,64},{64,0},{128,192},{192,128},{256,320},{320,256},{384,448},{4... | collective-permute-start | bytes 491528 | tf_op jit(solution)/shard_map/ppermute | solution.py:271
  42.2 11.5 %collective-permute-start.10 = (f32[320,128]{1,0:T(8,128)S(1)}, f32[320,128]{1,0:T(8,128)S(1)}, u32[]{:S(2)}, u32[]{:S(2)}) collective-permute-start(f32[320,128]{1,0:T(8,128)S(1)} %shard_map.46.field), channel_id=1, source_target_pairs={{8,16},{16,8},{24,32},{32,24},{40,48},{48,40},{9,17},{17,9},{25,33... | collective-permute-start | bytes 491528 | tf_op jit(solution)/shard_map/ppermute | solution.py:262
  49.8 6.1 %collective-permute-start.13 = (f32[320,128]{1,0:T(8,128)S(1)}, f32[320,128]{1,0:T(8,128)S(1)}, u32[]{:S(2)}, u32[]{:S(2)}) collective-permute-start(f32[320,128]{1,0:T(8,128)S(1)} %shard_map.46.field), channel_id=1, source_target_pairs={{64,128},{128,64},{192,256},{256,192},{320,384},{384,320},{8,72},{... | collective-permute-start | bytes 491528 | tf_op jit(solution)/shard_map/ppermute | solution.py:271
  51.8 4.0 %collective-permute-start.12 = (f32[320,128]{1,0:T(8,128)S(1)}, f32[320,128]{1,0:T(8,128)S(1)}, u32[]{:S(2)}, u32[]{:S(2)}) collective-permute-start(f32[320,128]{1,0:T(8,128)S(1)} %shard_map.46.field), channel_id=1, source_target_pairs={{0,8},{8,0},{16,24},{24,16},{32,40},{40,32},{48,56},{56,48},{1,9},... | collective-permute-start | bytes 491528 | tf_op jit(solution)/shard_map/ppermute | solution.py:262
  56.7 5.6 %collective-permute-start.15 = (f32[256,128]{1,0:T(8,128)S(1)}, f32[256,128]{1,0:T(8,128)S(1)}, u32[]{:S(2)}, u32[]{:S(2)}) collective-permute-start(f32[256,128]{1,0:T(8,128)S(1)} %get-tuple-element.14.field), channel_id=1, source_target_pairs={{64,0},{128,64},{192,128},{256,192},{320,256},{384,320},{448,384},... | collective-permute-start | bytes 393224 | tf_op jit(solution)/shard_map/ppermute | solution.py:281
  59.4 6.3 %collective-permute-start.14 = (f32[256,128]{1,0:T(8,128)S(1)}, f32[256,128]{1,0:T(8,128)S(1)}, u32[]{:S(2)}, u32[]{:S(2)}) collective-permute-start(f32[256,128]{1,0:T(8,128)S(1)} %get-tuple-element.14.field), channel_id=1, source_target_pairs={{8,0},{16,8},{24,16},{32,24},{40,32},{48,40},{56,48},{9,1},{17,9},... | collective-permute-start | bytes 393224 | tf_op jit(solution)/shard_map/ppermute | solution.py:285
  114.0 10.7 %collective-permute-start.16 = (f32[4,128]{1,0:T(4,128)S(1)}, f32[4,128]{1,0:T(4,128)S(1)}, u32[]{:S(2)}, u32[]{:S(2)}) collective-permute-start(f32[4,128]{1,0:T(4,128)S(1)} %psum.31), channel_id=1, source_target_pairs={{0,8},{8,0},{16,24},{24,16},{32,40},{40,32},{48,56},{56,48},{1,9},... | collective-permute-start | bytes 6152 | tf_op jit(solution)/shard_map/ppermute | solution.py:296

commit v8 on v3

--- a/solution.py
+++ b/solution.py
@@ -289,11 +289,11 @@
     if all(lax.axis_size(axis) == 8 for axis in ("gx", "gy", "gz")):
         fours = [[0, 1, 2, 3], [4, 5, 6, 7]]
         value = value + lax.ppermute(value, "gy", [(i, i ^ 1) for i in range(8)])
-        value = lax.psum(value, "gy", axis_index_groups=[[0, 2, 4, 6], [1, 3, 5, 7]])
+        rings = [[8 * gx + gz, 8 * gx + 32 + gz, 8 * gx + gz + 4, 8 * gx + 32 + gz + 4] for gx in range(4) for gz in range(4)]
+        value = lax.psum(value, ("gx", "gz"), axis_index_groups=rings)
         value = lax.psum(value, "gz", axis_index_groups=fours)
         value = lax.psum(value, "gx", axis_index_groups=fours)
-        rings = [[8 * gx + gz, 8 * gx + 32 + gz, 8 * gx + gz + 4, 8 * gx + 32 + gz + 4] for gx in range(4) for gz in range(4)]
-        return lax.psum(value, ("gx", "gz"), axis_index_groups=rings)
+        return lax.psum(value, "gy", axis_index_groups=[[0, 2, 4, 6], [1, 3, 5, 7]])
     return lax.psum(value, ("gx", "gy", "gz"))
 
 

time: 127 us -> 127 us (level)
    psum x2, blocking collectives: 27.6 us -> 32 us  [the longest x1 22.7 us: sum_everywhere(): value = lax.psum(value, ('gx', 'gz'), axis_index_groups=rings)]
    psum x1, blocking collectives: 12.2 us -> 9.33 us  [sum_everywhere(): value = lax.psum(value, 'gx', axis_index_groups=fours)]
    psum x1, blocking collectives: 15.3 us -> 13.9 us  [sum_everywhere(): value = lax.psum(value, 'gz', axis_index_groups=fours)]
where the time goes in v8:
time: 127 us
  blocking collectives  55.2 us (43%)
  starting transfers between devices  50.1 us (39%)
  Pallas kernels  12.9 us (10%)
  waiting for transfers between devices  5.89 us (5%)
  local copies, waits for them, and re-layouts  1.59 us (1%)
    ppermute x8, starting transfers between devices, swap(): return lax.ppermute(value, axis, pairs)  31 us
    psum x1, blocking collectives, sum_everywhere(): value = lax.psum(value, ('gx', 'gz'), axis_index_groups=rings)  22.7 us
    psum x1, blocking collectives, sum_everywhere(): value = lax.psum(value, 'gz', axis_index_groups=fours)  13.9 us
    pallas_call x11, Pallas kernels, run(): pl.pallas_call(kernel, out_shape=[jax.ShapeDtypeStruct(shape, jnp.float32...  12.9 us
    ppermute x6, starting transfers between devices, swap_x(): return lax.ppermute(value, ('gx', 'gy'), pairs)  11.9 us
    psum x1, blocking collectives, sum_everywhere(): value = lax.psum(value, 'gx', axis_index_groups=fours)  9.33 us
    psum x1, blocking collectives, sum_everywhere(): return lax.psum(value, 'gy', axis_index_groups=[[0, 2, 4, 6], [1, 3, 5, 7]])  9.32 us
    ppermute x1, starting transfers between devices, sum_everywhere(): value = value + lax.ppermute(value, 'gy', [(i, i ^ 1) for i in range(8)])  4.61 us
  transfers between devices with their start and end apart: 17, of which 3 were waited for; matrix products, arithmetic and copies ran while one was open for 0% of the time, Pallas kernels for 4%

profile of v8, /device:TPU:2, one launch (start us, length us, event | category | flops | bytes accessed | tf_op | source)
XLA Modules:
  0.0 126.6 jit_solution(13844506953156698701)
XLA Ops:
  1.4 0.9 copy-done
  2.3 0.7 shard_map.41
  3.0 3.4 %collective-permute-start = (f32[40,128]{1,0:T(8,128)S(1)}, f32[40,128]{1,0:T(8,128)S(1)}, u32[]{:S(2)}, u32[]{:S(2)}) collective-permute-start(f32[40,128]{1,0:T(8,128)S(1)} %get-tuple-element.10), channel_id=1, source_target_pairs={{1,2},{2,1},{3,4},{4,3},{5,6},{6,5},{9,10},{10,9},{11,12},{12,11},... | collective-permute-start | bytes 61448 | tf_op jit(solution)/shard_map/ppermute | solution.py:262
  6.4 5.1 %collective-permute-start.1 = (f32[40,128]{1,0:T(8,128)S(1)}, f32[40,128]{1,0:T(8,128)S(1)}, u32[]{:S(2)}, u32[]{:S(2)}) collective-permute-start(f32[40,128]{1,0:T(8,128)S(1)} %get-tuple-element.11), channel_id=1, source_target_pairs={{0,1},{1,0},{2,3},{3,2},{4,5},{5,4},{6,7},{7,6},{8,9},{9,8},{10,11... | collective-permute-start | bytes 61448 | tf_op jit(solution)/shard_map/ppermute | solution.py:262
  11.5 1.7 %collective-permute-done.1.first = f32[40,128]{1,0:T(8,128)S(1)} collective-permute-done((f32[40,128]{1,0:T(8,128)S(1)}, f32[40,128]{1,0:T(8,128)S(1)}, u32[]{:S(2)}, u32[]{:S(2)}) %collective-permute-start.1) | collective-permute-done | bytes 20512 | tf_op jit(solution)/shard_map/ppermute | solution.py:262
  13.2 0.8 shard_map.42
  14.0 2.7 %collective-permute-start.3 = (f32[320,128]{1,0:T(8,128)S(1)}, f32[320,128]{1,0:T(8,128)S(1)}, u32[]{:S(2)}, u32[]{:S(2)}) collective-permute-start(f32[320,128]{1,0:T(8,128)S(1)} %get-tuple-element.13.field.rest_0_), channel_id=1, source_target_pairs={{0,64},{64,0},{128,192},{192,128},{256,320},{320,256},{384,448},{4... | collective-permute-start | bytes 491528 | tf_op jit(solution)/shard_map/ppermute | solution.py:271
  16.7 0.7 collective-permute-start.2
  17.4 0.7 collective-permute-start.5
  18.1 6.1 %collective-permute-start.4 = (f32[320,128]{1,0:T(8,128)S(1)}, f32[320,128]{1,0:T(8,128)S(1)}, u32[]{:S(2)}, u32[]{:S(2)}) collective-permute-start(f32[320,128]{1,0:T(8,128)S(1)} %get-tuple-element.13.field.rest_0_), channel_id=1, source_target_pairs={{0,8},{8,0},{16,24},{24,16},{32,40},{40,32},{48,56},{56,48},{1,9},... | collective-permute-start | bytes 491528 | tf_op jit(solution)/shard_map/ppermute | solution.py:262
  24.2 1.5 %shard_map.43.part = f32[256,128]{1,0:T(8,128)S(1)} custom-call(s32[5]{0:T(128)S(1)} %stack.31.flags, f32[16,128]{1,0:T(8,128)S(1)} %bitcast.11, f32[320,128]{1,0:T(8,128)S(1)} %get-tuple-element.13.field.rest_0_, f32[320,128]{1,0:T(8,128)S(1)} %collective-permute-done.2.rest_0_.y2, f32[320,128]{1,0:T(8,128)S(1)} %collective-permute-done.3.rest_1_.x1), custom_call_target="tpu_custom_call" | custom-call | tf_op jit(solution)/shard_map/pallas_call | solution.py:305
  25.7 0.8 shard_map.44.field.rest_0_
  26.5 3.6 %collective-permute-start.7 = (f32[320,128]{1,0:T(8,128)S(1)}, f32[320,128]{1,0:T(8,128)S(1)}, u32[]{:S(2)}, u32[]{:S(2)}) collective-permute-start(f32[320,128]{1,0:T(8,128)S(1)} %shard_map.44.field.rest_0_), channel_id=1, source_target_pairs={{0,64},{64,0},{128,192},{192,128},{256,320},{320,256},{384,448},{4... | collective-permute-start | bytes 491528 | tf_op jit(solution)/shard_map/ppermute | solution.py:271
  31.5 6.6 %collective-permute-start.8 = (f32[320,128]{1,0:T(8,128)S(1)}, f32[320,128]{1,0:T(8,128)S(1)}, u32[]{:S(2)}, u32[]{:S(2)}) collective-permute-start(f32[320,128]{1,0:T(8,128)S(1)} %shard_map.44.field.rest_0_), channel_id=1, source_target_pairs={{0,8},{8,0},{16,24},{24,16},{32,40},{40,32},{48,56},{56,48},{1,9},... | collective-permute-start | bytes 491528 | tf_op jit(solution)/shard_map/ppermute | solution.py:262
  38.2 1.5 %shard_map.45.part = f32[256,128]{1,0:T(8,128)S(1)} custom-call(s32[5]{0:T(128)S(1)} %stack.31.flags, f32[16,128]{1,0:T(8,128)S(1)} %bitcast.12, f32[320,128]{1,0:T(8,128)S(1)} %shard_map.44.field.rest_0_, f32[320,128]{1,0:T(8,128)S(1)} %get-tuple-element.13.field.rest_0_, f32[320,128]{1,0:T(8,128)S(1)} %collective-permute-done.6.rest_1_.y2, ...), custom_call_target="tpu_custom_call" | custom-call | tf_op jit(solution)/shard_map/pallas_call | solution.py:305
  39.7 0.8 shard_map.46.field
  40.5 3.5 %collective-permute-start.11 = (f32[320,128]{1,0:T(8,128)S(1)}, f32[320,128]{1,0:T(8,128)S(1)}, u32[]{:S(2)}, u32[]{:S(2)}) collective-permute-start(f32[320,128]{1,0:T(8,128)S(1)} %shard_map.46.field), channel_id=1, source_target_pairs={{0,64},{64,0},{128,192},{192,128},{256,320},{320,256},{384,448},{4... | collective-permute-start | bytes 491528 | tf_op jit(solution)/shard_map/ppermute | solution.py:271
  45.4 7.8 %collective-permute-start.12 = (f32[320,128]{1,0:T(8,128)S(1)}, f32[320,128]{1,0:T(8,128)S(1)}, u32[]{:S(2)}, u32[]{:S(2)}) collective-permute-start(f32[320,128]{1,0:T(8,128)S(1)} %shard_map.46.field), channel_id=1, source_target_pairs={{0,8},{8,0},{16,24},{24,16},{32,40},{40,32},{48,56},{56,48},{1,9},... | collective-permute-start | bytes 491528 | tf_op jit(solution)/shard_map/ppermute | solution.py:262
  53.3 1.5 %shard_map.47.part = f32[256,128]{1,0:T(8,128)S(1)} custom-call(s32[5]{0:T(128)S(1)} %stack.31.flags, f32[16,128]{1,0:T(8,128)S(1)} %bitcast.13, f32[320,128]{1,0:T(8,128)S(1)} %shard_map.46.field, f32[320,128]{1,0:T(8,128)S(1)} %shard_map.44.field.rest_0_, f32[320,128]{1,0:T(8,128)S(1)} %collective-permute-done.10.rest_1_.y2, ...), custom_call_target="tpu_custom_call" | custom-call | tf_op jit(solution)/shard_map/pallas_call | solution.py:305
  54.8 0.8 shard_map.48
  55.6 1.3 %collective-permute-start.15 = (f32[256,128]{1,0:T(8,128)S(1)}, f32[256,128]{1,0:T(8,128)S(1)}, u32[]{:S(2)}, u32[]{:S(2)}) collective-permute-start(f32[256,128]{1,0:T(8,128)S(1)} %get-tuple-element.14.field), channel_id=1, source_target_pairs={{64,0},{128,64},{192,128},{256,192},{320,256},{384,320},{448,384},... | collective-permute-start | bytes 393224 | tf_op jit(solution)/shard_map/ppermute | solution.py:281
  56.9 1.3 %collective-permute-start.14 = (f32[256,128]{1,0:T(8,128)S(1)}, f32[256,128]{1,0:T(8,128)S(1)}, u32[]{:S(2)}, u32[]{:S(2)}) collective-permute-start(f32[256,128]{1,0:T(8,128)S(1)} %get-tuple-element.14.field), channel_id=1, source_target_pairs={{8,0},{16,8},{24,16},{32,24},{40,32},{48,40},{56,48},{9,1},{17,9},... | collective-permute-start | bytes 393224 | tf_op jit(solution)/shard_map/ppermute | solution.py:285
  58.2 0.9 shard_map.49.part
  59.2 3.3 %collective-permute-done.15.beside_x = f32[256,128]{1,0:T(8,128)S(1)} collective-permute-done((f32[256,128]{1,0:T(8,128)S(1)}, f32[256,128]{1,0:T(8,128)S(1)}, u32[]{:S(2)}, u32[]{:S(2)}) %collective-permute-start.15) | collective-permute-done | bytes 131104 | tf_op jit(solution)/shard_map/ppermute | solution.py:281
  62.5 1.0 shard_map.50
  63.4 4.6 %collective-permute-start.16 = (f32[4,128]{1,0:T(4,128)S(1)}, f32[4,128]{1,0:T(4,128)S(1)}, u32[]{:S(2)}, u32[]{:S(2)}) collective-permute-start(f32[4,128]{1,0:T(4,128)S(1)} %shard_map.50), channel_id=1, source_target_pairs={{0,8},{8,0},{16,24},{24,16},{32,40},{40,32},{48,56},{56,48},{1,9},... | collective-permute-start | bytes 6152 | tf_op jit(solution)/shard_map/ppermute | solution.py:291
  68.1 0.8 collective-permute-done.16
  68.9 22.7 %psum.28 = f32[4,128]{1,0:T(4,128)S(1)} all-reduce(f32[4,128]{1,0:T(4,128)S(1)} %add.28), channel_id=1, replica_groups={{0,256,4,260},{1,257,5,261},{2,258,6,262},{3,259,7,263},{64,320,68,324}..., use_global_device_ids=true, to_apply=%region_0.1 | all-reduce | flops 512 | bytes 4096 | tf_op jit(solution)/shard_map/psum | solution.py:293
  91.5 13.9 %psum.29 = f32[4,128]{1,0:T(4,128)S(1)} all-reduce(f32[4,128]{1,0:T(4,128)S(1)} %psum.28), channel_id=1, replica_groups={{0,1,2,3},{4,5,6,7},{8,9,10,11},{12,13,14,15},{16,17,18,19},{20,21,22,2..., use_global_device_ids=true, to_apply=%region_1.2 | all-reduce | flops 512 | bytes 4096 | tf_op jit(solution)/shard_map/psum | solution.py:294
  105.4 9.3 %psum.30 = f32[4,128]{1,0:T(4,128)S(1)} all-reduce(f32[4,128]{1,0:T(4,128)S(1)} %psum.29), channel_id=1, replica_groups={{0,64,128,192},{256,320,384,448},{1,65,129,193},{257,321,385,449},{2,66..., use_global_device_ids=true, to_apply=%region_2.3 | all-reduce | flops 512 | bytes 4096 | tf_op jit(solution)/shard_map/psum | solution.py:295
  114.7 9.3 %psum.31.sums = f32[4,128]{1,0:T(4,128)S(1)} all-reduce(f32[4,128]{1,0:T(4,128)S(1)} %psum.30), channel_id=1, replica_groups={{0,16,32,48},{8,24,40,56},{1,17,33,49},{9,25,41,57},{2,18,34,50},{10,26..., use_global_device_ids=true, to_apply=%region_3.4 | all-reduce | flops 512 | bytes 4096 | tf_op jit(solution)/shard_map/psum | solution.py:296
  124.1 2.6 %shard_map.51 = (f32[256,128]{1,0:T(8,128)}, f32[16,16]{1,0:T(8,128)}) custom-call(f32[4,128]{1,0:T(4,128)S(1)} %psum.31.sums, f32[256,128]{1,0:T(8,128)S(1)} %get-tuple-element.14.field), custom_call_target="tpu_custom_call" | custom-call | tf_op jit(solution)/shard_map/pallas_call | solution.py:305
  (23 shorter events, 3.4 us)
Async XLA Ops:
  0.7 0.7 copy-start.1
  1.4 0.9 copy-start
  3.0 8.5 %collective-permute-start = (f32[40,128]{1,0:T(8,128)S(1)}, f32[40,128]{1,0:T(8,128)S(1)}, u32[]{:S(2)}, u32[]{:S(2)}) collective-permute-start(f32[40,128]{1,0:T(8,128)S(1)} %get-tuple-element.10), channel_id=1, source_target_pairs={{1,2},{2,1},{3,4},{4,3},{5,6},{6,5},{9,10},{10,9},{11,12},{12,11},... | collective-permute-start | bytes 61448 | tf_op jit(solution)/shard_map/ppermute | solution.py:262
  6.4 6.8 %collective-permute-start.1 = (f32[40,128]{1,0:T(8,128)S(1)}, f32[40,128]{1,0:T(8,128)S(1)}, u32[]{:S(2)}, u32[]{:S(2)}) collective-permute-start(f32[40,128]{1,0:T(8,128)S(1)} %get-tuple-element.11), channel_id=1, source_target_pairs={{0,1},{1,0},{2,3},{3,2},{4,5},{5,4},{6,7},{7,6},{8,9},{9,8},{10,11... | collective-permute-start | bytes 61448 | tf_op jit(solution)/shard_map/ppermute | solution.py:262
  14.0 10.1 %collective-permute-start.3 = (f32[320,128]{1,0:T(8,128)S(1)}, f32[320,128]{1,0:T(8,128)S(1)}, u32[]{:S(2)}, u32[]{:S(2)}) collective-permute-start(f32[320,128]{1,0:T(8,128)S(1)} %get-tuple-element.13.field.rest_0_), channel_id=1, source_target_pairs={{0,64},{64,0},{128,192},{192,128},{256,320},{320,256},{384,448},{4... | collective-permute-start | bytes 491528 | tf_op jit(solution)/shard_map/ppermute | solution.py:271
  16.7 7.5 %collective-permute-start.2 = (f32[320,128]{1,0:T(8,128)S(1)}, f32[320,128]{1,0:T(8,128)S(1)}, u32[]{:S(2)}, u32[]{:S(2)}) collective-permute-start(f32[320,128]{1,0:T(8,128)S(1)} %get-tuple-element.13.field.rest_0_), channel_id=1, source_target_pairs={{8,16},{16,8},{24,32},{32,24},{40,48},{48,40},{9,17},{17,9},{25,33... | collective-permute-start | bytes 491528 | tf_op jit(solution)/shard_map/ppermute | solution.py:262
  17.4 8.3 %collective-permute-start.5 = (f32[320,128]{1,0:T(8,128)S(1)}, f32[320,128]{1,0:T(8,128)S(1)}, u32[]{:S(2)}, u32[]{:S(2)}) collective-permute-start(f32[320,128]{1,0:T(8,128)S(1)} %get-tuple-element.13.field.rest_0_), channel_id=1, source_target_pairs={{64,128},{128,64},{192,256},{256,192},{320,384},{384,320},{8,72},{... | collective-permute-start | bytes 491528 | tf_op jit(solution)/shard_map/ppermute | solution.py:271
  18.1 7.6 %collective-permute-start.4 = (f32[320,128]{1,0:T(8,128)S(1)}, f32[320,128]{1,0:T(8,128)S(1)}, u32[]{:S(2)}, u32[]{:S(2)}) collective-permute-start(f32[320,128]{1,0:T(8,128)S(1)} %get-tuple-element.13.field.rest_0_), channel_id=1, source_target_pairs={{0,8},{8,0},{16,24},{24,16},{32,40},{40,32},{48,56},{56,48},{1,9},... | collective-permute-start | bytes 491528 | tf_op jit(solution)/shard_map/ppermute | solution.py:262
  26.5 11.6 %collective-permute-start.7 = (f32[320,128]{1,0:T(8,128)S(1)}, f32[320,128]{1,0:T(8,128)S(1)}, u32[]{:S(2)}, u32[]{:S(2)}) collective-permute-start(f32[320,128]{1,0:T(8,128)S(1)} %shard_map.44.field.rest_0_), channel_id=1, source_target_pairs={{0,64},{64,0},{128,192},{192,128},{256,320},{320,256},{384,448},{4... | collective-permute-start | bytes 491528 | tf_op jit(solution)/shard_map/ppermute | solution.py:271
  30.2 8.0 %collective-permute-start.6 = (f32[320,128]{1,0:T(8,128)S(1)}, f32[320,128]{1,0:T(8,128)S(1)}, u32[]{:S(2)}, u32[]{:S(2)}) collective-permute-start(f32[320,128]{1,0:T(8,128)S(1)} %shard_map.44.field.rest_0_), channel_id=1, source_target_pairs={{8,16},{16,8},{24,32},{32,24},{40,48},{48,40},{9,17},{17,9},{25,33... | collective-permute-start | bytes 491528 | tf_op jit(solution)/shard_map/ppermute | solution.py:262
  30.8 8.8 %collective-permute-start.9 = (f32[320,128]{1,0:T(8,128)S(1)}, f32[320,128]{1,0:T(8,128)S(1)}, u32[]{:S(2)}, u32[]{:S(2)}) collective-permute-start(f32[320,128]{1,0:T(8,128)S(1)} %shard_map.44.field.rest_0_), channel_id=1, source_target_pairs={{64,128},{128,64},{192,256},{256,192},{320,384},{384,320},{8,72},{... | collective-permute-start | bytes 491528 | tf_op jit(solution)/shard_map/ppermute | solution.py:271
  31.5 8.2 %collective-permute-start.8 = (f32[320,128]{1,0:T(8,128)S(1)}, f32[320,128]{1,0:T(8,128)S(1)}, u32[]{:S(2)}, u32[]{:S(2)}) collective-permute-start(f32[320,128]{1,0:T(8,128)S(1)} %shard_map.44.field.rest_0_), channel_id=1, source_target_pairs={{0,8},{8,0},{16,24},{24,16},{32,40},{40,32},{48,56},{56,48},{1,9},... | collective-permute-start | bytes 491528 | tf_op jit(solution)/shard_map/ppermute | solution.py:262
  40.5 12.7 %collective-permute-start.11 = (f32[320,128]{1,0:T(8,128)S(1)}, f32[320,128]{1,0:T(8,128)S(1)}, u32[]{:S(2)}, u32[]{:S(2)}) collective-permute-start(f32[320,128]{1,0:T(8,128)S(1)} %shard_map.46.field), channel_id=1, source_target_pairs={{0,64},{64,0},{128,192},{192,128},{256,320},{320,256},{384,448},{4... | collective-permute-start | bytes 491528 | tf_op jit(solution)/shard_map/ppermute | solution.py:271
  44.1 9.2 %collective-permute-start.10 = (f32[320,128]{1,0:T(8,128)S(1)}, f32[320,128]{1,0:T(8,128)S(1)}, u32[]{:S(2)}, u32[]{:S(2)}) collective-permute-start(f32[320,128]{1,0:T(8,128)S(1)} %shard_map.46.field), channel_id=1, source_target_pairs={{8,16},{16,8},{24,32},{32,24},{40,48},{48,40},{9,17},{17,9},{25,33... | collective-permute-start | bytes 491528 | tf_op jit(solution)/shard_map/ppermute | solution.py:262
  44.7 10.0 %collective-permute-start.13 = (f32[320,128]{1,0:T(8,128)S(1)}, f32[320,128]{1,0:T(8,128)S(1)}, u32[]{:S(2)}, u32[]{:S(2)}) collective-permute-start(f32[320,128]{1,0:T(8,128)S(1)} %shard_map.46.field), channel_id=1, source_target_pairs={{64,128},{128,64},{192,256},{256,192},{320,384},{384,320},{8,72},{... | collective-permute-start | bytes 491528 | tf_op jit(solution)/shard_map/ppermute | solution.py:271
  45.4 9.4 %collective-permute-start.12 = (f32[320,128]{1,0:T(8,128)S(1)}, f32[320,128]{1,0:T(8,128)S(1)}, u32[]{:S(2)}, u32[]{:S(2)}) collective-permute-start(f32[320,128]{1,0:T(8,128)S(1)} %shard_map.46.field), channel_id=1, source_target_pairs={{0,8},{8,0},{16,24},{24,16},{32,40},{40,32},{48,56},{56,48},{1,9},... | collective-permute-start | bytes 491528 | tf_op jit(solution)/shard_map/ppermute | solution.py:262
  55.6 6.9 %collective-permute-start.15 = (f32[256,128]{1,0:T(8,128)S(1)}, f32[256,128]{1,0:T(8,128)S(1)}, u32[]{:S(2)}, u32[]{:S(2)}) collective-permute-start(f32[256,128]{1,0:T(8,128)S(1)} %get-tuple-element.14.field), channel_id=1, source_target_pairs={{64,0},{128,64},{192,128},{256,192},{320,256},{384,320},{448,384},... | collective-permute-start | bytes 393224 | tf_op jit(solution)/shard_map/ppermute | solution.py:281
  56.9 5.6 %collective-permute-start.14 = (f32[256,128]{1,0:T(8,128)S(1)}, f32[256,128]{1,0:T(8,128)S(1)}, u32[]{:S(2)}, u32[]{:S(2)}) collective-permute-start(f32[256,128]{1,0:T(8,128)S(1)} %get-tuple-element.14.field), channel_id=1, source_target_pairs={{8,0},{16,8},{24,16},{32,24},{40,32},{48,40},{56,48},{9,1},{17,9},... | collective-permute-start | bytes 393224 | tf_op jit(solution)/shard_map/ppermute | solution.py:285
  63.4 5.4 %collective-permute-start.16 = (f32[4,128]{1,0:T(4,128)S(1)}, f32[4,128]{1,0:T(4,128)S(1)}, u32[]{:S(2)}, u32[]{:S(2)}) collective-permute-start(f32[4,128]{1,0:T(4,128)S(1)} %shard_map.50), channel_id=1, source_target_pairs={{0,8},{8,0},{16,24},{24,16},{32,40},{40,32},{48,56},{56,48},{1,9},... | collective-permute-start | bytes 6152 | tf_op jit(solution)/shard_map/ppermute | solution.py:291
